TPU v7x, 32 devices: a whole 2x2x4 slice. The times are simulated.
32 devices in a mesh: dp: 8 (over y, x, core), tensor: 4 (over z).
Axes of the slice: x: 2, y: 2, z: 4, core: 2. Of those that a mesh axis runs over, the one named last changes fastest.
Arguments:
- tokens: bfloat16 [32768, 2048], P(('dp', 'tensor')), may hold values from -6 to 6
- lengths: int32 [8, 3], P('dp'), may hold values from 1024 to 2048, as said below
- first_norm_gain: float32 [2048], replicated, may hold values from 0.5 to 1.5
- w_in: bfloat16 [2048, 2048], P(None, 'tensor'), may hold values from -0.125 to 0.125
- w_forget: bfloat16 [2048, 2048], P(None, 'tensor'), may hold values from -0.125 to 0.125
- w_gate: bfloat16 [2048, 2048], P(None, 'tensor'), may hold values from -0.125 to 0.125
- lower_bound: float32 [2048], P('tensor'), may hold values from 0.3 to 0.97
- gate_gain: float32 [2048], P('tensor'), may hold values from 0.5 to 1.5
- w_out: bfloat16 [2048, 2048], P('tensor'), may hold values from -0.25 to 0.25
- feedforward_gain: float32 [2048], replicated, may hold values from 0.5 to 1.5
- w_up: bfloat16 [2048, 5632], P(None, 'tensor'), may hold values from -0.125 to 0.125
- w_glu: bfloat16 [2048, 5632], P(None, 'tensor'), may hold values from -0.125 to 0.125
- w_down: bfloat16 [5632, 2048], P('tensor'), may hold values from -0.15625 to 0.15625
- cotangent: bfloat16 [32768, 2048], P(('dp', 'tensor')), may hold values from -6 to 6
Outputs:
- output: bfloat16 [32768, 2048], P(('dp', 'tensor'))
- token_gradient: float32 [32768, 2048], P(('dp', 'tensor'))
- grad_norm_gain: float32 [2048], replicated
- grad_w_in: float32 [2048, 2048], P('dp', 'tensor')
- grad_w_forget: float32 [2048, 2048], P('dp', 'tensor')
- grad_w_gate: float32 [2048, 2048], P('dp', 'tensor')
- grad_lower_bound: float32 [2048], replicated
- grad_gate_gain: float32 [2048], replicated
- grad_w_out: float32 [2048, 2048], P('tensor', 'dp')
- grad_mlp_gain: float32 [2048], replicated
- grad_w_up: float32 [2048, 5632], P('dp', 'tensor')
- grad_w_glu: float32 [2048, 5632], P('dp', 'tensor')
- grad_w_down: float32 [5632, 2048], P('tensor', 'dp')
- mean_forget: float32 [], replicated
Inputs may be any that keep to these rules, and one draw needn't show every extreme that they name: `lengths`: each row sums to 4096; each row holds one sequence of 2048 tokens, at a position drawn from the seed; the other two sum to 2048 and are 1024 or more each.
All inputs are finite; a program needn't handle non-finite values.
Results may differ from a plain program's by a relative error of at most 0.014.
Values may be sent and summed in bfloat16 or wider, within the bound.
A program may use at most 448 MiB of HBM per device.

v0:
```python
import jax
import jax.numpy as jnp
from jax import lax
from jax.sharding import PartitionSpec as P

EPS = 1e-06


def silu_slope(value):
    sig = jax.nn.sigmoid(value)
    return sig * (1.0 + value * (1.0 - sig))


def affine(early, late):
    return (early[0] * late[0], late[0] * early[1] + late[1])


def keep_mask(lengths, total):
    ends = jnp.cumsum(lengths[0])
    starts = ends - lengths[0]
    rows = jnp.arange(total, dtype=jnp.int32)
    flag = jnp.any(rows[:, None] == starts[None, :], axis=1)
    return jnp.where(flag, 0.0, 1.0).astype(jnp.float32)[:, None]


def over_rows(left, right):
    return lax.dot_general(
        left, right, (((0,), (0,)), ((), ())), preferred_element_type=jnp.float32
    )


def over_cols(left, right):
    return lax.dot_general(
        left, right, (((1,), (1,)), ((), ())), preferred_element_type=jnp.float32
    )


def norm_pullback(upstream_gradient, unit_rows, inverse_rms, gain_vector):
    scaled_rows = upstream_gradient * gain_vector
    return inverse_rms * (
        scaled_rows - unit_rows * jnp.mean(scaled_rows * unit_rows, axis=1, keepdims=True)
    )


def local(
    tokens,
    lengths,
    first_norm_gain,
    w_in,
    w_forget,
    w_gate,
    lower_bound,
    gate_gain,
    w_out,
    feedforward_gain,
    w_up,
    w_glu,
    w_down,
    cotangent,
):
    rows_loc, width = tokens.shape
    chans = w_in.shape[1]
    group = rows_loc * lax.axis_size("tensor")
    input_float32 = tokens.astype(jnp.float32)
    inverse_rms1 = lax.rsqrt(jnp.mean(input_float32 * input_float32, axis=1, keepdims=True) + EPS)
    unit_rows1 = input_float32 * inverse_rms1
    normalized_rows = (unit_rows1 * first_norm_gain).astype(jnp.bfloat16)
    rows_in = lax.all_gather(normalized_rows, "tensor", axis=0, tiled=True)
    w_three = jnp.concatenate([w_in, w_forget, w_gate], axis=1)
    proj = jnp.dot(rows_in, w_three, preferred_element_type=jnp.float32)
    p_in = proj[:, :chans]
    p_forget = proj[:, chans : 2 * chans]
    p_gate = proj[:, 2 * chans :]
    sig_f = jax.nn.sigmoid(p_forget)
    lam = lower_bound + (1.0 - lower_bound) * sig_f
    act_in = jax.nn.silu(p_in)
    inject = act_in * (1.0 - lam)
    keep = keep_mask(lengths, group)
    decay = lam * keep
    _, state = lax.associative_scan(affine, (decay, inject), axis=0)
    sq_total = lax.psum(jnp.sum(state * state, axis=1, keepdims=True), "tensor")
    scale = lax.rsqrt(sq_total / width + EPS)
    gate_act = jax.nn.silu(p_gate)
    mixed = (state * scale * gate_gain * gate_act).astype(jnp.bfloat16)
    branch_sum = lax.psum_scatter(
        jnp.dot(mixed, w_out, preferred_element_type=jnp.float32),
        "tensor",
        scatter_dimension=0,
        tiled=True,
    )
    residual_stream = input_float32 + branch_sum
    inverse_rms2 = lax.rsqrt(
        jnp.mean(residual_stream * residual_stream, axis=1, keepdims=True) + EPS
    )
    unit_rows2 = residual_stream * inverse_rms2
    middle_stream = (unit_rows2 * feedforward_gain).astype(jnp.bfloat16)
    rows_mid = lax.all_gather(middle_stream, "tensor", axis=0, tiled=True)
    up = jnp.dot(rows_mid, w_up, preferred_element_type=jnp.float32)
    glu = jnp.dot(rows_mid, w_glu, preferred_element_type=jnp.float32)
    hidden = (jax.nn.silu(glu) * up).astype(jnp.bfloat16)
    output = (
        residual_stream
        + lax.psum_scatter(
            jnp.dot(hidden, w_down, preferred_element_type=jnp.float32).astype(jnp.bfloat16),
            "tensor",
            scatter_dimension=0,
            tiled=True,
        ).astype(jnp.float32)
    ).astype(jnp.bfloat16)
    grad_all = lax.all_gather(cotangent, "tensor", axis=0, tiled=True)
    g_hidden = over_cols(grad_all, w_down)
    d_down = over_rows(hidden, grad_all)
    g_up = (g_hidden * jax.nn.silu(glu)).astype(jnp.bfloat16)
    g_glu = (g_hidden * up * silu_slope(glu)).astype(jnp.bfloat16)
    d_up = over_rows(rows_mid, g_up)
    d_glu = over_rows(rows_mid, g_glu)
    middle_gradient = lax.psum_scatter(
        over_cols(g_up, w_up) + over_cols(g_glu, w_glu), "tensor", scatter_dimension=0, tiled=True
    )
    feedforward_gain_gradient = jnp.sum(middle_gradient * unit_rows2, axis=0)
    residual_gradient = cotangent.astype(jnp.float32) + norm_pullback(
        middle_gradient, unit_rows2, inverse_rms2, feedforward_gain
    )
    resid_all = lax.all_gather(residual_gradient.astype(jnp.bfloat16), "tensor", axis=0, tiled=True)
    d_out = over_rows(mixed, resid_all)
    g_mixed = over_cols(resid_all, w_out)
    inner = g_mixed * gate_gain * gate_act
    d_gate_gain = jnp.sum(g_mixed * state * scale * gate_act, axis=0)
    g_gate = g_mixed * state * scale * gate_gain * silu_slope(p_gate)
    cross = lax.psum(jnp.sum(inner * state, axis=1, keepdims=True), "tensor")
    g_state = inner * scale - state * scale * scale * scale * cross / width
    next_decay = jnp.concatenate([decay[1:], jnp.zeros((1, chans), jnp.float32)], axis=0)
    _, carry = lax.associative_scan(affine, (next_decay, g_state), reverse=True, axis=0)
    prev_state = jnp.concatenate([jnp.zeros((1, chans), jnp.float32), state[:-1]], axis=0)
    g_lam = carry * prev_state * keep - carry * act_in
    g_in = carry * (1.0 - lam) * silu_slope(p_in)
    d_lower = jnp.sum(g_lam * (1.0 - sig_f), axis=0)
    g_forget = g_lam * (1.0 - lower_bound) * sig_f * (1.0 - sig_f)
    g_proj = jnp.concatenate([g_in, g_forget, g_gate], axis=1).astype(jnp.bfloat16)
    d_three = over_rows(rows_in, g_proj)
    normalized_gradient = lax.psum_scatter(
        over_cols(g_proj, w_three).astype(jnp.bfloat16), "tensor", scatter_dimension=0, tiled=True
    ).astype(jnp.float32)
    first_gain_gradient = jnp.sum(normalized_gradient * unit_rows1, axis=0)
    token_gradient = residual_gradient + norm_pullback(
        normalized_gradient, unit_rows1, inverse_rms1, first_norm_gain
    )
    grad_w_in, grad_w_forget, grad_w_gate, grad_w_out, grad_w_up, grad_w_glu, grad_w_down = (
        lax.psum_scatter(
            d_three[:, :chans].astype(jnp.bfloat16), "dp", scatter_dimension=0, tiled=True
        ).astype(jnp.float32),
        lax.psum_scatter(
            d_three[:, chans : 2 * chans].astype(jnp.bfloat16),
            "dp",
            scatter_dimension=0,
            tiled=True,
        ).astype(jnp.float32),
        lax.psum_scatter(
            d_three[:, 2 * chans :].astype(jnp.bfloat16), "dp", scatter_dimension=0, tiled=True
        ).astype(jnp.float32),
        lax.psum_scatter(d_out.astype(jnp.bfloat16), "dp", scatter_dimension=1, tiled=True).astype(
            jnp.float32
        ),
        lax.psum_scatter(d_up.astype(jnp.bfloat16), "dp", scatter_dimension=0, tiled=True).astype(
            jnp.float32
        ),
        lax.psum_scatter(d_glu.astype(jnp.bfloat16), "dp", scatter_dimension=0, tiled=True).astype(
            jnp.float32
        ),
        lax.psum_scatter(d_down.astype(jnp.bfloat16), "dp", scatter_dimension=1, tiled=True).astype(
            jnp.float32
        ),
    )
    offset = lax.axis_index("tensor") * chans
    gate_full = lax.dynamic_update_slice_in_dim(
        jnp.zeros((width,), jnp.float32), d_gate_gain, offset, 0
    )
    lower_full = lax.dynamic_update_slice_in_dim(
        jnp.zeros((width,), jnp.float32), d_lower, offset, 0
    )
    grad_norm_gain, grad_mlp_gain, grad_gate_gain, grad_lower_bound, forget_total = lax.psum(
        (first_gain_gradient, feedforward_gain_gradient, gate_full, lower_full, jnp.sum(lam)),
        ("dp", "tensor"),
    )
    mean_forget = forget_total / (group * lax.axis_size("dp") * width)
    return (
        output,
        token_gradient,
        grad_norm_gain,
        grad_w_in,
        grad_w_forget,
        grad_w_gate,
        grad_lower_bound,
        grad_gate_gain,
        grad_w_out,
        grad_mlp_gain,
        grad_w_up,
        grad_w_glu,
        grad_w_down,
        mean_forget,
    )


def solution(mesh):
    return jax.shard_map(
        local,
        mesh=mesh,
        in_specs=(
            P(("dp", "tensor"), None),
            P("dp", None),
            P(),
            P(None, "tensor"),
            P(None, "tensor"),
            P(None, "tensor"),
            P("tensor"),
            P("tensor"),
            P("tensor", None),
            P(),
            P(None, "tensor"),
            P(None, "tensor"),
            P("tensor", None),
            P(("dp", "tensor"), None),
        ),
        out_specs=(
            P(("dp", "tensor"), None),
            P(("dp", "tensor"), None),
            P(),
            P("dp", "tensor"),
            P("dp", "tensor"),
            P("dp", "tensor"),
            P(),
            P(),
            P("tensor", "dp"),
            P(),
            P("dp", "tensor"),
            P("dp", "tensor"),
            P("tensor", "dp"),
            P(),
        ),
        check_vma=False,
    )
```

profile of v0, /device:TPU:0, one launch (start us, length us, event | category | flops | bytes accessed | tf_op | source)
XLA Modules:
  0.0 4393.5 jit_solution(13164360649750119217)
XLA Ops:
  24.8 281.2 %all-gather.5.cloned.1.call-done = bf16[4096,2048]{1,0:T(8,128)(2,1)} async-done(((bf16[1024,2048]{1,0:T(8,128)(2,1)}), bf16[4096,2048]{1,0:T(8,128)(2,1)}) %all-gather.5.cloned.1.call-update) | async-done | bytes 16777232 | tf_op jit(solution)/shard_map/all_gather | solution.py:68
  848.4 549.8 %reduce-scatter.12.cloned.1.call-done = f32[1024,2048]{1,0:T(8,128)} async-done(((f32[4096,2048]{1,0:T(8,128)}), f32[1024,2048]{1,0:T(8,128)}) %reduce-scatter.12.cloned.1.call-update) | async-done | bytes 8388624 | tf_op jit(solution)/shard_map/reduce_scatter | solution.py:85
  1410.3 277.1 %all-gather.9.cloned.1.call-done = bf16[4096,2048]{1,0:T(8,128)(2,1)} async-done(((bf16[1024,2048]{1,0:T(8,128)(2,1)}), bf16[4096,2048]{1,0:T(8,128)(2,1)}) %all-gather.9.cloned.1.call-update) | async-done | bytes 16777232 | tf_op jit(solution)/shard_map/all_gather | solution.py:110
  1687.4 33.3 fusion.77
  1720.8 253.8 %all-gather.7.cloned.1.call-done = bf16[4096,2048]{1,0:T(8,128)(2,1)} async-done(((bf16[1024,2048]{1,0:T(8,128)(2,1)}), bf16[4096,2048]{1,0:T(8,128)(2,1)}) %all-gather.7.cloned.1.call-update) | async-done | bytes 16777232 | tf_op jit(solution)/shard_map/all_gather | solution.py:97
  1974.5 33.1 fusion.76
  2007.6 47.5 %multiply_convert_fusion = (bf16[4096,1408]{1,0:T(8,128)(2,1)}, bf16[4096,1408]{1,0:T(8,128)(2,1)}, bf16[4096,1408]{1,0:T(8,128)(2,1)}) fusion(f32[4096,1408]{1,0:T(8,128)} %fusion.77, f32[4096,1408]{1,0:T(8,128)} %fusion.76, bf16[4096,2048]{1,0:T(8,128)(2,1)} %all-gather.7.cloned.1.call-done, bf16[2048,1408]{1,0:T(8,128)(2,1)} %param.25), kind=kOutput, calls=%fused_computation | convolution fusion | flops 23708827648 | bytes 103284736 | tf_op jit(solution)/shard_map/dot_general | solution.py:99
  2055.1 33.5 fusion.78
  2088.6 37.0 convolution_add_fusion
  2125.7 550.4 %reduce-scatter.16.cloned.1.call-done = f32[1024,2048]{1,0:T(8,128)} async-done(((f32[4096,2048]{1,0:T(8,128)}), f32[1024,2048]{1,0:T(8,128)}) %reduce-scatter.16.cloned.1.call-update) | async-done | bytes 8388624 | tf_op jit(solution)/shard_map/reduce_scatter | solution.py:117
  2723.0 33.8 convolution_convert_fusion.2
  2861.8 33.7 slice.701
  2895.5 32.7 slice.703
  2939.4 33.7 convolution_convert_fusion.3
  3075.0 32.7 slice.705
  3107.7 32.8 slice.707
  3362.1 33.6 slice.795
  3526.7 64.2 %rev.2 = f32[4096,512]{1,0:T(8,128)} reverse(f32[4096,512]{1,0:T(8,128)} %add.506), dimensions={0} | reverse | bytes 16777216 | tf_op jit(solution)/shard_map/rev | solution.py:133
  3626.9 38.0 convolution_convert_fusion.5
  3669.2 33.4 convolution_convert_fusion
  3758.1 42.7 reduce-scatter.24.cloned.1.call-done
  3802.6 280.9 %reduce-scatter.18.cloned.1.call-done = bf16[1024,2048]{1,0:T(8,128)(2,1)} async-done(((bf16[4096,2048]{1,0:T(8,128)(2,1)}), bf16[1024,2048]{1,0:T(8,128)(2,1)}) %reduce-scatter.18.cloned.1.call-update) | async-done | bytes 4194320 | tf_op jit(solution)/shard_map/reduce_scatter | solution.py:141
  4088.5 45.9 %all-reduce.50 = (f32[2048]{0:T(1024)}, f32[2048]{0:T(1024)}, f32[2048]{0:T(1024)}, f32[2048]{0:T(1024)}, f32[]{:T(128)}) all-reduce(f32[2048]{0:T(1024)S(1)} %get-tuple-element.20, f32[2048]{0:T(1024)S(1)} %dynamic_update_slice.6, f32[2048]{0:T(1024)S(1)} %dynamic_update_slice.7, ...), channel_id=1, replica_groups=mesh['dp'=8,'tensor'=4] {'dp','tensor'}, use_global_device_ids=true, to_apply=%region_15.16 | all-reduce | flops 8193 | bytes 65544 | tf_op jit(solution)/shard_map/psum | solution.py:181
  4135.1 232.6 %reduce-scatter.14.cloned.1.call-done = bf16[1024,2048]{1,0:T(8,128)(2,1)} async-done(((bf16[4096,2048]{1,0:T(8,128)(2,1)}), bf16[1024,2048]{1,0:T(8,128)(2,1)}) %reduce-scatter.14.cloned.1.call-update) | async-done | bytes 4194320 | tf_op jit(solution)/shard_map/reduce_scatter | solution.py:103
  (445 shorter events, 1309.1 us)
Async XLA Ops:
  7.2 825.9 %copy-start = (bf16[512,2048]{1,0:T(8,128)(2,1)S(1)}, bf16[512,2048]{1,0:T(8,128)(2,1)}, u32[]{:S(2)}) copy-start(bf16[512,2048]{1,0:T(8,128)(2,1)} %param.22) | copy-start | bytes 6291460
  7.2 298.7 %all-gather.5.cloned.1.call-start = ((), (), s32[]{:S(2)}) async-start(), calls=%async_computation.11 | async-start | bytes 20971520 | tf_op jit(solution)/shard_map/all_gather | solution.py:68
  16.3 1381.9 %reduce-scatter.12.cloned.1.call-start = ((), (), s32[]{:S(2)}) async-start(), calls=%async_computation.12 | async-start | bytes 41943040 | tf_op jit(solution)/shard_map/reduce_scatter | solution.py:85
  847.6 839.8 %all-gather.9.cloned.1.call-start = ((), (), s32[]{:S(2)}) async-start(), calls=%async_computation.15 | async-start | bytes 20971520 | tf_op jit(solution)/shard_map/all_gather | solution.py:110
  848.3 559.0 %copy-start.16 = (f32[2048]{0:T(1024)S(1)}, f32[2048]{0:T(1024)}, u32[]{:S(2)}) copy-start(f32[2048]{0:T(1024)} %param.23) | copy-start | bytes 24580
  848.3 1126.2 %all-gather.7.cloned.1.call-start = ((), (), s32[]{:S(2)}) async-start(), calls=%async_computation.13 | async-start | bytes 20971520 | tf_op jit(solution)/shard_map/all_gather | solution.py:97
  1410.3 1265.8 %reduce-scatter.16.cloned.1.call-start = ((), (), s32[]{:S(2)}) async-start(), calls=%async_computation.16 | async-start | bytes 41943040 | tf_op jit(solution)/shard_map/reduce_scatter | solution.py:117
  2125.6 550.4 %copy-start.17 = (f32[2048]{0:T(1024)S(1)}, f32[2048]{0:T(1024)}, u32[]{:S(2)}) copy-start(f32[2048]{0:T(1024)} %param.23) | copy-start | bytes 24580
  2125.6 550.4 %copy-start.20 = (f32[1024]{0:T(1024)S(1)}, f32[1024]{0:T(1024)}, u32[]{:S(2)}) copy-start(f32[1024]{0:T(1024)} %copy-done.19) | copy-start | bytes 12292
  2125.6 853.4 %all-gather.11.cloned.1.call-start = ((), (), s32[]{:S(2)}) async-start(), calls=%async_computation.17 | async-start | bytes 20971520 | tf_op jit(solution)/shard_map/all_gather | solution.py:124
  2691.4 1043.9 %reduce-scatter.32.cloned.1.call-start = ((), (), s32[]{:S(2)}) async-start(), calls=%async_computation.25 | async-start | bytes 6488064 | tf_op jit(solution)/shard_map/reduce_scatter | solution.py:170
  2723.0 1014.8 %reduce-scatter.30.cloned.1.call-start = ((), (), s32[]{:S(2)}) async-start(), calls=%async_computation.24 | async-start | bytes 6488064 | tf_op jit(solution)/shard_map/reduce_scatter | solution.py:167
  2756.9 983.2 %reduce-scatter.28.cloned.1.call-start = ((), (), s32[]{:S(2)}) async-start(), calls=%async_computation.23 | async-start | bytes 6488064 | tf_op jit(solution)/shard_map/reduce_scatter | solution.py:164
  2973.1 769.9 %reduce-scatter.26.cloned.1.call-start = ((), (), s32[]{:S(2)}) async-start(), calls=%async_computation.22 | async-start | bytes 2359296 | tf_op jit(solution)/shard_map/reduce_scatter | solution.py:161
  3626.9 117.8 %reduce-scatter.20.cloned.1.call-start = ((), (), s32[]{:S(2)}) async-start(), calls=%async_computation.19 | async-start | bytes 2359296 | tf_op jit(solution)/shard_map/reduce_scatter | solution.py:149
  3667.9 88.4 %reduce-scatter.22.cloned.1.call-start = ((), (), s32[]{:S(2)}) async-start(), calls=%async_computation.20 | async-start | bytes 2359296 | tf_op jit(solution)/shard_map/reduce_scatter | solution.py:152
  3668.4 132.3 %reduce-scatter.24.cloned.1.call-start = ((), (), s32[]{:S(2)}) async-start(), calls=%async_computation.21 | async-start | bytes 2359296 | tf_op jit(solution)/shard_map/reduce_scatter | solution.py:158
  3669.2 414.3 %reduce-scatter.18.cloned.1.call-start = ((), (), s32[]{:S(2)}) async-start(), calls=%async_computation.18 | async-start | bytes 20971520 | tf_op jit(solution)/shard_map/reduce_scatter | solution.py:141
  3702.6 665.1 %reduce-scatter.14.cloned.1.call-start = ((), (), s32[]{:S(2)}) async-start(), calls=%async_computation.14 | async-start | bytes 20971520 | tf_op jit(solution)/shard_map/reduce_scatter | solution.py:103
  3735.2 348.2 %copy-start.22 = (f32[2048]{0:T(1024)S(1)}, f32[2048]{0:T(1024)}, u32[]{:S(2)}) copy-start(f32[2048]{0:T(1024)} %param.16) | copy-start | bytes 24580
  3737.8 350.7 %copy-start.27 = (f32[2048]{0:T(1024)S(1)}, f32[2048]{0:T(1024)}, u32[]{:S(2)}) copy-start(f32[2048]{0:T(1024)} %get-tuple-element.18) | copy-start | bytes 24580
  3737.8 629.9 %copy-start.18 = (f32[2048]{0:T(1024)S(1)}, f32[2048]{0:T(1024)}, u32[]{:S(2)}) copy-start(f32[2048]{0:T(1024)} %param.23) | copy-start | bytes 24580
  3737.8 629.9 %copy-start.21 = (f32[1024]{0:T(1024)S(1)}, f32[1024]{0:T(1024)}, u32[]{:S(2)}) copy-start(f32[1024]{0:T(1024)} %copy-done.19) | copy-start | bytes 12292
  3737.8 629.9 %copy-start.26 = (f32[1024]{0:T(1024)S(1)}, f32[1024]{0:T(1024)}, u32[]{:S(2)}) copy-start(f32[1024]{0:T(1024)} %copy-done.25) | copy-start | bytes 12292
  (28 other events, 1402.5 us)
Sparse Core Ops, SparseCore 0:
  16.4 289.4 all-gather.4
  847.7 550.4 reduce-scatter.11
  1399.9 287.4 all-gather.8
  1689.5 284.9 all-gather.6
  2125.8 550.2 reduce-scatter.15
  2691.5 287.4 all-gather.10
  2982.5 57.2 reduce-scatter.31
  3043.6 58.9 reduce-scatter.29
  3106.1 59.0 reduce-scatter.27
  3627.0 39.8 reduce-scatter.25
  3670.2 41.2 reduce-scatter.19
  3715.0 41.2 reduce-scatter.21
  3759.5 41.1 reduce-scatter.23
  3803.1 280.3 reduce-scatter.17
  4085.7 281.9 reduce-scatter.13
where the time goes:
time: 4430 us; the launch traced here: 4390 us
  waiting for transfers between devices  2490 us (56%)
  local copies, waits for them, and re-layouts  1050 us (24%)
  matrix products  468 us (11%)
  other arithmetic  289 us (7%)
  blocking collectives  78.1 us (2%)
    reduce_scatter x1, waiting for transfers between devices, local(): lax.psum_scatter(over_cols(g_up, w_up) + over_cols(g_glu, w_glu), 'tensor...  550 us
    reduce_scatter x1, waiting for transfers between devices, local(): lax.psum_scatter(jnp.dot(mixed, w_out, preferred_element_type=jnp.float32...  550 us
    slice x80, local copies, waits for them, and re-layouts, local(): lax.associative_scan(affine, (next_decay, g_state), reverse=True, axis=0)  458 us
    all_gather x1, waiting for transfers between devices, local(): rows_in = lax.all_gather(normalized_rows, 'tensor', axis=0, tiled=True)  281 us
    reduce_scatter x1, waiting for transfers between devices, local(): lax.psum_scatter(over_cols(g_proj, w_three).astype(jnp.bfloat16), 'tensor...  281 us
    all_gather x1, waiting for transfers between devices, local(): grad_all = lax.all_gather(cotangent, 'tensor', axis=0, tiled=True)  277 us
    slice x74, local copies, waits for them, and re-layouts, local(): _, state = lax.associative_scan(affine, (decay, inject), axis=0)  261 us
    all_gather x1, waiting for transfers between devices, local(): rows_mid = lax.all_gather(middle_stream, 'tensor', axis=0, tiled=True)  254 us
  transfers between devices with their start and end apart: 15, of which 10 were waited for; matrix products, arithmetic and copies ran while one was open for 25% of the time, Pallas kernels for 0%

commit v1 on v0

v1 whole, which is shorter than its diff:
```python
import functools

import jax
import jax.numpy as jnp
from jax import lax
from jax.experimental import pallas as pl
from jax.experimental.pallas import tpu as pltpu
from jax.sharding import Mesh
from jax.sharding import PartitionSpec as P

EPS = 1e-06
VMEM_LIMIT = 60 * 1024 * 1024
F32 = jnp.float32
BF16 = jnp.bfloat16


def params(**kw):
    return pltpu.CompilerParams(vmem_limit_bytes=VMEM_LIMIT, **kw)


def nn(left, right):
    return lax.dot_general(left, right, (((1,), (0,)), ((), ())), preferred_element_type=F32)


def nt(left, right):
    return lax.dot_general(left, right, (((1,), (1,)), ((), ())), preferred_element_type=F32)


def tn(left, right):
    return lax.dot_general(left, right, (((0,), (0,)), ((), ())), preferred_element_type=F32)


def sigmoid(v):
    return jax.nn.sigmoid(v)


def whole(shape):
    zeros = (0,) * len(shape)
    return pl.BlockSpec(shape, lambda *_: zeros)


def proj_kernel(x_ref, w_ref, o_ref):
    o_ref[0] = nn(x_ref[...], w_ref[0])


def project(normed, w3, chans):
    rows, width = normed.shape
    ways, _, wide = w3.shape
    return pl.pallas_call(
        proj_kernel,
        grid=(ways, wide // chans),
        in_specs=[
            whole((rows, width)),
            pl.BlockSpec((1, width, chans), lambda t, j: (t, 0, j)),
        ],
        out_specs=pl.BlockSpec((1, rows, chans), lambda t, j: (t, 0, j)),
        out_shape=jax.ShapeDtypeStruct((ways, rows, wide), F32),
        compiler_params=params(),
        name="project",
    )(normed, w3)


def gates(p_in, p_forget, lower, ids, starts):
    sig = sigmoid(p_forget)
    lam = lower + (1.0 - lower) * sig
    fresh = ids == starts[0]
    for s in starts[1:]:
        fresh = jnp.logical_or(fresh, ids == s)
    keep = jnp.where(fresh, 0.0, 1.0)
    return sig, lam, keep


def forward_total_kernel(starts_ref, p_ref, lower_ref, o_ref):
    rows, chans = p_ref.shape[1], p_ref.shape[2] // 2
    lower = lower_ref[0]
    starts = [starts_ref[i] for i in range(starts_ref.shape[0])]
    iota = lax.broadcasted_iota(jnp.int32, (8, chans), 0)

    def step(g, carry):
        total, last = carry
        at = pl.multiple_of(g * 8, 8)
        p_in = p_ref[0, pl.ds(at, 8), :chans]
        p_forget = p_ref[0, pl.ds(at, 8), chans:]
        _, lam, keep = gates(p_in, p_forget, lower, iota + at, starts)
        a = lam * keep
        b = p_in * sigmoid(p_in) * (1.0 - lam)
        for s in (1, 2, 4):
            b = a * pltpu.roll(b, s, 0) + b
            a = a * pltpu.roll(a, s, 0)
        a, b = a[7:8], b[7:8]
        return total * a, a * last + b

    total, last = lax.fori_loop(
        0, rows // 8, step, (jnp.ones((1, chans), F32), jnp.zeros((1, chans), F32)), unroll=2
    )
    o_ref[0, 0:1] = total
    o_ref[0, 1:2] = last


def forward_total(p, lower, starts):
    ways, rows, wide = p.shape
    chans = wide // 3
    return pl.pallas_call(
        forward_total_kernel,
        grid=(ways,),
        in_specs=[
            pl.BlockSpec(memory_space=pltpu.SMEM),
            pl.BlockSpec((1, rows, 2 * chans), lambda t: (t, 0, 0)),
            pl.BlockSpec((1, 1, chans), lambda t: (t, 0, 0)),
        ],
        out_specs=pl.BlockSpec((1, 2, chans), lambda t: (t, 0, 0)),
        out_shape=jax.ShapeDtypeStruct((ways, 2, chans), F32),
        compiler_params=params(),
        name="forward_total",
    )(starts, p, lower)


def forward_scan_kernel(starts_ref, p_ref, lower_ref, gain_ref, enter_ref, state_ref, mixed_ref, lam_ref, held):
    ways, rows, wide = p_ref.shape
    chans = wide // 3
    block = pl.program_id(0)
    starts = [starts_ref[i] for i in range(starts_ref.shape[0])]
    iota = lax.broadcasted_iota(jnp.int32, (8, chans), 0)

    @pl.when(block == 0)
    def _():
        held[...] = enter_ref[...]
        lam_ref[...] = jnp.zeros_like(lam_ref)

    for t in range(ways):
        lower = lower_ref[t]

        def step(g, carry):
            before, lam_sum = carry
            at = pl.multiple_of(g * 8, 8)
            p_in = p_ref[t, pl.ds(at, 8), :chans]
            p_forget = p_ref[t, pl.ds(at, 8), chans : 2 * chans]
            _, lam, keep = gates(p_in, p_forget, lower, iota + (at + block * rows), starts)
            a = lam * keep
            b = p_in * sigmoid(p_in) * (1.0 - lam)
            for s in (1, 2, 4):
                far = iota >= s
                b = jnp.where(far, a * pltpu.roll(b, s, 0) + b, b)
                a = jnp.where(far, a * pltpu.roll(a, s, 0), a)
            state = a * before + b
            state_ref[t, pl.ds(at, 8), :] = state
            return state[7:8], lam_sum + lam

        last, lam_sum = lax.fori_loop(
            0, rows // 8, step, (held[t], jnp.zeros((8, chans), F32)), unroll=2
        )
        held[t] = last
        lam_ref[t] += lam_sum

    squares = jnp.zeros((rows, 1), F32)
    for t in range(ways):
        state = state_ref[t]
        squares += jnp.sum(state * state, axis=1, keepdims=True)
    scale = lax.rsqrt(squares / (ways * chans) + EPS)
    for t in range(ways):
        gate = p_ref[t, :, 2 * chans :]
        mixed = state_ref[t] * scale * gain_ref[t] * (gate * sigmoid(gate))
        mixed_ref[t] = mixed.astype(BF16)


def forward_scan(p, lower, gain, starts, enter):
    ways, rows, wide = p.shape
    chans = wide // 3
    part = min(rows, 128)
    return pl.pallas_call(
        forward_scan_kernel,
        grid=(rows // part,),
        in_specs=[
            pl.BlockSpec(memory_space=pltpu.SMEM),
            pl.BlockSpec((ways, part, wide), lambda i: (0, i, 0)),
            whole((ways, 1, chans)),
            whole((ways, 1, chans)),
            whole((ways, 1, chans)),
        ],
        out_specs=[
            pl.BlockSpec((ways, part, chans), lambda i: (0, i, 0)),
            pl.BlockSpec((ways, part, chans), lambda i: (0, i, 0)),
            whole((ways, 8, chans)),
        ],
        out_shape=[
            jax.ShapeDtypeStruct((ways, rows, chans), F32),
            jax.ShapeDtypeStruct((ways, rows, chans), BF16),
            jax.ShapeDtypeStruct((ways, 8, chans), F32),
        ],
        scratch_shapes=[pltpu.VMEM((ways, 1, chans), F32)],
        compiler_params=params(),
        name="forward_scan",
    )(starts, p, lower, gain, enter)


def backward_total_kernel(
    starts_ref, pf_ref, pg_ref, state_ref, gm_ref, lower_ref, gain_ref,
    gstate_ref, ggate_ref, dgain_ref, total_ref, held,
):
    ways, rows, chans = pf_ref.shape
    step_id = pl.program_id(0)
    block = pl.num_programs(0) - 1 - step_id
    starts = [starts_ref[i] for i in range(starts_ref.shape[0])]
    iota = lax.broadcasted_iota(jnp.int32, (8, chans), 0)
    width = ways * chans

    @pl.when(step_id == 0)
    def _():
        held[...] = jnp.zeros_like(held)
        dgain_ref[...] = jnp.zeros_like(dgain_ref)

    squares = jnp.zeros((rows, 1), F32)
    cross = jnp.zeros((rows, 1), F32)
    for t in range(ways):
        state = state_ref[t]
        gate = pg_ref[t]
        inner = gm_ref[t] * gain_ref[t] * (gate * sigmoid(gate))
        gstate_ref[t] = inner
        squares += jnp.sum(state * state, axis=1, keepdims=True)
        cross += jnp.sum(inner * state, axis=1, keepdims=True)
    scale = lax.rsqrt(squares / width + EPS)
    pull = scale * scale * scale * cross / width
    for t in range(ways):
        state = state_ref[t]
        gate = pg_ref[t]
        sig = sigmoid(gate)
        slope = sig * (1.0 + gate * (1.0 - sig))
        unit = gm_ref[t] * state * scale
        ggate_ref[t] = (unit * gain_ref[t] * slope).astype(BF16)
        dgain_ref[t] += jnp.sum((unit * (gate * sig)).reshape(rows // 8, 8, chans), axis=0)
        gstate_ref[t] = gstate_ref[t] * scale - state * pull

    for t in range(ways):
        lower = lower_ref[t]

        def step(k, last):
            at = pl.multiple_of(rows - 8 - k * 8, 8)
            p_forget = pf_ref[t, pl.ds(at, 8), :]
            _, lam, keep = gates(None, p_forget, lower, iota + (at + block * rows), starts)
            a = lam * keep
            b = a * gstate_ref[t, pl.ds(at, 8), :]
            for s in (1, 2, 4):
                b = a * pltpu.roll(b, 8 - s, 0) + b
                a = a * pltpu.roll(a, 8 - s, 0)
            return a[0:1] * last + b[0:1]

        held[t] = lax.fori_loop(0, rows // 8, step, held[t], unroll=2)
    total_ref[...] = held[...]


def backward_total(p, state, g_mixed, lower, gain, starts):
    ways, rows, wide = p.shape
    chans = wide // 3
    part = min(rows, 128)
    last = rows // part - 1
    back = lambda i: (0, last - i, 0)
    block = pl.BlockSpec((ways, part, chans), back)
    return pl.pallas_call(
        backward_total_kernel,
        grid=(rows // part,),
        in_specs=[
            pl.BlockSpec(memory_space=pltpu.SMEM),
            pl.BlockSpec((ways, part, chans), lambda i: (0, last - i, 1)),
            pl.BlockSpec((ways, part, chans), lambda i: (0, last - i, 2)),
            block,
            block,
            whole((ways, 1, chans)),
            whole((ways, 1, chans)),
        ],
        out_specs=[block, block, whole((ways, 8, chans)), whole((ways, 1, chans))],
        out_shape=[
            jax.ShapeDtypeStruct((ways, rows, chans), F32),
            jax.ShapeDtypeStruct((ways, rows, chans), BF16),
            jax.ShapeDtypeStruct((ways, 8, chans), F32),
            jax.ShapeDtypeStruct((ways, 1, chans), F32),
        ],
        scratch_shapes=[pltpu.VMEM((ways, 1, chans), F32)],
        compiler_params=params(),
        name="backward_total",
    )(starts, p, p, state, g_mixed, lower, gain)


def backward_scan_kernel(
    starts_ref, pi_ref, pf_ref, state_ref, early_ref, gstate_ref, lower_ref, enter_ref, after_ref,
    gin_ref, gforget_ref, dlower_ref, held,
):
    ways, rows, chans = pi_ref.shape
    step_id = pl.program_id(0)
    block = pl.num_programs(0) - 1 - step_id
    starts = [starts_ref[i] for i in range(starts_ref.shape[0])]
    iota = lax.broadcasted_iota(jnp.int32, (8, chans), 0)

    @pl.when(step_id == 0)
    def _():
        held[...] = after_ref[...]
        dlower_ref[...] = jnp.zeros_like(dlower_ref)

    for t in range(ways):
        lower = lower_ref[t]
        first = jnp.where(block == 0, enter_ref[t], early_ref[t, 7:8])

        def eight(at, after, before):
            p_in = pi_ref[t, pl.ds(at, 8), :]
            p_forget = pf_ref[t, pl.ds(at, 8), :]
            grad = gstate_ref[t, pl.ds(at, 8), :]
            state = state_ref[t, pl.ds(at, 8), :]
            sig, lam, keep = gates(None, p_forget, lower, iota + (at + block * rows), starts)
            a = lam * keep
            b = a * grad
            for s in (1, 2, 4):
                near = iota < 8 - s
                b = jnp.where(near, a * pltpu.roll(b, 8 - s, 0) + b, b)
                a = jnp.where(near, a * pltpu.roll(a, 8 - s, 0), a)
            handed = a * after + b
            carry = grad + jnp.where(iota == 7, after, pltpu.roll(handed, 7, 0))
            previous = jnp.where(iota == 0, before, pltpu.roll(state, 1, 0))
            sig_in = sigmoid(p_in)
            act = p_in * sig_in
            g_lam = carry * previous * keep - carry * act
            g_in = carry * (1.0 - lam) * (sig_in * (1.0 + p_in * (1.0 - sig_in)))
            lower_part = g_lam * (1.0 - sig)
            g_forget = lower_part * (1.0 - lower) * sig
            return handed[0:1], g_in, g_forget, lower_part

        def step(k, carry):
            after, total = carry
            at = pl.multiple_of(rows - 16 - k * 16, 16)
            middle = state_ref[t, pl.ds(at, 8), :][7:8]
            ahead = jnp.maximum(at - 8, 0)
            held_before = state_ref[t, pl.ds(pl.multiple_of(ahead, 8), 8), :][7:8]
            before = jnp.where(at == 0, first, held_before)
            after, in_late, forget_late, part_late = eight(pl.multiple_of(at + 8, 8), after, middle)
            after, in_early, forget_early, part_early = eight(at, after, before)
            gin_ref[t, pl.ds(at, 16), :] = jnp.concatenate([in_early, in_late], 0).astype(BF16)
            gforget_ref[t, pl.ds(at, 16), :] = jnp.concatenate([forget_early, forget_late], 0).astype(BF16)
            return after, total + part_late + part_early

        after, total = lax.fori_loop(
            0, rows // 16, step, (held[t], jnp.zeros((8, chans), F32))
        )
        held[t] = after
        dlower_ref[t] += total


def backward_scan(p, state, g_state, lower, starts, enter, after):
    ways, rows, wide = p.shape
    chans = wide // 3
    part = min(rows, 128)
    last = rows // part - 1
    block = pl.BlockSpec((ways, part, chans), lambda i: (0, last - i, 0))
    eights = part // 8
    return pl.pallas_call(
        backward_scan_kernel,
        grid=(rows // part,),
        in_specs=[
            pl.BlockSpec(memory_space=pltpu.SMEM),
            pl.BlockSpec((ways, part, chans), lambda i: (0, last - i, 0)),
            pl.BlockSpec((ways, part, chans), lambda i: (0, last - i, 1)),
            block,
            pl.BlockSpec((ways, 8, chans), lambda i: (0, jnp.maximum((last - i) * eights - 1, 0), 0)),
            block,
            whole((ways, 1, chans)),
            whole((ways, 1, chans)),
            whole((ways, 1, chans)),
        ],
        out_specs=[block, block, whole((ways, 8, chans))],
        out_shape=[
            jax.ShapeDtypeStruct((ways, rows, chans), BF16),
            jax.ShapeDtypeStruct((ways, rows, chans), BF16),
            jax.ShapeDtypeStruct((ways, 8, chans), F32),
        ],
        scratch_shapes=[pltpu.VMEM((ways, 1, chans), F32)],
        compiler_params=params(),
        name="backward_scan",
    )(starts, p, p, state, state, g_state, lower, enter, after)


def branch_kernel(mixed_ref, w_ref, x_ref, gain_ref, resid_ref, middle_ref):
    ways = mixed_ref.shape[0]
    total = x_ref[...].astype(F32)
    acc = nn(mixed_ref[0], w_ref[0])
    for t in range(1, ways):
        acc += nn(mixed_ref[t], w_ref[t])
    resid = total + acc
    resid_ref[...] = resid
    inverse = lax.rsqrt(jnp.mean(resid * resid, axis=1, keepdims=True) + EPS)
    middle_ref[...] = (resid * inverse * gain_ref[...]).astype(BF16)


def branch(mixed, w_out, tokens, gain):
    ways, rows, chans = mixed.shape
    width = tokens.shape[1]
    part = min(rows, 256)
    line = pl.BlockSpec((part, width), lambda i: (i, 0))
    return pl.pallas_call(
        branch_kernel,
        grid=(rows // part,),
        in_specs=[
            pl.BlockSpec((ways, part, chans), lambda i: (0, i, 0)),
            whole((ways, chans, width)),
            line,
            whole((1, width)),
        ],
        out_specs=[line, line],
        out_shape=[
            jax.ShapeDtypeStruct((rows, width), F32),
            jax.ShapeDtypeStruct((rows, width), BF16),
        ],
        compiler_params=params(),
        name="branch",
    )(mixed, w_out, tokens, gain)


def up_kernel(x_ref, up_ref, glu_ref, hidden_ref, act_ref, slope_ref):
    x = x_ref[...]
    glu = nn(x, glu_ref[0])
    sig = sigmoid(glu)
    act = glu * sig
    up = nn(x, up_ref[0])
    hidden_ref[0] = (act * up).astype(BF16)
    act_ref[0] = act.astype(BF16)
    slope_ref[0] = (up * (sig * (1.0 + glu * (1.0 - sig)))).astype(BF16)


def feed_up(middle, w_up, w_glu):
    rows, width = middle.shape
    ways, _, units = w_up.shape
    part = min(rows, 512)
    weights = pl.BlockSpec((1, width, units), lambda t, i: (t, 0, 0))
    out = pl.BlockSpec((1, part, units), lambda t, i: (t, i, 0))
    return pl.pallas_call(
        up_kernel,
        grid=(ways, rows // part),
        in_specs=[pl.BlockSpec((part, width), lambda t, i: (i, 0)), weights, weights],
        out_specs=[out, out, out],
        out_shape=[jax.ShapeDtypeStruct((ways, rows, units), BF16)] * 3,
        compiler_params=params(),
        name="feed_up",
    )(middle, w_up, w_glu)


def down_kernel(h_ref, w_ref, resid_ref, o_ref):
    acc = nn(h_ref[0], w_ref[0])
    for t in range(1, h_ref.shape[0]):
        acc += nn(h_ref[t], w_ref[t])
    o_ref[...] = (resid_ref[...] + acc).astype(BF16)


def feed_down(hidden, w_down, resid):
    ways, rows, units = hidden.shape
    width = w_down.shape[2]
    part = 512
    return pl.pallas_call(
        down_kernel,
        grid=(width // part,),
        in_specs=[
            whole((ways, rows, units)),
            pl.BlockSpec((ways, units, part), lambda j: (0, 0, j)),
            pl.BlockSpec((rows, part), lambda j: (0, j)),
        ],
        out_specs=pl.BlockSpec((rows, part), lambda j: (0, j)),
        out_shape=jax.ShapeDtypeStruct((rows, width), BF16),
        compiler_params=params(),
        name="feed_down",
    )(hidden, w_down, resid)


def hidden_grad_kernel(dy_ref, w_ref, act_ref, slope_ref, gup_ref, gglu_ref):
    g_hidden = nt(dy_ref[...], w_ref[0])
    gup_ref[0] = (g_hidden * act_ref[0].astype(F32)).astype(BF16)
    gglu_ref[0] = (g_hidden * slope_ref[0].astype(F32)).astype(BF16)


def hidden_grad(dy, w_down, act, slope):
    rows, width = dy.shape
    ways, units, _ = w_down.shape
    part = min(rows, 512)
    out = pl.BlockSpec((1, part, units), lambda t, i: (t, i, 0))
    return pl.pallas_call(
        hidden_grad_kernel,
        grid=(ways, rows // part),
        in_specs=[
            pl.BlockSpec((part, width), lambda t, i: (i, 0)),
            pl.BlockSpec((1, units, width), lambda t, i: (t, 0, 0)),
            out,
            out,
        ],
        out_specs=[out, out],
        out_shape=[jax.ShapeDtypeStruct((ways, rows, units), BF16)] * 2,
        compiler_params=params(),
        name="hidden_grad",
    )(dy, w_down, act, slope)


def back_kernel(n, *refs):
    g_refs, w_refs, o_ref = refs[:n], refs[n : 2 * n], refs[2 * n]
    acc = nt(g_refs[0][0], w_refs[0][0])
    for g_ref, w_ref in zip(g_refs[1:], w_refs[1:]):
        acc += nt(g_ref[0], w_ref[0])
    first = pl.program_id(1) == 0

    @pl.when(first)
    def _():
        o_ref[...] = acc

    @pl.when(jnp.logical_not(first))
    def _():
        o_ref[...] += acc


def back(grads, weights, picks, units):
    ways, rows, _ = grads[0].shape
    width = weights[0].shape[1]
    part = min(width, 1024)
    return pl.pallas_call(
        functools.partial(back_kernel, len(grads)),
        grid=(width // part, ways),
        in_specs=[pl.BlockSpec((1, rows, units), lambda j, t: (t, 0, 0)) for _ in grads]
        + [pl.BlockSpec((1, part, units), functools.partial(lambda k, j, t: (t, j, k), k)) for k in picks],
        out_specs=pl.BlockSpec((rows, part), lambda j, t: (0, j)),
        out_shape=jax.ShapeDtypeStruct((rows, width), F32),
        compiler_params=params(),
        name="back",
    )(*grads, *weights)


def mixed_grad_kernel(g_ref, w_ref, o_ref):
    o_ref[0] = nt(g_ref[...], w_ref[0])


def mixed_grad(g_branch, w_out):
    rows, width = g_branch.shape
    ways, chans, _ = w_out.shape
    return pl.pallas_call(
        mixed_grad_kernel,
        grid=(ways,),
        in_specs=[whole((rows, width)), pl.BlockSpec((1, chans, width), lambda t: (t, 0, 0))],
        out_specs=pl.BlockSpec((1, rows, chans), lambda t: (t, 0, 0)),
        out_shape=jax.ShapeDtypeStruct((ways, rows, chans), F32),
        compiler_params=params(),
        name="mixed_grad",
    )(g_branch, w_out)


def by_rows_kernel(chips, n, *refs):
    left_ref, right_refs, o_ref = refs[0], refs[1 : 1 + n], refs[-1]
    add_ref = refs[1 + n] if len(refs) == n + 3 else None
    each = o_ref.shape[2]
    at = 0
    for right_ref in right_refs:
        wide = right_ref.shape[2]
        acc = tn(left_ref[...], right_ref[0])
        for j in range(chips):
            got = acc[j * each : (j + 1) * each]
            if add_ref is not None:
                got = got + add_ref[j, 0, :, at : at + wide].astype(F32)
            o_ref[j, 0, :, at : at + wide] = got.astype(BF16)
        at += wide


def by_rows(left, rights, add, chips):
    rows, tall = left.shape
    ways = rights[0].shape[0]
    each = tall // chips
    wide = sum(r.shape[2] for r in rights)
    block = pl.BlockSpec((chips, 1, each, wide), lambda t: (0, t, 0, 0))
    return pl.pallas_call(
        functools.partial(by_rows_kernel, chips, len(rights)),
        grid=(ways,),
        in_specs=[whole((rows, tall))]
        + [pl.BlockSpec((1, rows, r.shape[2]), lambda t: (t, 0, 0)) for r in rights]
        + ([block] if add is not None else []),
        out_specs=block,
        out_shape=jax.ShapeDtypeStruct((chips, ways, each, wide), BF16),
        compiler_params=params(),
        name="by_rows",
    )(left, *rights, *([add] if add is not None else []))


def by_cols_kernel(chips, *refs):
    left_ref, right_ref, o_ref = refs[0], refs[1], refs[-1]
    add_ref = refs[2] if len(refs) == 4 else None
    each = o_ref.shape[3]
    acc = tn(left_ref[0], right_ref[...])
    for j in range(chips):
        got = acc[:, j * each : (j + 1) * each]
        if add_ref is not None:
            got = got + add_ref[j, 0].astype(F32)
        o_ref[j, 0] = got.astype(BF16)


def by_cols(left, right, add, chips):
    ways, rows, tall = left.shape
    wide = right.shape[1]
    each = wide // chips
    block = pl.BlockSpec((chips, 1, tall, each), lambda t: (0, t, 0, 0))
    return pl.pallas_call(
        functools.partial(by_cols_kernel, chips),
        grid=(ways,),
        in_specs=[pl.BlockSpec((1, rows, tall), lambda t: (t, 0, 0)), whole((rows, wide))]
        + ([block] if add is not None else []),
        out_specs=block,
        out_shape=jax.ShapeDtypeStruct((chips, ways, tall, each), BF16),
        compiler_params=params(),
        name="by_cols",
    )(left, right, *([add] if add is not None else []))


def norm_pullback(upstream_gradient, unit_rows, inverse_rms, gain_vector):
    scaled_rows = upstream_gradient * gain_vector
    return inverse_rms * (
        scaled_rows - unit_rows * jnp.mean(scaled_rows * unit_rows, axis=1, keepdims=True)
    )


SWAP = ((0, 1), (1, 0))


def local(
    tokens,
    lengths,
    first_norm_gain,
    w_in,
    w_forget,
    w_gate,
    lower_bound,
    gate_gain,
    w_out,
    feedforward_gain,
    w_up,
    w_glu,
    w_down,
    cotangent,
):
    rows, width = tokens.shape
    chans = w_in.shape[1]
    units = w_up.shape[1]
    ways = lax.axis_size("tensor")
    chips = lax.axis_size("chip")
    groups = 2 * chips
    way = lax.axis_index("tensor")
    core = lax.axis_index("core")
    group = lax.axis_index("chip") * 2 + core
    every = ("tensor", "chip", "core")

    def mine(weights):
        tall = weights.shape[0] // groups
        return lax.dynamic_slice_in_dim(weights, group * tall, tall, 0)

    def gather(piece):
        return lax.all_gather(piece, every, axis=0, tiled=True)

    w3 = gather(jnp.concatenate([mine(w_in), mine(w_forget), mine(w_gate)], axis=1))
    w3 = w3.reshape(ways, width, 3 * chans)
    w_out_all = gather(mine(w_out)).reshape(ways, chans, width)
    w_glu_all = gather(mine(w_glu)).reshape(ways, width, units)
    w_up_all = gather(mine(w_up)).reshape(ways, width, units)
    w_down_all = gather(mine(w_down)).reshape(ways, units, width)

    lower = lax.all_gather(lower_bound, "tensor", axis=0).reshape(ways, 1, chans)
    gain = lax.all_gather(gate_gain, "tensor", axis=0).reshape(ways, 1, chans)
    l0, l1 = lengths[0, 0], lengths[0, 1]
    starts = jnp.stack([jnp.zeros_like(l0), l0, l0 + l1]) - way * rows

    x = tokens.astype(F32)
    inverse1 = lax.rsqrt(jnp.mean(x * x, axis=1, keepdims=True) + EPS)
    normed = (x * inverse1 * first_norm_gain).astype(BF16)

    p = project(normed, w3, chans)
    totals = forward_total(p, lower, starts)
    all_totals = lax.all_gather(totals, "tensor", axis=0)
    enter = jnp.zeros((ways, 1, chans), F32)
    seen = jnp.zeros((ways, 1, chans), F32)
    for k in range(ways - 1):
        seen = all_totals[k, :, 0:1] * seen + all_totals[k, :, 1:2]
        enter = jnp.where(way == k + 1, seen, enter)
    state, mixed, lam_sum = forward_scan(p, lower, gain, starts, enter)

    resid, middle = branch(mixed, w_out_all, tokens, feedforward_gain.reshape(1, width))
    hidden, act, slope = feed_up(middle, w_up_all, w_glu_all)

    def halves(array):
        cut = array.reshape(rows, chips, 2, width // groups)
        pick = lambda c: lax.dynamic_index_in_dim(cut, c, 2, False).reshape(rows, width // 2)
        return pick(1 - core), pick(core)

    def swap(array):
        return lax.ppermute(array, "core", SWAP)

    def scatter(array):
        array = lax.psum_scatter(array, "chip", scatter_dimension=0, tiled=True)
        array = array.reshape(array.shape[1:])
        array = lax.psum_scatter(array, "tensor", scatter_dimension=0, tiled=True)
        return array.reshape(array.shape[1:]).astype(F32)

    def grad_rows(left, rights):
        theirs, ours = left
        return scatter(by_rows(ours, rights, swap(by_rows(theirs, rights, None, chips)), chips))

    def grad_cols(left, right):
        theirs, ours = right
        return scatter(by_cols(left, ours, swap(by_cols(left, theirs, None, chips)), chips))

    grad_w_down = grad_cols(hidden, halves(cotangent))
    output = feed_down(hidden, w_down_all, resid)

    g_up, g_glu = hidden_grad(cotangent, w_down_all, act, slope)
    middle_halves = halves(middle)
    grad_w_up = grad_rows(middle_halves, [g_up])
    grad_w_glu = grad_rows(middle_halves, [g_glu])
    g_middle = back([g_up, g_glu], [w_up_all, w_glu_all], [0, 0], units)

    inverse2 = lax.rsqrt(jnp.mean(resid * resid, axis=1, keepdims=True) + EPS)
    unit2 = resid * inverse2
    mlp_gain_part = jnp.sum(g_middle * unit2, axis=0)
    g_resid = cotangent.astype(F32) + norm_pullback(g_middle, unit2, inverse2, feedforward_gain)
    g_branch = g_resid.astype(BF16)
    grad_w_out = grad_cols(mixed, halves(g_branch))
    g_mixed = mixed_grad(g_branch, w_out_all)

    g_state, g_gate, gain_part, back_totals = backward_total(p, state, g_mixed, lower, gain, starts)
    all_back = lax.all_gather(back_totals, "tensor", axis=0)
    after = jnp.zeros((ways, 1, chans), F32)
    seen = jnp.zeros((ways, 1, chans), F32)
    for k in range(ways - 1, 0, -1):
        seen = all_totals[k, :, 0:1] * seen + all_back[k]
        after = jnp.where(way == k - 1, seen, after)
    g_in, g_forget, lower_part = backward_scan(p, state, g_state, lower, starts, enter, after)

    normed_halves = halves(normed)
    grad_three = grad_rows(normed_halves, [g_in, g_forget, g_gate])
    g_normed = back([g_in, g_forget, g_gate], [w3, w3, w3], [0, 1, 2], chans)

    unit1 = x * inverse1
    norm_gain_part = jnp.sum(g_normed * unit1, axis=0)
    token_gradient = g_resid + norm_pullback(g_normed, unit1, inverse1, first_norm_gain)

    small = jnp.stack(
        [
            norm_gain_part,
            mlp_gain_part,
            jnp.sum(gain_part, axis=1).reshape(width),
            jnp.sum(lower_part, axis=1).reshape(width),
            jnp.sum(lam_sum, axis=1).reshape(width),
        ]
    )
    small = lax.psum(small, every)
    mean_forget = jnp.sum(small[4]) / (rows * ways * groups * width)
    return (
        output,
        token_gradient,
        small[0],
        grad_three[:, :chans],
        grad_three[:, chans : 2 * chans],
        grad_three[:, 2 * chans :],
        small[3],
        small[2],
        grad_w_out,
        small[1],
        grad_w_up,
        grad_w_glu,
        grad_w_down,
        mean_forget,
    )


def solution(mesh):
    groups, ways = mesh.shape["dp"], mesh.shape["tensor"]
    parts = Mesh(mesh.devices.reshape(groups // 2, 2, ways), ("chip", "core", "tensor"))
    dp = ("chip", "core")
    tokens = P(("chip", "core", "tensor"), None)
    return jax.shard_map(
        local,
        mesh=parts,
        in_specs=(
            tokens,
            P(dp, None),
            P(),
            P(None, "tensor"),
            P(None, "tensor"),
            P(None, "tensor"),
            P("tensor"),
            P("tensor"),
            P("tensor", None),
            P(),
            P(None, "tensor"),
            P(None, "tensor"),
            P("tensor", None),
            tokens,
        ),
        out_specs=(
            tokens,
            tokens,
            P(),
            P(dp, "tensor"),
            P(dp, "tensor"),
            P(dp, "tensor"),
            P(),
            P(),
            P("tensor", dp),
            P(),
            P(dp, "tensor"),
            P(dp, "tensor"),
            P("tensor", dp),
            P(),
        ),
        check_vma=False,
    )
```

time: 4430 us -> 1730 us (0.39)
  waiting for transfers between devices: 2490 us -> 819 us
  local copies, waits for them, and re-layouts: 1050 us -> 175 us
  Pallas kernels: 0 us -> 549 us
  matrix products: 468 us -> 0 us
  other arithmetic: 289 us -> 62.5 us
    reduce_scatter x11 -> x5, waiting for transfers between devices: 1670 us -> 119 us  [scatter(): array = lax.psum_scatter(array, 'tensor', scatter_dimension=0, tiled=True)]
    slice x156 -> x2, local copies, waits for them, and re-layouts: 727 us -> 1.76 us  [the longest x1 1.18 us: local(): grad_three[:, 2 * chans:]]
    pallas_call x0 -> x22, Pallas kernels: none -> 549 us  [the longest x6 114 us: by_rows(): pl.pallas_call(functools.partial(by_rows_kernel, chips, len(rights)), gri...]
    dot_general x15 -> x0, matrix products: 468 us -> none  [the longest x5 158 us: over_cols(): lax.dot_general(left, right, (((1,), (1,)), ((), ())), preferred_element_...]
    all_gather x4 -> x5, waiting for transfers between devices: 818 us -> 467 us  [gather(): return lax.all_gather(piece, every, axis=0, tiled=True)]
    pad x44 -> x0, local copies, waits for them, and re-layouts: 238 us -> none  [the longest x22 119 us: local(): _, state = lax.associative_scan(affine, (decay, inject), axis=0)]
    unnamed x15 -> x20, waiting for transfers between devices: 2.1 us -> 178 us
    dynamic_slice x0 -> x10, local copies, waits for them, and re-layouts: none -> 122 us  [the longest x4 113 us: halves(): lax.dynamic_index_in_dim(cut, c, 2, False).reshape(rows, width // 2)]
  transfers between devices with their start and end apart: 15 -> 20, of which waited for: 10 -> 13; matrix products, arithmetic and copies ran while one was open for 25% -> 10% of each run, Pallas kernels for 0% -> 25%
where the time goes in v1:
time: 1730 us; the launch traced here: 1720 us
  waiting for transfers between devices  819 us (47%)
  Pallas kernels  549 us (32%)
  local copies, waits for them, and re-layouts  175 us (10%)
  blocking collectives  96.6 us (6%)
  other arithmetic  62.5 us (4%)
  between operations  17.7 us (1%)
    all_gather x5, waiting for transfers between devices, gather(): return lax.all_gather(piece, every, axis=0, tiled=True)  467 us
    unnamed x20, waiting for transfers between devices  178 us
    reduce_scatter x5, waiting for transfers between devices, scatter(): array = lax.psum_scatter(array, 'tensor', scatter_dimension=0, tiled=True)  119 us
    pallas_call x6, Pallas kernels, by_rows(): pl.pallas_call(functools.partial(by_rows_kernel, chips, len(rights)), gri...  114 us
    dynamic_slice x4, local copies, waits for them, and re-layouts, halves(): lax.dynamic_index_in_dim(cut, c, 2, False).reshape(rows, width // 2)  113 us
    pallas_call x2, Pallas kernels, back(): pl.pallas_call(functools.partial(back_kernel, len(grads)), grid=(width //...  99.9 us
    pallas_call x1, Pallas kernels, feed_up(): pl.pallas_call(up_kernel, grid=(ways, rows // part), in_specs=[pl.BlockSp...  60.8 us
    ppermute x5, waiting for transfers between devices, swap(): return lax.ppermute(array, 'core', SWAP)  54.8 us
  transfers between devices with their start and end apart: 20, of which 13 were waited for; matrix products, arithmetic and copies ran while one was open for 10% of the time, Pallas kernels for 25%

profile of v1, /device:TPU:0, one launch (start us, length us, event | category | flops | bytes accessed | tf_op | source)
XLA Modules:
  0.0 1721.7 jit_solution(17973053117859736458)
XLA Ops:
  55.4 113.7 %all-gather.12.cloned.1.call-done = bf16[8192,1536]{1,0:T(8,128)(2,1)} async-done(((bf16[256,1536]{1,0:T(8,128)(2,1)}), bf16[8192,1536]{1,0:T(8,128)(2,1)}) %all-gather.12.cloned.1.call-update) | async-done | bytes 25165840 | tf_op jit(solution)/shard_map/all_gather | solution.py:651
  169.1 32.7 %project.1.p_ref.pf_ref.pg_ref.pi_ref = f32[4,1024,1536]{2,1,0:T(8,128)} custom-call(bf16[1024,2048]{1,0:T(8,128)(2,1)} %fusion.4.x_ref, bf16[4,2048,1536]{2,1,0:T(8,128)(2,1)} %bitcast.104), custom_call_target="tpu_custom_call" | custom-call | tf_op jit(solution)/shard_map/project/pallas_call | solution.py:49
  230.3 21.8 %forward_scan.1 = (f32[4,1024,512]{2,1,0:T(8,128)}, bf16[4,1024,512]{2,1,0:T(8,128)(2,1)}, f32[4,8,512]{2,1,0:T(8,128)}) custom-call(s32[3]{0:T(128)} %add_subtract_fusion.starts_ref, f32[4,1024,1536]{2,1,0:T(8,128)} %project.1.p_ref.pf_ref.pg_ref.pi_ref, f32[4,1,512]{2,1,0:T(1,128)} %all-gather.4.lower_ref, f32[4,1,512]{2,1,0:T(1,128)} %all-gather.5.gain_ref, ...), custom_call_target="tpu_custom_call" | custom-call | tf_op jit(solution)/shard_map/forward_scan/pallas_call | solution.py:170
  268.0 126.9 %all-gather.16.cloned.1.call-done = bf16[8192,1408]{1,0:T(8,128)(2,1)} async-done(((bf16[256,1408]{1,0:T(8,128)(2,1)}), bf16[8192,1408]{1,0:T(8,128)(2,1)}) %all-gather.16.cloned.1.call-update) | async-done | bytes 23068688 | tf_op jit(solution)/shard_map/all_gather | solution.py:651
  394.9 146.1 %all-gather.18.cloned.1.call-done = bf16[8192,1408]{1,0:T(8,128)(2,1)} async-done(((bf16[256,1408]{1,0:T(8,128)(2,1)}), bf16[8192,1408]{1,0:T(8,128)(2,1)}) %all-gather.18.cloned.1.call-update) | async-done | bytes 23068688 | tf_op jit(solution)/shard_map/all_gather | solution.py:651
  540.9 60.8 %feed_up.1 = (bf16[4,1024,1408]{2,1,0:T(8,128)(2,1)}, bf16[4,1024,1408]{2,1,0:T(8,128)(2,1)}, bf16[4,1024,1408]{2,1,0:T(8,128)(2,1)}) custom-call(bf16[1024,2048]{1,0:T(8,128)(2,1)} %get-tuple-element.32.x_ref, bf16[4,2048,1408]{2,1,0:T(8,128)(2,1)} %bitcast.108, bf16[4,2048,1408]{2,1,0:T(8,128)(2,1)} %bitcast.110), custom_call_target="tpu_custom_call" | custom-call | tf_op jit(solution)/shard_map/feed_up/pallas_call | solution.py:431
  605.7 80.7 %all-gather.20.cloned.1.call-done = bf16[5632,2048]{1,0:T(8,128)(2,1)} async-done(((bf16[176,2048]{1,0:T(8,128)(2,1)}), bf16[5632,2048]{1,0:T(8,128)(2,1)}) %all-gather.20.cloned.1.call-update) | async-done | bytes 23068688 | tf_op jit(solution)/shard_map/all_gather | solution.py:651
  686.4 41.9 %hidden_grad.1 = (bf16[4,1024,1408]{2,1,0:T(8,128)(2,1)}, bf16[4,1024,1408]{2,1,0:T(8,128)(2,1)}) custom-call(bf16[1024,2048]{1,0:T(8,128)(2,1)} %dy_ref.1, bf16[4,1408,2048]{2,1,0:T(8,128)(2,1)} %bitcast.112, bf16[4,1024,1408]{2,1,0:T(8,128)(2,1)} %get-tuple-element.35.act_ref, bf16[4,1024,1408]{2,1,0:T(8,128)(2,1)} %get-tuple-element.36.slope_ref), custom_call_target="tpu_custom_call" | custom-call | tf_op jit(solution)/shard_map/hidden_grad/pallas_call | solution.py:479
  728.4 63.3 %back.2 = f32[1024,2048]{1,0:T(8,128)} custom-call(bf16[4,1024,1408]{2,1,0:T(8,128)(2,1)} %get-tuple-element.37.refs_0_.refs_1_, bf16[4,1024,1408]{2,1,0:T(8,128)(2,1)} %get-tuple-element.38.refs_1_, bf16[4,2048,1408]{2,1,0:T(8,128)(2,1)} %bitcast.109, bf16[4,2048,1408]{2,1,0:T(8,128)(2,1)} %bitcast.111), custom_call_target="tpu_custom_call" | custom-call | tf_op jit(solution)/shard_map/back/pallas_call | solution.py:515
  814.8 29.4 %dynamic-slice_reduce_fusion.4 = (bf16[1024,4,256]{2,1,0:T(4,128)(2,1)S(1)}, bf16[1024,4,256]{2,1,0:T(4,128)(2,1)}) fusion(bf16[1024,4,2,256]{3,2,1,0:T(2,128)(2,1)} %reshape.340, s32[]{:T(128)S(6)} %select_n.106, s32[]{:T(128)S(6)} %select_n.105), kind=kLoop, calls=%fused_computation.21 | loop fusion | bytes 8388616 | tf_op jit(solution)/shard_map/jit(dynamic_index_in_dim)/dynamic_slice | solution.py:684
  862.5 27.8 %dynamic-slice_reduce_fusion.2 = (bf16[1024,4,256]{2,1,0:T(4,128)(2,1)S(1)}, bf16[1024,4,256]{2,1,0:T(4,128)(2,1)S(1)}) fusion(bf16[1024,4,2,256]{3,2,1,0:T(2,128)(2,1)} %reshape.344, s32[]{:T(128)S(6)} %select_n.106, s32[]{:T(128)S(6)} %select_n.105), kind=kLoop, calls=%fused_computation.19 | loop fusion | bytes 8388616 | tf_op jit(solution)/shard_map/jit(dynamic_index_in_dim)/dynamic_slice | solution.py:684
  983.9 19.8 %by_rows.9 = bf16[4,4,256,1408]{3,2,1,0:T(8,128)(2,1)} custom-call(bf16[1024,1024]{1,0:T(8,128)(2,1)} %bitcast.119, bf16[4,1024,1408]{2,1,0:T(8,128)(2,1)} %get-tuple-element.37.refs_0_.refs_1_, bf16[4,4,256,1408]{3,2,1,0:T(8,128)(2,1)} %collective-permute-done.2.refs_2_), custom_call_target="tpu_custom_call" | custom-call | tf_op jit(solution)/shard_map/by_rows/pallas_call | solution.py:567
  1011.8 27.8 %dynamic-slice_reduce_fusion = (bf16[1024,4,256]{2,1,0:T(4,128)(2,1)S(1)}, bf16[1024,4,256]{2,1,0:T(4,128)(2,1)S(1)}) fusion(bf16[1024,4,2,256]{3,2,1,0:T(2,128)(2,1)} %reshape.349, s32[]{:T(128)S(6)} %select_n.106, s32[]{:T(128)S(6)} %select_n.105), kind=kLoop, calls=%fused_computation.17 | loop fusion | bytes 8388616 | tf_op jit(solution)/shard_map/jit(dynamic_index_in_dim)/dynamic_slice | solution.py:684
  1103.4 27.8 %dynamic-slice_reduce_fusion.6 = (bf16[1024,4,256]{2,1,0:T(4,128)(2,1)S(1)}, bf16[1024,4,256]{2,1,0:T(4,128)(2,1)S(1)}) fusion(bf16[1024,4,2,256]{3,2,1,0:T(2,128)(2,1)} %reshape.336, s32[]{:T(128)S(6)} %select_n.106, s32[]{:T(128)S(6)} %select_n.105), kind=kLoop, calls=%fused_computation.23 | loop fusion | bytes 8388616 | tf_op jit(solution)/shard_map/jit(dynamic_index_in_dim)/dynamic_slice | solution.py:684
  1147.2 22.8 %backward_total.1 = (f32[4,1024,512]{2,1,0:T(8,128)}, bf16[4,1024,512]{2,1,0:T(8,128)(2,1)}, f32[4,8,512]{2,1,0:T(8,128)}, f32[4,1,512]{2,1,0:T(1,128)}) custom-call(s32[3]{0:T(128)} %add_subtract_fusion.starts_ref, f32[4,1024,1536]{2,1,0:T(8,128)} %project.1.p_ref.pf_ref.pg_ref.pi_ref, f32[4,1024,1536]{2,1,0:T(8,128)} %project.1.p_ref.pf_ref.pg_ref.pi_ref, ...), custom_call_target="tpu_custom_call" | custom-call | tf_op jit(solution)/shard_map/backward_total/pallas_call | solution.py:258
  1184.7 24.2 %backward_scan.1 = (bf16[4,1024,512]{2,1,0:T(8,128)(2,1)}, bf16[4,1024,512]{2,1,0:T(8,128)(2,1)}, f32[4,8,512]{2,1,0:T(8,128)}) custom-call(s32[3]{0:T(128)} %add_subtract_fusion.starts_ref, f32[4,1024,1536]{2,1,0:T(8,128)} %project.1.p_ref.pf_ref.pg_ref.pi_ref, f32[4,1024,1536]{2,1,0:T(8,128)} %project.1.p_ref.pf_ref.pg_ref.pi_ref, ...), custom_call_target="tpu_custom_call" | custom-call | tf_op jit(solution)/shard_map/backward_scan/pallas_call | solution.py:352
  1247.2 19.8 %by_rows.7 = bf16[4,4,256,1536]{3,2,1,0:T(8,128)(2,1)} custom-call(bf16[1024,1024]{1,0:T(8,128)(2,1)} %bitcast.126, bf16[4,1024,512]{2,1,0:T(8,128)(2,1)} %get-tuple-element.42.refs_0_.refs_1_, bf16[4,1024,512]{2,1,0:T(8,128)(2,1)} %get-tuple-element.43.refs_1_.refs_2_, bf16[4,1024,512]{2,1,0:T(8,128)(2,1)} %get-tuple-element.44.refs_2_.refs_3_, ...), custom_call_target="tpu_custom_call" | custom-call | tf_op jit(solution)/shard_map/by_rows/pallas_call | solution.py:567
  1269.1 52.1 %reduce-scatter.39.cloned.1.call-done = bf16[1,4,1408,256]{3,2,1,0:T(8,128)(2,1)} async-done(((bf16[4,4,1408,256]{3,2,1,0:T(8,128)(2,1)}), bf16[1,4,1408,256]{3,2,1,0:T(8,128)(2,1)}) %reduce-scatter.39.cloned.1.call-update) | async-done | bytes 2883600
  1321.3 123.9 %reduce-scatter.31.cloned.1.call-done = bf16[1,4,256,1536]{3,2,1,0:T(8,128)(2,1)} async-done(((bf16[4,4,256,1536]{3,2,1,0:T(8,128)(2,1)}), bf16[1,4,256,1536]{3,2,1,0:T(8,128)(2,1)}) %reduce-scatter.31.cloned.1.call-update) | async-done | bytes 3145744
  1445.2 36.6 %back.3 = f32[1024,2048]{1,0:T(8,128)} custom-call(bf16[4,1024,512]{2,1,0:T(8,128)(2,1)} %get-tuple-element.42.refs_0_.refs_1_, bf16[4,1024,512]{2,1,0:T(8,128)(2,1)} %get-tuple-element.43.refs_1_.refs_2_, bf16[4,1024,512]{2,1,0:T(8,128)(2,1)} %get-tuple-element.44.refs_2_.refs_3_, bf16[4,2048,1536]{2,1,0:T(8,128)(2,1)} %bitcast.105, ...), custom_call_target="tpu_custom_call" | custom-call | tf_op jit(solution)/shard_map/back/pallas_call | solution.py:515
  1481.8 34.3 %feed_down.1 = bf16[1024,2048]{1,0:T(8,128)(2,1)} custom-call(bf16[4,1024,1408]{2,1,0:T(8,128)(2,1)} %get-tuple-element.33.h_ref.refs_0_, bf16[4,1408,2048]{2,1,0:T(8,128)(2,1)} %bitcast.113, f32[1024,2048]{1,0:T(8,128)} %get-tuple-element.34.resid_ref), custom_call_target="tpu_custom_call" | custom-call | tf_op jit(solution)/shard_map/feed_down/pallas_call | solution.py:453
  1522.4 42.0 %psum.7 = f32[5,2048]{1,0:T(8,128)S(1)} all-reduce(f32[5,2048]{1,0:T(8,128)S(1)} %stack.19), channel_id=1, replica_groups=mesh['chip'=4,'core'=2,'tensor'=4] {'tensor','chip','core'}, use_global_device_ids=true, to_apply=%region_9.10 | all-reduce | flops 10240 | bytes 81920 | tf_op jit(solution)/shard_map/psum | solution.py:747
  1593.2 55.8 %reduce-scatter.29.cloned.1.call-done = bf16[1,1408,256]{2,1,0:T(8,128)(2,1)} async-done(((bf16[4,1408,256]{2,1,0:T(8,128)(2,1)}), bf16[1,1408,256]{2,1,0:T(8,128)(2,1)}) %reduce-scatter.29.cloned.1.call-update) | async-done | bytes 720912 | tf_op jit(solution)/shard_map/reduce_scatter | solution.py:693
  1651.3 60.0 %reduce-scatter.21.cloned.1.call-done = bf16[1,256,1536]{2,1,0:T(8,128)(2,1)} async-done(((bf16[4,256,1536]{2,1,0:T(8,128)(2,1)}), bf16[1,256,1536]{2,1,0:T(8,128)(2,1)}) %reduce-scatter.21.cloned.1.call-update) | async-done | bytes 786448 | tf_op jit(solution)/shard_map/reduce_scatter | solution.py:693
  (156 shorter events, 412.2 us)
Async XLA Ops:
  7.2 161.9 %all-gather.12.cloned.1.call-start = ((), (), s32[]{:S(2)}) async-start(), calls=%async_computation.10 | async-start | bytes 25952256 | tf_op jit(solution)/shard_map/all_gather | solution.py:651
  10.8 241.3 %all-gather.14.cloned.1.call-start = ((), (), s32[]{:S(2)}) async-start(), calls=%async_computation.11 | async-start | bytes 8650752 | tf_op jit(solution)/shard_map/all_gather | solution.py:651
  12.6 382.3 %all-gather.16.cloned.1.call-start = ((), (), s32[]{:S(2)}) async-start(), calls=%async_computation.12 | async-start | bytes 23789568 | tf_op jit(solution)/shard_map/all_gather | solution.py:651
  14.7 526.2 %all-gather.18.cloned.1.call-start = ((), (), s32[]{:S(2)}) async-start(), calls=%async_computation.13 | async-start | bytes 23789568 | tf_op jit(solution)/shard_map/all_gather | solution.py:651
  16.8 669.6 %all-gather.20.cloned.1.call-start = ((), (), s32[]{:S(2)}) async-start(), calls=%async_computation.14 | async-start | bytes 23789568 | tf_op jit(solution)/shard_map/all_gather | solution.py:651
  19.0 1248.1 %reduce-scatter.33.cloned.1.call-start = ((), (), s32[]{:S(2)}) async-start(), calls=%async_computation.21 | async-start | bytes 5242880
  52.3 149.4 %copy-start.10 = (f32[1024]{0:T(1024)}, f32[1024]{0:T(1024)S(1)}, u32[]{:S(2)}) copy-start(f32[1024]{0:T(1024)S(1)} %add_rsqrt_fusion.1) | copy-start | bytes 12292
  605.7 193.6 %copy-start.15 = (f32[1024]{0:T(1024)}, f32[1024]{0:T(1024)S(1)}, u32[]{:S(2)}) copy-start(f32[1024]{0:T(1024)S(1)} %add_rsqrt_fusion) | copy-start | bytes 12292
  728.4 63.3 %copy-start.6 = (f32[2048]{0:T(1024)S(1)}, f32[2048]{0:T(1024)}, u32[]{:S(2)}) copy-start(f32[2048]{0:T(1024)} %param.23) | copy-start | bytes 24580
  854.5 59.7 %collective-permute-start.1 = (bf16[4,4,512,256]{3,2,1,0:T(8,128)(2,1)}, bf16[4,4,512,256]{3,2,1,0:T(8,128)(2,1)}, u32[]{:S(2)}, u32[]{:S(2)}) collective-permute-start(bf16[4,4,512,256]{3,2,1,0:T(8,128)(2,1)} %by_cols.4), channel_id=1, source_target_pairs={{0,4},{4,0},{1,5},{5,1},{2,6},{6,2},{3,7},{7,3},{8,12},{12,8},{9,1... | collective-permute-start | bytes 12582920 | tf_op jit(solution)/shard_map/ppermute | solution.py:688
  910.5 18.1 %collective-permute-start.3 = (bf16[4,4,256,1408]{3,2,1,0:T(8,128)(2,1)}, bf16[4,4,256,1408]{3,2,1,0:T(8,128)(2,1)}, u32[]{:S(2)}, u32[]{:S(2)}) collective-permute-start(bf16[4,4,256,1408]{3,2,1,0:T(8,128)(2,1)} %by_rows.10), channel_id=1, source_target_pairs={{0,4},{4,0},{1,5},{5,1},{2,6},{6,2},{3,7},{7,3},{8,12},{12,8},{9,1... | collective-permute-start | bytes 34603016 | tf_op jit(solution)/shard_map/ppermute | solution.py:688
  923.4 344.4 %reduce-scatter.37.cloned.1.call-start = ((), (), s32[]{:S(2)}) async-start(), calls=%async_computation.23 | async-start | bytes 14417920
  947.9 320.5 %reduce-scatter.35.cloned.1.call-start = ((), (), s32[]{:S(2)}) async-start(), calls=%async_computation.22 | async-start | bytes 14417920
  965.9 18.0 %collective-permute-start.2 = (bf16[4,4,256,1408]{3,2,1,0:T(8,128)(2,1)}, bf16[4,4,256,1408]{3,2,1,0:T(8,128)(2,1)}, u32[]{:S(2)}, u32[]{:S(2)}) collective-permute-start(bf16[4,4,256,1408]{3,2,1,0:T(8,128)(2,1)} %by_rows.8), channel_id=1, source_target_pairs={{0,4},{4,0},{1,5},{5,1},{2,6},{6,2},{3,7},{7,3},{8,12},{12,8},{9,1... | collective-permute-start | bytes 34603016 | tf_op jit(solution)/shard_map/ppermute | solution.py:688
  1003.7 317.4 %reduce-scatter.39.cloned.1.call-start = ((), (), s32[]{:S(2)}) async-start(), calls=%async_computation.24 | async-start | bytes 14417920
  1058.5 18.0 %collective-permute-start.4 = (bf16[4,4,1408,256]{3,2,1,0:T(8,128)(2,1)}, bf16[4,4,1408,256]{3,2,1,0:T(8,128)(2,1)}, u32[]{:S(2)}, u32[]{:S(2)}) collective-permute-start(bf16[4,4,1408,256]{3,2,1,0:T(8,128)(2,1)} %by_cols.6), channel_id=1, source_target_pairs={{0,4},{4,0},{1,5},{5,1},{2,6},{6,2},{3,7},{7,3},{8,12},{12,8},{9,1... | collective-permute-start | bytes 34603016 | tf_op jit(solution)/shard_map/ppermute | solution.py:688
  1095.1 350.1 %reduce-scatter.31.cloned.1.call-start = ((), (), s32[]{:S(2)}) async-start(), calls=%async_computation.20 | async-start | bytes 15728640
  1227.7 19.5 %collective-permute-start = (bf16[4,4,256,1536]{3,2,1,0:T(8,128)(2,1)}, bf16[4,4,256,1536]{3,2,1,0:T(8,128)(2,1)}, u32[]{:S(2)}, u32[]{:S(2)}) collective-permute-start(bf16[4,4,256,1536]{3,2,1,0:T(8,128)(2,1)} %by_rows.6), channel_id=1, source_target_pairs={{0,4},{4,0},{1,5},{5,1},{2,6},{6,2},{3,7},{7,3},{8,12},{12,8},{9,1... | collective-permute-start | bytes 37748744 | tf_op jit(solution)/shard_map/ppermute | solution.py:688
  1267.0 316.2 %reduce-scatter.23.cloned.1.call-start = ((), (), s32[]{:S(2)}) async-start(), calls=%async_computation.16 | async-start | bytes 1310720 | tf_op jit(solution)/shard_map/reduce_scatter | solution.py:693
  1267.8 317.4 %reduce-scatter.27.cloned.1.call-start = ((), (), s32[]{:S(2)}) async-start(), calls=%async_computation.18 | async-start | bytes 3604480 | tf_op jit(solution)/shard_map/reduce_scatter | solution.py:693
  1268.3 322.6 %reduce-scatter.25.cloned.1.call-start = ((), (), s32[]{:S(2)}) async-start(), calls=%async_computation.17 | async-start | bytes 3604480 | tf_op jit(solution)/shard_map/reduce_scatter | solution.py:693
  1269.1 380.0 %reduce-scatter.29.cloned.1.call-start = ((), (), s32[]{:S(2)}) async-start(), calls=%async_computation.19 | async-start | bytes 3604480 | tf_op jit(solution)/shard_map/reduce_scatter | solution.py:693
  1321.2 390.1 %reduce-scatter.21.cloned.1.call-start = ((), (), s32[]{:S(2)}) async-start(), calls=%async_computation.15 | async-start | bytes 3932160 | tf_op jit(solution)/shard_map/reduce_scatter | solution.py:693
  1583.2 130.6 %copy-start.1 = (bf16[2048,512]{1,0:T(8,128)(2,1)S(1)}, bf16[2048,512]{1,0:T(8,128)(2,1)}, u32[]{:S(2)}) copy-start(bf16[2048,512]{1,0:T(8,128)(2,1)} %param.17) | copy-start | bytes 6291460
  (19 other events, 502.0 us)
Sparse Core Ops, SparseCore 0:
  11.5 157.5 all-gather.11
  172.5 75.6 all-gather.13
  251.6 143.1 all-gather.15
  398.1 142.7 all-gather.17
  543.6 142.7 all-gather.19
  923.5 50.8 reduce-scatter.32
  977.9 112.1 reduce-scatter.36
  1093.4 112.1 reduce-scatter.34
  1209.0 112.1 reduce-scatter.38
  1324.4 120.6 reduce-scatter.30
  1447.6 27.1 reduce-scatter.22
  1476.9 54.8 reduce-scatter.26
  1534.1 56.7 reduce-scatter.24
  1593.0 55.9 reduce-scatter.28
  1651.2 60.1 reduce-scatter.20

commit v2 on v1

--- a/solution.py
+++ b/solution.py
@@ -12,6 +12,8 @@
 VMEM_LIMIT = 60 * 1024 * 1024
 F32 = jnp.float32
 BF16 = jnp.bfloat16
+MESH = pl.DeviceIdType.MESH
+SPLITS = (True, True, True, True, True)
 
 
 def params(**kw):
@@ -37,6 +39,227 @@
 def whole(shape):
     zeros = (0,) * len(shape)
     return pl.BlockSpec(shape, lambda *_: zeros)
+
+
+GATHER_SLOTS = 9
+
+
+def gather_kernel(n, ways, *refs):
+    ins, outs, held = refs[:n], refs[n : 2 * n], refs[2 * n : 3 * n]
+    in_sem, own_sem, send_sem, recv_sem = refs[3 * n :]
+    way = lax.axis_index("tensor")
+    chip = lax.axis_index("chip")
+    core = lax.axis_index("core")
+    chip_x = chip + 1 - 2 * lax.rem(chip, 2)
+    chip_y = lax.rem(chip + 2, 4)
+    chip_d = 3 - chip
+    here = chip * 2 + core
+    over_x, over_y, over_d = chip_x * 2 + core, chip_y * 2 + core, chip_d * 2 + core
+    x_id, y_id, core_id = {"chip": chip_x}, {"chip": chip_y}, {"core": 1 - core}
+
+    barrier = pltpu.get_barrier_semaphore()
+    for target in (x_id, y_id, core_id):
+        pl.semaphore_signal(barrier, inc=1, device_id=target, device_id_type=MESH)
+
+    @pl.when(way > 0)
+    def _():
+        pl.semaphore_signal(barrier, inc=1, device_id={"tensor": way - 1}, device_id_type=MESH)
+
+    @pl.when(way < ways - 1)
+    def _():
+        pl.semaphore_signal(barrier, inc=1, device_id={"tensor": way + 1}, device_id_type=MESH)
+
+    ends = jnp.where(way == 0, 1, 0) + jnp.where(way == ways - 1, 1, 0)
+    pl.semaphore_wait(barrier, 5 - ends)
+
+    def piece(k, shard, owner, part=None):
+        tall = ins[k].shape[0] // 8
+        start, size = owner * tall, tall
+        if part is not None:
+            size = tall // 2
+            start = start + part * size
+        return outs[k].at[shard, pl.ds(pl.multiple_of(start, 8), size)]
+
+    def copy(src, dst, k, kind, slot, target):
+        return pltpu.make_async_remote_copy(
+            src_ref=src,
+            dst_ref=dst,
+            send_sem=send_sem.at[k, kind, slot],
+            recv_sem=recv_sem.at[k, kind, slot],
+            device_id=target,
+            device_id_type=MESH,
+        )
+
+    def along(block, k, kind, slot, target):
+        return copy(block, block, k, kind, slot, target)
+
+    def first(k, up):
+        tall = ins[k].shape[0] // 8
+        src = ins[k].at[pl.ds(pl.multiple_of(here * tall, 8), tall)]
+        return copy(src, piece(k, way, here), k, 0 if up else 1, 0, {"tensor": way + (1 if up else -1)})
+
+    def guard(hop, up):
+        arrives = way >= hop if up else way + hop < ways
+        goes_on = jnp.logical_and(arrives, way < ways - 1) if up else jnp.logical_and(arrives, way > 0)
+        return arrives, goes_on
+
+    def shard_of(hop, up):
+        return way - hop if up else way + hop
+
+    def z_copy(k, hop, up):
+        kind = 2 * (hop - 1) + (0 if up else 1)
+        return along(piece(k, shard_of(hop, up), here), k, kind, 0, {"tensor": way + (1 if up else -1)})
+
+    def z_next(k, hop, up):
+        kind = 2 * hop + (0 if up else 1)
+        return along(piece(k, shard_of(hop, up), here), k, kind, 0, {"tensor": way + (1 if up else -1)})
+
+    def plane(k, hop, up):
+        kind = 2 * (hop - 1) + (0 if up else 1)
+        s = shard_of(hop, up)
+        make = lambda block, slot, target: (lambda: along(block, k, kind, slot, target))
+        return dict(
+            x=make(piece(k, s, here), 1, x_id),
+            y=make(piece(k, s, here), 2, y_id),
+            dy=make(piece(k, s, over_x, 0), 3, y_id),
+            dx=make(piece(k, s, over_y, 1), 4, x_id),
+            c0=make(piece(k, s, here), 5, core_id),
+            c1=make(piece(k, s, over_x), 6, core_id),
+            c2=make(piece(k, s, over_y), 7, core_id),
+            c3=make(piece(k, s, over_d), 8, core_id),
+        )
+
+    def both(fn):
+        for up in (True, False):
+            fn(up)
+
+    def start_own(k):
+        @pl.when(way < ways - 1)
+        def _():
+            first(k, True).start()
+
+        @pl.when(way > 0)
+        def _():
+            first(k, False).start()
+
+    def stage1(k, hop):
+        def run(up):
+            arrives, goes_on = guard(hop, up)
+
+            @pl.when(arrives)
+            def _():
+                z_copy(k, hop, up).wait_recv()
+                to = plane(k, hop, up)
+                to["x"]().start()
+                to["y"]().start()
+                to["c0"]().start()
+
+            if hop < ways - 1:
+
+                @pl.when(goes_on)
+                def _():
+                    z_next(k, hop, up).start()
+
+        both(run)
+
+    def stage2(k, hop):
+        def run(up):
+            @pl.when(guard(hop, up)[0])
+            def _():
+                to = plane(k, hop, up)
+                to["x"]().wait_recv()
+                to["dy"]().start()
+                to["c1"]().start()
+                to["y"]().wait_recv()
+                to["dx"]().start()
+                to["c2"]().start()
+
+        both(run)
+
+    def stage3(k, hop):
+        def run(up):
+            @pl.when(guard(hop, up)[0])
+            def _():
+                to = plane(k, hop, up)
+                to["dy"]().wait_recv()
+                to["dx"]().wait_recv()
+                to["c3"]().start()
+
+        both(run)
+
+    def finish(k, hop):
+        def run(up):
+            arrives, goes_on = guard(hop, up)
+
+            @pl.when(arrives)
+            def _():
+                to = plane(k, hop, up)
+                for name in ("c0", "c1", "c2", "c3"):
+                    to[name]().wait_recv()
+                for name in to:
+                    to[name]().wait_send()
+
+            if hop < ways - 1:
+
+                @pl.when(goes_on)
+                def _():
+                    z_next(k, hop, up).wait_send()
+
+        both(run)
+
+    steps = [(k, hop) for k in range(n) for hop in range(1, ways)]
+    start_own(0)
+    load = lambda k: pltpu.make_async_copy(ins[k], held[k], in_sem.at[k])
+    own = lambda k: pltpu.make_async_copy(held[k], outs[k].at[way], own_sem.at[k])
+    for k in range(n):
+        load(k).start()
+    for i in range(len(steps) + 2):
+        if i < len(steps):
+            k, hop = steps[i]
+            if hop == 1:
+                load(k).wait()
+                own(k).start()
+                if k + 1 < n:
+                    start_own(k + 1)
+            stage1(k, hop)
+        if 0 <= i - 1 < len(steps):
+            stage2(*steps[i - 1])
+        if 0 <= i - 2 < len(steps):
+            stage3(*steps[i - 2])
+    for k in range(n):
+        own(k).wait()
+
+        @pl.when(way < ways - 1)
+        def _():
+            first(k, True).wait_send()
+
+        @pl.when(way > 0)
+        def _():
+            first(k, False).wait_send()
+
+        for hop in range(1, ways):
+            finish(k, hop)
+
+
+def gather_weights(shards, ways):
+    n = len(shards)
+    any_space = pl.BlockSpec(memory_space=pl.ANY)
+    kinds = 2 * (ways - 1)
+    return pl.pallas_call(
+        functools.partial(gather_kernel, n, ways),
+        in_specs=[any_space] * n,
+        out_specs=[any_space] * n,
+        out_shape=[jax.ShapeDtypeStruct((ways,) + w.shape, w.dtype) for w in shards],
+        scratch_shapes=[pltpu.VMEM(w.shape, w.dtype) for w in shards]
+        + [
+            pltpu.SemaphoreType.DMA((n,)),
+            pltpu.SemaphoreType.DMA((n,)),
+            pltpu.SemaphoreType.DMA((n, kinds, GATHER_SLOTS)),
+            pltpu.SemaphoreType.DMA((n, kinds, GATHER_SLOTS)),
+        ],
+        compiler_params=params(collective_id=1, has_side_effects=True),
+        name="gather_weights",
+    )(*shards)
 
 
 def proj_kernel(x_ref, w_ref, o_ref):
@@ -542,68 +765,78 @@
     )(g_branch, w_out)
 
 
-def by_rows_kernel(chips, n, *refs):
-    left_ref, right_refs, o_ref = refs[0], refs[1 : 1 + n], refs[-1]
-    add_ref = refs[1 + n] if len(refs) == n + 3 else None
-    each = o_ref.shape[2]
+def columns(ref, at_ref, chips, each):
+    picks = [ref[:, pl.ds(pl.multiple_of(at_ref[j] * each, each), each)] for j in range(chips)]
+    return jnp.concatenate(picks, axis=1)
+
+
+def put(outs, adds, j, at, wide, value):
+    if len(outs) == 1:
+        if adds:
+            value = value + adds[0][j, 0, :, at : at + wide].astype(F32)
+        outs[0][j, 0, :, at : at + wide] = value.astype(BF16)
+        return
+    half = value.shape[0] // 2
+    far_y, far_x = j // 2, j % 2
+    spots = ((0 if far_y else 1, far_x), (2 if far_x else 3, far_y))
+    for part, (which, row) in enumerate(spots):
+        got = value[part * half : (part + 1) * half]
+        if adds:
+            got = got + adds[which][row, 0, :, at : at + wide].astype(F32)
+        outs[which][row, 0, :, at : at + wide] = got.astype(BF16)
+
+
+def by_rows_kernel(chips, n, n_out, each, at_ref, left_ref, *refs):
+    rights, adds, outs = refs[:n], refs[n : len(refs) - n_out], refs[len(refs) - n_out :]
+    left = columns(left_ref, at_ref, chips, each)
     at = 0
-    for right_ref in right_refs:
+    for right_ref in rights:
         wide = right_ref.shape[2]
-        acc = tn(left_ref[...], right_ref[0])
+        acc = tn(left, right_ref[0])
         for j in range(chips):
-            got = acc[j * each : (j + 1) * each]
-            if add_ref is not None:
-                got = got + add_ref[j, 0, :, at : at + wide].astype(F32)
-            o_ref[j, 0, :, at : at + wide] = got.astype(BF16)
+            put(outs, adds, j, at, wide, acc[j * each : (j + 1) * each])
         at += wide
 
 
-def by_rows(left, rights, add, chips):
-    rows, tall = left.shape
-    ways = rights[0].shape[0]
-    each = tall // chips
+def by_cols_kernel(chips, n_out, each, at_ref, right_ref, left_ref, *refs):
+    adds, outs = refs[: len(refs) - n_out], refs[len(refs) - n_out :]
+    acc = tn(left_ref[0], columns(right_ref, at_ref, chips, each))
+    for j in range(chips):
+        put(outs, adds, j, 0, each, acc[:, j * each : (j + 1) * each])
+
+
+def weight_grad(kernel, whole_side, parted, tall, wide, at, adds, chips, split, name):
+    ways, rows, _ = parted[0].shape
+    if split:
+        shapes = [(2, ways, tall // 2, wide)] * 4
+    else:
+        shapes = [(chips, ways, tall, wide)]
+    blocks = [pl.BlockSpec((c, 1, h, w), lambda t: (0, t, 0, 0)) for c, _, h, w in shapes]
+    adds = list(adds or [])
+    return pl.pallas_call(
+        kernel,
+        grid=(ways,),
+        in_specs=[pl.BlockSpec(memory_space=pltpu.SMEM), whole(whole_side.shape)]
+        + [pl.BlockSpec((1, rows, p.shape[2]), lambda t: (t, 0, 0)) for p in parted]
+        + blocks[: len(adds)],
+        out_specs=blocks,
+        out_shape=[jax.ShapeDtypeStruct(s, BF16) for s in shapes],
+        compiler_params=params(),
+        name=name,
+    )(at, whole_side, *parted, *adds)
+
+
+def by_rows(left, rights, at, adds, chips, split):
+    each = left.shape[1] // (2 * chips)
+    kernel = functools.partial(by_rows_kernel, chips, len(rights), 4 if split else 1, each)
     wide = sum(r.shape[2] for r in rights)
-    block = pl.BlockSpec((chips, 1, each, wide), lambda t: (0, t, 0, 0))
-    return pl.pallas_call(
-        functools.partial(by_rows_kernel, chips, len(rights)),
-        grid=(ways,),
-        in_specs=[whole((rows, tall))]
-        + [pl.BlockSpec((1, rows, r.shape[2]), lambda t: (t, 0, 0)) for r in rights]
-        + ([block] if add is not None else []),
-        out_specs=block,
-        out_shape=jax.ShapeDtypeStruct((chips, ways, each, wide), BF16),
-        compiler_params=params(),
-        name="by_rows",
-    )(left, *rights, *([add] if add is not None else []))
-
-
-def by_cols_kernel(chips, *refs):
-    left_ref, right_ref, o_ref = refs[0], refs[1], refs[-1]
-    add_ref = refs[2] if len(refs) == 4 else None
-    each = o_ref.shape[3]
-    acc = tn(left_ref[0], right_ref[...])
-    for j in range(chips):
-        got = acc[:, j * each : (j + 1) * each]
-        if add_ref is not None:
-            got = got + add_ref[j, 0].astype(F32)
-        o_ref[j, 0] = got.astype(BF16)
-
-
-def by_cols(left, right, add, chips):
-    ways, rows, tall = left.shape
-    wide = right.shape[1]
-    each = wide // chips
-    block = pl.BlockSpec((chips, 1, tall, each), lambda t: (0, t, 0, 0))
-    return pl.pallas_call(
-        functools.partial(by_cols_kernel, chips),
-        grid=(ways,),
-        in_specs=[pl.BlockSpec((1, rows, tall), lambda t: (t, 0, 0)), whole((rows, wide))]
-        + ([block] if add is not None else []),
-        out_specs=block,
-        out_shape=jax.ShapeDtypeStruct((chips, ways, tall, each), BF16),
-        compiler_params=params(),
-        name="by_cols",
-    )(left, right, *([add] if add is not None else []))
+    return weight_grad(kernel, left, rights, each, wide, at, adds, chips, split, "by_rows")
+
+
+def by_cols(left, right, at, adds, chips, split):
+    each = right.shape[1] // (2 * chips)
+    kernel = functools.partial(by_cols_kernel, chips, 4 if split else 1, each)
+    return weight_grad(kernel, right, [left], left.shape[2], each, at, adds, chips, split, "by_cols")
 
 
 def norm_pullback(upstream_gradient, unit_rows, inverse_rms, gain_vector):
@@ -614,6 +847,23 @@
 
 
 SWAP = ((0, 1), (1, 0))
+OVER_X = ((0, 1), (1, 0), (2, 3), (3, 2))
+OVER_Y = ((0, 2), (2, 0), (1, 3), (3, 1))
+
+
+def behind(value, *done):
+    return lax.optimization_barrier((value,) + done)[0]
+
+
+def from_all(value, axis):
+    n = lax.axis_size(axis)
+    if n > 4:
+        return lax.all_gather(value, axis, axis=0)
+    me = lax.axis_index(axis)
+    seen = [value]
+    for k in range(1, n):
+        seen.append(lax.ppermute(value, axis, [((i + k) % n, i) for i in range(n)]))
+    return lax.dynamic_slice_in_dim(jnp.stack(seen + seen), (n - me) % n, n, 0)
 
 
 def local(
@@ -640,35 +890,36 @@
     groups = 2 * chips
     way = lax.axis_index("tensor")
     core = lax.axis_index("core")
-    group = lax.axis_index("chip") * 2 + core
+    chip = lax.axis_index("chip")
+    group = chip * 2 + core
     every = ("tensor", "chip", "core")
-
-    def mine(weights):
+    square = chips == 4 and ways == 4
+
+    def gather(weights):
         tall = weights.shape[0] // groups
-        return lax.dynamic_slice_in_dim(weights, group * tall, tall, 0)
-
-    def gather(piece):
-        return lax.all_gather(piece, every, axis=0, tiled=True)
-
-    w3 = gather(jnp.concatenate([mine(w_in), mine(w_forget), mine(w_gate)], axis=1))
-    w3 = w3.reshape(ways, width, 3 * chans)
-    w_out_all = gather(mine(w_out)).reshape(ways, chans, width)
-    w_glu_all = gather(mine(w_glu)).reshape(ways, width, units)
-    w_up_all = gather(mine(w_up)).reshape(ways, width, units)
-    w_down_all = gather(mine(w_down)).reshape(ways, units, width)
-
-    lower = lax.all_gather(lower_bound, "tensor", axis=0).reshape(ways, 1, chans)
-    gain = lax.all_gather(gate_gain, "tensor", axis=0).reshape(ways, 1, chans)
+        piece = lax.dynamic_slice_in_dim(weights, group * tall, tall, 0)
+        piece = lax.all_gather(piece, every, axis=0, tiled=True)
+        return piece.reshape((ways,) + weights.shape)
+
+    vectors = from_all(jnp.stack([lower_bound, gate_gain]), "tensor")
+    lower, gain = vectors[:, 0:1], vectors[:, 1:2]
     l0, l1 = lengths[0, 0], lengths[0, 1]
     starts = jnp.stack([jnp.zeros_like(l0), l0, l0 + l1]) - way * rows
-
     x = tokens.astype(F32)
     inverse1 = lax.rsqrt(jnp.mean(x * x, axis=1, keepdims=True) + EPS)
     normed = (x * inverse1 * first_norm_gain).astype(BF16)
 
+    shards = [jnp.concatenate([w_in, w_forget, w_gate], axis=1), w_out, w_glu, w_up]
+    if square:
+        w3, w_out_all, w_glu_all, w_up_all = gather_weights(shards, ways)
+        w_down_all = gather(behind(w_down, w_out_all))
+    else:
+        w3, w_out_all, w_glu_all, w_up_all = [gather(w) for w in shards]
+        w_down_all = gather(w_down)
+
     p = project(normed, w3, chans)
     totals = forward_total(p, lower, starts)
-    all_totals = lax.all_gather(totals, "tensor", axis=0)
+    all_totals = from_all(totals, "tensor")
     enter = jnp.zeros((ways, 1, chans), F32)
     seen = jnp.zeros((ways, 1, chans), F32)
     for k in range(ways - 1):
@@ -679,47 +930,70 @@
     resid, middle = branch(mixed, w_out_all, tokens, feedforward_gain.reshape(1, width))
     hidden, act, slope = feed_up(middle, w_up_all, w_glu_all)
 
-    def halves(array):
-        cut = array.reshape(rows, chips, 2, width // groups)
-        pick = lambda c: lax.dynamic_index_in_dim(cut, c, 2, False).reshape(rows, width // 2)
-        return pick(1 - core), pick(core)
-
-    def swap(array):
-        return lax.ppermute(array, "core", SWAP)
-
-    def scatter(array):
-        array = lax.psum_scatter(array, "chip", scatter_dimension=0, tiled=True)
-        array = array.reshape(array.shape[1:])
-        array = lax.psum_scatter(array, "tensor", scatter_dimension=0, tiled=True)
-        return array.reshape(array.shape[1:]).astype(F32)
-
-    def grad_rows(left, rights):
-        theirs, ours = left
-        return scatter(by_rows(ours, rights, swap(by_rows(theirs, rights, None, chips)), chips))
-
-    def grad_cols(left, right):
-        theirs, ours = right
-        return scatter(by_cols(left, ours, swap(by_cols(left, theirs, None, chips)), chips))
-
-    grad_w_down = grad_cols(hidden, halves(cotangent))
-    output = feed_down(hidden, w_down_all, resid)
-
-    g_up, g_glu = hidden_grad(cotangent, w_down_all, act, slope)
-    middle_halves = halves(middle)
-    grad_w_up = grad_rows(middle_halves, [g_up])
-    grad_w_glu = grad_rows(middle_halves, [g_glu])
-    g_middle = back([g_up, g_glu], [w_up_all, w_glu_all], [0, 0], units)
+    places = jnp.arange(chips, dtype=jnp.int32)
+
+    def blocks_of(c, split):
+        return (jnp.bitwise_xor(places, chip) if split else places) * 2 + c
+
+    def swap(arrays):
+        return [lax.ppermute(a, "core", SWAP) for a in arrays]
+
+    def add(a, b):
+        return a.astype(F32) + b.astype(F32)
+
+    def scatter(arrays):
+        if len(arrays) == 1:
+            part = lax.psum_scatter(arrays[0], "chip", scatter_dimension=0, tiled=True)
+            part = part.reshape(part.shape[1:])
+        else:
+            y_send, y_keep, x_send, x_keep = arrays
+            from_y = lax.ppermute(y_send, "chip", OVER_Y)
+            from_x = lax.ppermute(x_send, "chip", OVER_X)
+            upper = add(y_keep[1], from_y[1]).astype(BF16)
+            lower_half = add(x_keep[1], from_x[1]).astype(BF16)
+            upper = lax.ppermute(upper, "chip", OVER_X)
+            lower_half = lax.ppermute(lower_half, "chip", OVER_Y)
+            upper = add(add(y_keep[0], from_y[0]), upper).astype(BF16)
+            lower_half = add(add(x_keep[0], from_x[0]), lower_half).astype(BF16)
+            part = jnp.concatenate([upper, lower_half], axis=1)
+        part = lax.psum_scatter(part, "tensor", scatter_dimension=0, tiled=True)
+        return part.reshape(part.shape[1:]).astype(F32)
+
+    split_down, split_up, split_glu, split_out, split_three = [square and s for s in SPLITS]
+    gy = cotangent
+
+    theirs_down = by_cols(hidden, gy, blocks_of(1 - core, split_down), None, chips, split_down)
+    swap_down = swap(theirs_down)
+    g_up, g_glu = hidden_grad(behind(gy, *theirs_down), w_down_all, act, slope)
+    ours_down = by_cols(behind(hidden, g_up), gy, blocks_of(core, split_down), swap_down, chips, split_down)
+    grad_w_down = scatter(ours_down)
+
+    middle_now = behind(middle, *ours_down)
+    theirs_up = by_rows(middle_now, [g_up], blocks_of(1 - core, split_up), None, chips, split_up)
+    swap_up = swap(theirs_up)
+    theirs_glu = by_rows(behind(middle, *theirs_up), [g_glu], blocks_of(1 - core, split_glu), None, chips, split_glu)
+    swap_glu = swap(theirs_glu)
+    ours_up = by_rows(behind(middle, *theirs_glu), [g_up], blocks_of(core, split_up), swap_up, chips, split_up)
+    grad_w_up = scatter(ours_up)
+    ours_glu = by_rows(behind(middle, *ours_up), [g_glu], blocks_of(core, split_glu), swap_glu, chips, split_glu)
+    grad_w_glu = scatter(ours_glu)
+    g_middle = back([behind(g_up, *ours_glu), g_glu], [w_up_all, w_glu_all], [0, 0], units)
 
     inverse2 = lax.rsqrt(jnp.mean(resid * resid, axis=1, keepdims=True) + EPS)
     unit2 = resid * inverse2
     mlp_gain_part = jnp.sum(g_middle * unit2, axis=0)
     g_resid = cotangent.astype(F32) + norm_pullback(g_middle, unit2, inverse2, feedforward_gain)
     g_branch = g_resid.astype(BF16)
-    grad_w_out = grad_cols(mixed, halves(g_branch))
-    g_mixed = mixed_grad(g_branch, w_out_all)
-
-    g_state, g_gate, gain_part, back_totals = backward_total(p, state, g_mixed, lower, gain, starts)
-    all_back = lax.all_gather(back_totals, "tensor", axis=0)
+    theirs_out = by_cols(mixed, g_branch, blocks_of(1 - core, split_out), None, chips, split_out)
+    swap_out = swap(theirs_out)
+    g_mixed = mixed_grad(behind(g_branch, *theirs_out), w_out_all)
+    ours_out = by_cols(behind(mixed, g_mixed), g_branch, blocks_of(core, split_out), swap_out, chips, split_out)
+    grad_w_out = scatter(ours_out)
+
+    g_state, g_gate, gain_part, back_totals = backward_total(
+        p, state, behind(g_mixed, *ours_out), lower, gain, starts
+    )
+    all_back = from_all(back_totals, "tensor")
     after = jnp.zeros((ways, 1, chans), F32)
     seen = jnp.zeros((ways, 1, chans), F32)
     for k in range(ways - 1, 0, -1):
@@ -727,9 +1001,13 @@
         after = jnp.where(way == k - 1, seen, after)
     g_in, g_forget, lower_part = backward_scan(p, state, g_state, lower, starts, enter, after)
 
-    normed_halves = halves(normed)
-    grad_three = grad_rows(normed_halves, [g_in, g_forget, g_gate])
-    g_normed = back([g_in, g_forget, g_gate], [w3, w3, w3], [0, 1, 2], chans)
+    g_three = [g_in, g_forget, g_gate]
+    theirs_three = by_rows(normed, g_three, blocks_of(1 - core, split_three), None, chips, split_three)
+    swap_three = swap(theirs_three)
+    output = feed_down(behind(hidden, *theirs_three), w_down_all, resid)
+    ours_three = by_rows(behind(normed, output), g_three, blocks_of(core, split_three), swap_three, chips, split_three)
+    grad_three = scatter(ours_three)
+    g_normed = back([behind(g_in, *ours_three), g_forget, g_gate], [w3, w3, w3], [0, 1, 2], chans)
 
     unit1 = x * inverse1
     norm_gain_part = jnp.sum(g_normed * unit1, axis=0)

time: 1730 us -> 1370 us (0.79)
  waiting for transfers between devices: 819 us -> 303 us
  Pallas kernels: 549 us -> 831 us
  local copies, waits for them, and re-layouts: 175 us -> 14.6 us
  blocking collectives: 96.6 us -> 39.7 us
  other arithmetic: 62.5 us -> 116 us
  starting transfers between devices: 1.38 us -> 38.8 us
    all_gather x5 -> x1, waiting for transfers between devices: 467 us -> 0.01 us  [gather(): piece = lax.all_gather(piece, every, axis=0, tiled=True)]
    pallas_call x10 -> x11, Pallas kernels: 167 us -> 449 us  [the longest x1 277 us: gather_weights(): pl.pallas_call(functools.partial(gather_kernel, n, ways), in_specs=[any_s...]
    ppermute x5 -> x49, waiting for transfers between devices: 54.8 us -> 303 us  [the longest x5 155 us: scatter(): upper = lax.ppermute(upper, 'chip', OVER_X)]
    unnamed x20 -> x6, waiting for transfers between devices: 178 us -> 0.1 us
    dynamic_slice x10 -> x1, local copies, waits for them, and re-layouts: 122 us -> 2.05 us  [gather(): piece = lax.dynamic_slice_in_dim(weights, group * tall, tall, 0)]
    reduce_scatter x5, waiting for transfers between devices: 119 us -> 0.01 us  [scatter(): part = lax.psum_scatter(part, 'tensor', scatter_dimension=0, tiled=True)]
    all_gather x4 -> x0, blocking collectives: 54.6 us -> none  [the longest x1 14.5 us: local(): all_totals = lax.all_gather(totals, 'tensor', axis=0)]
    convert_element_type x5 -> x25, other arithmetic: 10.2 us -> 48.5 us  [the longest x5 10.9 us: scatter(): upper = add(y_keep[1], from_y[1]).astype(BF16)]
  transfers between devices with their start and end apart: 20 -> 55, of which waited for: 13 -> 13; matrix products, arithmetic and copies ran while one was open for 10% -> 8% of each run, Pallas kernels for 25% -> 38%
where the time goes in v2:
time: 1370 us; the launch traced here: 1360 us
  Pallas kernels  831 us (61%)
  waiting for transfers between devices  303 us (22%)
  other arithmetic  116 us (8%)
  blocking collectives  39.7 us (3%)
  starting transfers between devices  38.8 us (3%)
  between operations  18.6 us (1%)
  local copies, waits for them, and re-layouts  14.6 us (1%)
    pallas_call x1, Pallas kernels, gather_weights(): pl.pallas_call(functools.partial(gather_kernel, n, ways), in_specs=[any_s...  277 us
    pallas_call x10, Pallas kernels, weight_grad(): pl.pallas_call(kernel, grid=(ways,), in_specs=[pl.BlockSpec(memory_space=...  173 us
    ppermute x5, waiting for transfers between devices, scatter(): upper = lax.ppermute(upper, 'chip', OVER_X)  155 us
    ppermute x5, waiting for transfers between devices, scatter(): from_y = lax.ppermute(y_send, 'chip', OVER_Y)  101 us
    pallas_call x2, Pallas kernels, back(): pl.pallas_call(functools.partial(back_kernel, len(grads)), grid=(width //...  99.7 us
    pallas_call x1, Pallas kernels, feed_up(): pl.pallas_call(up_kernel, grid=(ways, rows // part), in_specs=[pl.BlockSp...  60.8 us
    pallas_call x1, Pallas kernels, hidden_grad(): pl.pallas_call(hidden_grad_kernel, grid=(ways, rows // part), in_specs=[p...  42.1 us
    psum x1, blocking collectives, local(): small = lax.psum(small, every)  39.7 us
  transfers between devices with their start and end apart: 55, of which 13 were waited for; matrix products, arithmetic and copies ran while one was open for 8% of the time, Pallas kernels for 38%

profile of v2, /device:TPU:0, one launch (start us, length us, event | category | flops | bytes accessed | tf_op | source)
XLA Modules:
  0.0 1361.6 jit_solution(7637062700562694996)
XLA Ops:
  13.6 276.7 %gather_weights.1 = (bf16[4,2048,1536]{2,1,0:T(8,128)(2,1)}, bf16[4,512,2048]{2,1,0:T(8,128)(2,1)}, bf16[4,2048,1408]{2,1,0:T(8,128)(2,1)}, bf16[4,2048,1408]{2,1,0:T(8,128)(2,1)}) custom-call(bf16[2048,1536]{1,0:T(8,128)(2,1)} %pad_maximum_fusion.refs_0_, bf16[512,2048]{1,0:T(8,128)(2,1)} %refs_1_.1, bf16[2048,1408]{1,0:T(8,128)(2,1)} %refs_2_.1, ...), custom_call_target="tpu_custom_call" | custom-call | tf_op jit(solution)/shard_map/gather_weights/pallas_call | solution.py:248
  309.4 32.7 %project.1.p_ref.pf_ref.pg_ref.pi_ref = f32[4,1024,1536]{2,1,0:T(8,128)} custom-call(bf16[1024,2048]{1,0:T(8,128)(2,1)} %fusion.4.x_ref.left_ref, bf16[4,2048,1536]{2,1,0:T(8,128)(2,1)} %get-tuple-element.89.w_ref.refs_3_.refs_4_.refs_5_), custom_call_target="tpu_custom_call" | custom-call | tf_op jit(solution)/shard_map/project/pallas_call | solution.py:272
  366.1 22.6 %forward_scan.1 = (f32[4,1024,512]{2,1,0:T(8,128)}, bf16[4,1024,512]{2,1,0:T(8,128)(2,1)}, f32[4,8,512]{2,1,0:T(8,128)}) custom-call(s32[3]{0:T(128)} %add_subtract_fusion.starts_ref, f32[4,1024,1536]{2,1,0:T(8,128)} %project.1.p_ref.pf_ref.pg_ref.pi_ref, f32[4,1,512]{2,1,0:T(1,128)} %get-tuple-element.177.lower_ref, ...), custom_call_target="tpu_custom_call" | custom-call | tf_op jit(solution)/shard_map/forward_scan/pallas_call | solution.py:393
  404.5 60.8 %feed_up.1 = (bf16[4,1024,1408]{2,1,0:T(8,128)(2,1)}, bf16[4,1024,1408]{2,1,0:T(8,128)(2,1)}, bf16[4,1024,1408]{2,1,0:T(8,128)(2,1)}) custom-call(bf16[1024,2048]{1,0:T(8,128)(2,1)} %get-tuple-element.128.x_ref.left_ref, bf16[4,2048,1408]{2,1,0:T(8,128)(2,1)} %get-tuple-element.93.up_ref.refs_2_, bf16[4,2048,1408]{2,1,0:T(8,128)(2,1)} %get-tuple-element.94.glu_ref.refs_3_), custom_call_target="tpu_custom_call" | custom-call | tf_op jit(solution)/shard_map/feed_up/pallas_call | solution.py:654
  484.5 42.1 %hidden_grad.1 = (bf16[4,1024,1408]{2,1,0:T(8,128)(2,1)}, bf16[4,1024,1408]{2,1,0:T(8,128)(2,1)}) custom-call(bf16[1024,2048]{1,0:T(8,128)(2,1)} %right_ref.3, bf16[4,1408,2048]{2,1,0:T(8,128)(2,1)} %bitcast.176, bf16[4,1024,1408]{2,1,0:T(8,128)(2,1)} %get-tuple-element.104.act_ref, bf16[4,1024,1408]{2,1,0:T(8,128)(2,1)} %get-tuple-element.105.slope_ref), custom_call_target="tpu_custom_call" | custom-call | tf_op jit(solution)/shard_map/hidden_grad/pallas_call | solution.py:702
  528.2 19.0 %by_cols.5 = (bf16[2,4,704,256]{3,2,1,0:T(8,128)(2,1)}, bf16[2,4,704,256]{3,2,1,0:T(8,128)(2,1)}, bf16[2,4,704,256]{3,2,1,0:T(8,128)(2,1)}, bf16[2,4,704,256]{3,2,1,0:T(8,128)(2,1)}) custom-call(s32[4]{0:T(128)} %fusion.37.at_ref, bf16[1024,2048]{1,0:T(8,128)(2,1)} %right_ref.3, bf16[4,1024,1408]{2,1,0:T(8,128)(2,1)} %get-tuple-element.154.left_ref.h_ref, ...), custom_call_target="tpu_custom_call" | custom-call | tf_op jit(solution)/shard_map/by_cols/pallas_call | solution.py:816
  566.9 18.7 %by_rows.7 = (bf16[2,4,128,1408]{3,2,1,0:T(8,128)(2,1)}, bf16[2,4,128,1408]{3,2,1,0:T(8,128)(2,1)}, bf16[2,4,128,1408]{3,2,1,0:T(8,128)(2,1)}, bf16[2,4,128,1408]{3,2,1,0:T(8,128)(2,1)}) custom-call(s32[4]{0:T(128)} %fusion.38.at_ref, bf16[1024,2048]{1,0:T(8,128)(2,1)} %get-tuple-element.128.x_ref.left_ref, ...), custom_call_target="tpu_custom_call" | custom-call | tf_op jit(solution)/shard_map/by_rows/pallas_call | solution.py:816
  591.7 20.1 %by_rows.8 = (bf16[2,4,128,1408]{3,2,1,0:T(8,128)(2,1)}, bf16[2,4,128,1408]{3,2,1,0:T(8,128)(2,1)}, bf16[2,4,128,1408]{3,2,1,0:T(8,128)(2,1)}, bf16[2,4,128,1408]{3,2,1,0:T(8,128)(2,1)}) custom-call(s32[4]{0:T(128)} %fusion.37.at_ref, bf16[1024,2048]{1,0:T(8,128)(2,1)} %get-tuple-element.128.x_ref.left_ref, ...), custom_call_target="tpu_custom_call" | custom-call | tf_op jit(solution)/shard_map/by_rows/pallas_call | solution.py:816
  613.5 19.8 %by_rows.9 = (bf16[2,4,128,1408]{3,2,1,0:T(8,128)(2,1)}, bf16[2,4,128,1408]{3,2,1,0:T(8,128)(2,1)}, bf16[2,4,128,1408]{3,2,1,0:T(8,128)(2,1)}, bf16[2,4,128,1408]{3,2,1,0:T(8,128)(2,1)}) custom-call(s32[4]{0:T(128)} %fusion.37.at_ref, bf16[1024,2048]{1,0:T(8,128)(2,1)} %get-tuple-element.128.x_ref.left_ref, ...), custom_call_target="tpu_custom_call" | custom-call | tf_op jit(solution)/shard_map/by_rows/pallas_call | solution.py:816
  633.2 63.2 %back.2 = f32[1024,2048]{1,0:T(8,128)} custom-call(bf16[4,1024,1408]{2,1,0:T(8,128)(2,1)} %get-tuple-element.133.refs_0_, bf16[4,1024,1408]{2,1,0:T(8,128)(2,1)} %get-tuple-element.118.refs_0_.refs_1_, bf16[4,2048,1408]{2,1,0:T(8,128)(2,1)} %get-tuple-element.93.up_ref.refs_2_, bf16[4,2048,1408]{2,1,0:T(8,128)(2,1)} %get-tuple-element.94.glu_ref.refs_3_), custom_call_target="tpu_custom_call" | custom-call | tf_op jit(solution)/shard_map/back/pallas_call | solution.py:738
  755.5 19.1 %collective-permute-done.33 = bf16[2,4,256,256]{3,2,1,0:T(8,128)(2,1)S(1)} collective-permute-done((bf16[2,4,256,256]{3,2,1,0:T(8,128)(2,1)}, bf16[2,4,256,256]{3,2,1,0:T(8,128)(2,1)S(1)}, u32[]{:S(2)}, u32[]{:S(2)}) %collective-permute-start.33) | collective-permute-done | bytes 1048608 | tf_op jit(solution)/shard_map/ppermute | solution.py:950
  775.8 33.3 %collective-permute-done.35 = bf16[2,4,256,256]{3,2,1,0:T(8,128)(2,1)S(1)} collective-permute-done((bf16[2,4,256,256]{3,2,1,0:T(8,128)(2,1)}, bf16[2,4,256,256]{3,2,1,0:T(8,128)(2,1)S(1)}, u32[]{:S(2)}, u32[]{:S(2)}) %collective-permute-start.35) | collective-permute-done | bytes 1048608 | tf_op jit(solution)/shard_map/ppermute | solution.py:951
  814.1 36.6 %collective-permute-done.34 = bf16[4,256,256]{2,1,0:T(8,128)(2,1)S(1)} collective-permute-done((bf16[4,256,256]{2,1,0:T(8,128)(2,1)S(1)}, bf16[4,256,256]{2,1,0:T(8,128)(2,1)S(1)}, u32[]{:S(2)}, u32[]{:S(2)}) %collective-permute-start.34) | collective-permute-done | bytes 524320 | tf_op jit(solution)/shard_map/ppermute | solution.py:954
  863.5 22.9 %backward_total.1 = (f32[4,1024,512]{2,1,0:T(8,128)}, bf16[4,1024,512]{2,1,0:T(8,128)(2,1)}, f32[4,8,512]{2,1,0:T(8,128)}, f32[4,1,512]{2,1,0:T(1,128)}) custom-call(s32[3]{0:T(128)} %add_subtract_fusion.starts_ref, f32[4,1024,1536]{2,1,0:T(8,128)} %project.1.p_ref.pf_ref.pg_ref.pi_ref, f32[4,1024,1536]{2,1,0:T(8,128)} %project.1.p_ref.pf_ref.pg_ref.pi_ref, ...), custom_call_target="tpu_custom_call" | custom-call | tf_op jit(solution)/shard_map/backward_total/pallas_call | solution.py:481
  897.5 20.6 %collective-permute-done.37 = bf16[2,4,128,1408]{3,2,1,0:T(8,128)(2,1)} collective-permute-done((bf16[2,4,128,1408]{3,2,1,0:T(8,128)(2,1)}, bf16[2,4,128,1408]{3,2,1,0:T(8,128)(2,1)}, u32[]{:S(2)}, u32[]{:S(2)}) %collective-permute-start.37) | collective-permute-done | bytes 2883616 | tf_op jit(solution)/shard_map/ppermute | solution.py:950
  923.4 86.8 %collective-permute-done.38 = bf16[4,128,1408]{2,1,0:T(8,128)(2,1)S(1)} collective-permute-done((bf16[4,128,1408]{2,1,0:T(8,128)(2,1)S(1)}, bf16[4,128,1408]{2,1,0:T(8,128)(2,1)S(1)}, u32[]{:S(2)}, u32[]{:S(2)}) %collective-permute-start.38) | collective-permute-done | bytes 1441824 | tf_op jit(solution)/shard_map/ppermute | solution.py:954
  1017.4 23.3 %backward_scan.1 = (bf16[4,1024,512]{2,1,0:T(8,128)(2,1)}, bf16[4,1024,512]{2,1,0:T(8,128)(2,1)}, f32[4,8,512]{2,1,0:T(8,128)}) custom-call(s32[3]{0:T(128)} %add_subtract_fusion.starts_ref, f32[4,1024,1536]{2,1,0:T(8,128)} %project.1.p_ref.pf_ref.pg_ref.pi_ref, f32[4,1024,1536]{2,1,0:T(8,128)} %project.1.p_ref.pf_ref.pg_ref.pi_ref, ...), custom_call_target="tpu_custom_call" | custom-call | tf_op jit(solution)/shard_map/backward_scan/pallas_call | solution.py:575
  1040.7 19.3 %by_rows.10 = (bf16[2,4,128,1536]{3,2,1,0:T(8,128)(2,1)}, bf16[2,4,128,1536]{3,2,1,0:T(8,128)(2,1)}, bf16[2,4,128,1536]{3,2,1,0:T(8,128)(2,1)}, bf16[2,4,128,1536]{3,2,1,0:T(8,128)(2,1)}) custom-call(s32[4]{0:T(128)} %fusion.38.at_ref, bf16[1024,2048]{1,0:T(8,128)(2,1)} %fusion.4.x_ref.left_ref, bf16[4,1024,512]{2,1,0:T(8,128)(2,1)} %get-tuple-element.160.refs_0_, ...), custom_call_target="tpu_custom_call" | custom-call | tf_op jit(solution)/shard_map/by_rows/pallas_call | solution.py:816
  1070.6 34.4 %feed_down.1 = bf16[1024,2048]{1,0:T(8,128)(2,1)} custom-call(bf16[4,1024,1408]{2,1,0:T(8,128)(2,1)} %get-tuple-element.154.left_ref.h_ref, bf16[4,1408,2048]{2,1,0:T(8,128)(2,1)} %bitcast.177, f32[1024,2048]{1,0:T(8,128)} %get-tuple-element.97.resid_ref), custom_call_target="tpu_custom_call" | custom-call | tf_op jit(solution)/shard_map/feed_down/pallas_call | solution.py:676
  1105.0 20.4 %by_rows.11 = (bf16[2,4,128,1536]{3,2,1,0:T(8,128)(2,1)}, bf16[2,4,128,1536]{3,2,1,0:T(8,128)(2,1)}, bf16[2,4,128,1536]{3,2,1,0:T(8,128)(2,1)}, bf16[2,4,128,1536]{3,2,1,0:T(8,128)(2,1)}) custom-call(s32[4]{0:T(128)} %fusion.37.at_ref, bf16[1024,2048]{1,0:T(8,128)(2,1)} %fusion.4.x_ref.left_ref, bf16[4,1024,512]{2,1,0:T(8,128)(2,1)} %get-tuple-element.160.refs_0_, ...), custom_call_target="tpu_custom_call" | custom-call | tf_op jit(solution)/shard_map/by_rows/pallas_call | solution.py:816
  1134.4 61.6 %collective-permute-done.29 = bf16[2,4,128,1536]{3,2,1,0:T(8,128)(2,1)} collective-permute-done((bf16[2,4,128,1536]{3,2,1,0:T(8,128)(2,1)}, bf16[2,4,128,1536]{3,2,1,0:T(8,128)(2,1)}, u32[]{:S(2)}, u32[]{:S(2)}) %collective-permute-start.29) | collective-permute-done | bytes 3145760 | tf_op jit(solution)/shard_map/ppermute | solution.py:950
  1202.4 31.6 %collective-permute-done.30 = bf16[4,128,1536]{2,1,0:T(8,128)(2,1)S(1)} collective-permute-done((bf16[4,128,1536]{2,1,0:T(8,128)(2,1)S(1)}, bf16[4,128,1536]{2,1,0:T(8,128)(2,1)S(1)}, u32[]{:S(2)}, u32[]{:S(2)}) %collective-permute-start.30) | collective-permute-done | bytes 1572896 | tf_op jit(solution)/shard_map/ppermute | solution.py:954
  1241.2 36.4 %back.3 = f32[1024,2048]{1,0:T(8,128)} custom-call(bf16[4,1024,512]{2,1,0:T(8,128)(2,1)} %get-tuple-element.160.refs_0_, bf16[4,1024,512]{2,1,0:T(8,128)(2,1)} %get-tuple-element.148.refs_1_, bf16[4,1024,512]{2,1,0:T(8,128)(2,1)} %get-tuple-element.149.refs_2_, bf16[4,2048,1536]{2,1,0:T(8,128)(2,1)} %get-tuple-element.89.w_ref.refs_3_.refs_4_.refs_5_, ...), custom_call_target="tpu_custom_call" | custom-call | tf_op jit(solution)/shard_map/back/pallas_call | solution.py:738
  1283.7 39.7 %psum.7 = f32[5,2048]{1,0:T(8,128)S(1)} all-reduce(f32[5,2048]{1,0:T(8,128)S(1)} %stack.103), channel_id=1, replica_groups=mesh['chip'=4,'core'=2,'tensor'=4] {'tensor','chip','core'}, use_global_device_ids=true, to_apply=%region_9.10 | all-reduce | flops 10240 | bytes 81920 | tf_op jit(solution)/shard_map/psum | solution.py:1025
  (266 shorter events, 281.3 us)
Async XLA Ops:
  7.2 477.3 %all-gather.2.cloned.1.call-start = ((), (), s32[]{:S(2)}) async-start(), calls=%async_computation.5 | async-start | bytes 23789568 | tf_op jit(solution)/shard_map/all_gather | solution.py:901
  292.3 1049.7 %reduce-scatter.8.cloned.1.call-start = ((), (), s32[]{:S(2)}) async-start(), calls=%async_computation.7 | async-start | bytes 1310720 | tf_op jit(solution)/shard_map/reduce_scatter | solution.py:959
  292.4 49.7 %collective-permute-start.1 = (f32[2,512]{1,0:T(2,128)S(1)}, f32[2,512]{1,0:T(2,128)S(1)}, u32[]{:S(2)}, u32[]{:S(2)}) collective-permute-start(f32[2,512]{1,0:T(2,128)S(1)} %pad_maximum_fusion.6), channel_id=1, source_target_pairs={{2,0},{3,1},{0,2},{1,3},{6,4},{7,5},{4,6},{5,7},{10,8},{11,9},{8,1... | collective-permute-start | bytes 12296 | tf_op jit(solution)/shard_map/ppermute | solution.py:865
  292.5 49.6 %collective-permute-start = (f32[2,512]{1,0:T(2,128)S(1)}, f32[2,512]{1,0:T(2,128)S(1)}, u32[]{:S(2)}, u32[]{:S(2)}) collective-permute-start(f32[2,512]{1,0:T(2,128)S(1)} %pad_maximum_fusion.6), channel_id=1, source_target_pairs={{1,0},{2,1},{3,2},{0,3},{5,4},{6,5},{7,6},{4,7},{9,8},{10,9},{11,1... | collective-permute-start | bytes 12296 | tf_op jit(solution)/shard_map/ppermute | solution.py:865
  590.7 160.1 %collective-permute-start.45 = (bf16[2,4,704,256]{3,2,1,0:T(8,128)(2,1)}, bf16[2,4,704,256]{3,2,1,0:T(8,128)(2,1)}, u32[]{:S(2)}, u32[]{:S(2)}) collective-permute-start(bf16[2,4,704,256]{3,2,1,0:T(8,128)(2,1)} %get-tuple-element.108), channel_id=1, source_target_pairs={{0,16},{16,0},{8,24},{24,8},{1,17},{17,1},{9,25},{25,9},{2,18},{18... | collective-permute-start | bytes 8650760 | tf_op jit(solution)/shard_map/ppermute | solution.py:950
  721.1 89.3 %collective-permute-start.47 = (bf16[2,4,704,256]{3,2,1,0:T(8,128)(2,1)}, bf16[2,4,704,256]{3,2,1,0:T(8,128)(2,1)}, u32[]{:S(2)}, u32[]{:S(2)}) collective-permute-start(bf16[2,4,704,256]{3,2,1,0:T(8,128)(2,1)} %get-tuple-element.110), channel_id=1, source_target_pairs={{0,8},{8,0},{16,24},{24,16},{1,9},{9,1},{17,25},{25,17},{2,10},{10... | collective-permute-start | bytes 8650760 | tf_op jit(solution)/shard_map/ppermute | solution.py:951
  750.2 58.9 %collective-permute-start.35 = (bf16[2,4,256,256]{3,2,1,0:T(8,128)(2,1)}, bf16[2,4,256,256]{3,2,1,0:T(8,128)(2,1)S(1)}, u32[]{:S(2)}, u32[]{:S(2)}) collective-permute-start(bf16[2,4,256,256]{3,2,1,0:T(8,128)(2,1)} %get-tuple-element.142), channel_id=1, source_target_pairs={{0,8},{8,0},{16,24},{24,16},{1,9},{9,1},{17,25},{25,17},{2,10},{10... | collective-permute-start | bytes 3145736 | tf_op jit(solution)/shard_map/ppermute | solution.py:951
  754.4 99.7 %collective-permute-start.46 = (bf16[4,704,256]{2,1,0:T(8,128)(2,1)}, bf16[4,704,256]{2,1,0:T(8,128)(2,1)}, u32[]{:S(2)}, u32[]{:S(2)}) collective-permute-start(bf16[4,704,256]{2,1,0:T(8,128)(2,1)} %fusion.25), channel_id=1, source_target_pairs={{0,8},{8,0},{16,24},{24,16},{1,9},{9,1},{17,25},{25,17},{2,10},{10... | collective-permute-start | bytes 4325384 | tf_op jit(solution)/shard_map/ppermute | solution.py:954
  774.7 76.0 %collective-permute-start.34 = (bf16[4,256,256]{2,1,0:T(8,128)(2,1)S(1)}, bf16[4,256,256]{2,1,0:T(8,128)(2,1)S(1)}, u32[]{:S(2)}, u32[]{:S(2)}) collective-permute-start(bf16[4,256,256]{2,1,0:T(8,128)(2,1)S(1)} %fusion.29), channel_id=1, source_target_pairs={{0,8},{8,0},{16,24},{24,16},{1,9},{9,1},{17,25},{25,17},{2,10},{10... | collective-permute-start | bytes 1572872 | tf_op jit(solution)/shard_map/ppermute | solution.py:954
  852.3 491.5 %reduce-scatter.14.cloned.1.call-start = ((), (), s32[]{:S(2)}) async-start(), calls=%async_computation.10 | async-start | bytes 3604480 | tf_op jit(solution)/shard_map/reduce_scatter | solution.py:959
  852.4 65.8 %collective-permute-start.37 = (bf16[2,4,128,1408]{3,2,1,0:T(8,128)(2,1)}, bf16[2,4,128,1408]{3,2,1,0:T(8,128)(2,1)}, u32[]{:S(2)}, u32[]{:S(2)}) collective-permute-start(bf16[2,4,128,1408]{3,2,1,0:T(8,128)(2,1)} %get-tuple-element.124), channel_id=1, source_target_pairs={{0,16},{16,0},{8,24},{24,8},{1,17},{17,1},{9,25},{25,9},{2,18},{18... | collective-permute-start | bytes 8650760 | tf_op jit(solution)/shard_map/ppermute | solution.py:950
  853.5 67.5 %collective-permute-start.39 = (bf16[2,4,128,1408]{3,2,1,0:T(8,128)(2,1)}, bf16[2,4,128,1408]{3,2,1,0:T(8,128)(2,1)}, u32[]{:S(2)}, u32[]{:S(2)}) collective-permute-start(bf16[2,4,128,1408]{3,2,1,0:T(8,128)(2,1)} %get-tuple-element.126), channel_id=1, source_target_pairs={{0,8},{8,0},{16,24},{24,16},{1,9},{9,1},{17,25},{25,17},{2,10},{10... | collective-permute-start | bytes 8650760 | tf_op jit(solution)/shard_map/ppermute | solution.py:951
  861.2 484.9 %reduce-scatter.10.cloned.1.call-start = ((), (), s32[]{:S(2)}) async-start(), calls=%async_computation.8 | async-start | bytes 3604480 | tf_op jit(solution)/shard_map/reduce_scatter | solution.py:959
  861.2 199.5 %collective-permute-start.41 = (bf16[2,4,128,1408]{3,2,1,0:T(8,128)(2,1)}, bf16[2,4,128,1408]{3,2,1,0:T(8,128)(2,1)}, u32[]{:S(2)}, u32[]{:S(2)}) collective-permute-start(bf16[2,4,128,1408]{3,2,1,0:T(8,128)(2,1)} %get-tuple-element.129), channel_id=1, source_target_pairs={{0,16},{16,0},{8,24},{24,8},{1,17},{17,1},{9,25},{25,9},{2,18},{18... | collective-permute-start | bytes 8650760 | tf_op jit(solution)/shard_map/ppermute | solution.py:950
  862.7 201.7 %collective-permute-start.43 = (bf16[2,4,128,1408]{3,2,1,0:T(8,128)(2,1)}, bf16[2,4,128,1408]{3,2,1,0:T(8,128)(2,1)}, u32[]{:S(2)}, u32[]{:S(2)}) collective-permute-start(bf16[2,4,128,1408]{3,2,1,0:T(8,128)(2,1)} %get-tuple-element.131), channel_id=1, source_target_pairs={{0,8},{8,0},{16,24},{24,16},{1,9},{9,1},{17,25},{25,17},{2,10},{10... | collective-permute-start | bytes 8650760 | tf_op jit(solution)/shard_map/ppermute | solution.py:951
  919.9 90.4 %collective-permute-start.38 = (bf16[4,128,1408]{2,1,0:T(8,128)(2,1)S(1)}, bf16[4,128,1408]{2,1,0:T(8,128)(2,1)S(1)}, u32[]{:S(2)}, u32[]{:S(2)}) collective-permute-start(bf16[4,128,1408]{2,1,0:T(8,128)(2,1)S(1)} %fusion.21), channel_id=1, source_target_pairs={{0,8},{8,0},{16,24},{24,16},{1,9},{9,1},{17,25},{25,17},{2,10},{10... | collective-permute-start | bytes 4325384 | tf_op jit(solution)/shard_map/ppermute | solution.py:954
  922.7 89.5 %collective-permute-start.40 = (bf16[4,128,1408]{2,1,0:T(8,128)(2,1)S(1)}, bf16[4,128,1408]{2,1,0:T(8,128)(2,1)S(1)}, u32[]{:S(2)}, u32[]{:S(2)}) collective-permute-start(bf16[4,128,1408]{2,1,0:T(8,128)(2,1)S(1)} %fusion.22), channel_id=1, source_target_pairs={{0,16},{16,0},{8,24},{24,8},{1,17},{17,1},{9,25},{25,9},{2,18},{18... | collective-permute-start | bytes 4325384 | tf_op jit(solution)/shard_map/ppermute | solution.py:955
  1015.9 332.5 %reduce-scatter.12.cloned.1.call-start = ((), (), s32[]{:S(2)}) async-start(), calls=%async_computation.9 | async-start | bytes 3604480 | tf_op jit(solution)/shard_map/reduce_scatter | solution.py:959
  1060.1 44.9 %collective-permute-start.26 = (bf16[2,4,128,1536]{3,2,1,0:T(8,128)(2,1)}, bf16[2,4,128,1536]{3,2,1,0:T(8,128)(2,1)}, u32[]{:S(2)}, u32[]{:S(2)}) collective-permute-start(bf16[2,4,128,1536]{3,2,1,0:T(8,128)(2,1)} %get-tuple-element.151), channel_id=1, source_target_pairs={{0,4},{4,0},{1,5},{5,1},{2,6},{6,2},{3,7},{7,3},{8,12},{12,8},{9,1... | collective-permute-start | bytes 9437192 | tf_op jit(solution)/shard_map/ppermute | solution.py:939
  1064.4 63.3 %collective-permute-start.42 = (bf16[4,128,1408]{2,1,0:T(8,128)(2,1)}, bf16[4,128,1408]{2,1,0:T(8,128)(2,1)}, u32[]{:S(2)}, u32[]{:S(2)}) collective-permute-start(bf16[4,128,1408]{2,1,0:T(8,128)(2,1)} %fusion.23), channel_id=1, source_target_pairs={{0,8},{8,0},{16,24},{24,16},{1,9},{9,1},{17,25},{25,17},{2,10},{10... | collective-permute-start | bytes 4325384 | tf_op jit(solution)/shard_map/ppermute | solution.py:954
  1069.7 60.3 %collective-permute-start.44 = (bf16[4,128,1408]{2,1,0:T(8,128)(2,1)}, bf16[4,128,1408]{2,1,0:T(8,128)(2,1)}, u32[]{:S(2)}, u32[]{:S(2)}) collective-permute-start(bf16[4,128,1408]{2,1,0:T(8,128)(2,1)} %fusion.24), channel_id=1, source_target_pairs={{0,16},{16,0},{8,24},{24,8},{1,17},{17,1},{9,25},{25,9},{2,18},{18... | collective-permute-start | bytes 4325384 | tf_op jit(solution)/shard_map/ppermute | solution.py:955
  1125.4 70.6 %collective-permute-start.29 = (bf16[2,4,128,1536]{3,2,1,0:T(8,128)(2,1)}, bf16[2,4,128,1536]{3,2,1,0:T(8,128)(2,1)}, u32[]{:S(2)}, u32[]{:S(2)}) collective-permute-start(bf16[2,4,128,1536]{3,2,1,0:T(8,128)(2,1)} %get-tuple-element.156), channel_id=1, source_target_pairs={{0,16},{16,0},{8,24},{24,8},{1,17},{17,1},{9,25},{25,9},{2,18},{18... | collective-permute-start | bytes 9437192 | tf_op jit(solution)/shard_map/ppermute | solution.py:950
  1126.5 72.6 %collective-permute-start.31 = (bf16[2,4,128,1536]{3,2,1,0:T(8,128)(2,1)}, bf16[2,4,128,1536]{3,2,1,0:T(8,128)(2,1)}, u32[]{:S(2)}, u32[]{:S(2)}) collective-permute-start(bf16[2,4,128,1536]{3,2,1,0:T(8,128)(2,1)} %get-tuple-element.158), channel_id=1, source_target_pairs={{0,8},{8,0},{16,24},{24,16},{1,9},{9,1},{17,25},{25,17},{2,10},{10... | collective-permute-start | bytes 9437192 | tf_op jit(solution)/shard_map/ppermute | solution.py:951
  1134.1 216.6 %reduce-scatter.6.cloned.1.call-start = ((), (), s32[]{:S(2)}) async-start(), calls=%async_computation.6 | async-start | bytes 3932160 | tf_op jit(solution)/shard_map/reduce_scatter | solution.py:959
  (64 other events, 2242.6 us)
Sparse Core Ops, SparseCore 0:
  292.5 148.3 all-gather.1
  852.4 26.4 reduce-scatter.7
  881.3 55.1 reduce-scatter.13
  1016.0 55.4 reduce-scatter.9
  1134.2 55.7 reduce-scatter.11
  1240.3 59.9 reduce-scatter.5

commit v3 on v2

--- a/solution.py
+++ b/solution.py
@@ -13,7 +13,7 @@
 F32 = jnp.float32
 BF16 = jnp.bfloat16
 MESH = pl.DeviceIdType.MESH
-SPLITS = (True, True, True, True, True)
+SPLITS = (False, False, False, False, False)
 
 
 def params(**kw):
@@ -697,7 +697,7 @@
 def hidden_grad(dy, w_down, act, slope):
     rows, width = dy.shape
     ways, units, _ = w_down.shape
-    part = min(rows, 512)
+    part = min(rows, 1024)
     out = pl.BlockSpec((1, part, units), lambda t, i: (t, i, 0))
     return pl.pallas_call(
         hidden_grad_kernel,
@@ -771,7 +771,7 @@
 
 
 def put(outs, adds, j, at, wide, value):
-    if len(outs) == 1:
+    if len(outs[0].shape) == 4 and len(outs) == 1:
         if adds:
             value = value + adds[0][j, 0, :, at : at + wide].astype(F32)
         outs[0][j, 0, :, at : at + wide] = value.astype(BF16)
@@ -782,11 +782,15 @@
     for part, (which, row) in enumerate(spots):
         got = value[part * half : (part + 1) * half]
         if adds:
-            got = got + adds[which][row, 0, :, at : at + wide].astype(F32)
-        outs[which][row, 0, :, at : at + wide] = got.astype(BF16)
-
-
-def by_rows_kernel(chips, n, n_out, each, at_ref, left_ref, *refs):
+            got = got + adds[0][which, row, 0, :, at : at + wide].astype(F32)
+        got = got.astype(BF16)
+        if len(outs) == 1:
+            outs[0][which, row, 0, :, at : at + wide] = got
+        else:
+            outs[which][row, 0, :, at : at + wide] = got
+
+
+def by_rows_kernel(chips, n, each, n_out, at_ref, left_ref, *refs):
     rights, adds, outs = refs[:n], refs[n : len(refs) - n_out], refs[len(refs) - n_out :]
     left = columns(left_ref, at_ref, chips, each)
     at = 0
@@ -798,7 +802,7 @@
         at += wide
 
 
-def by_cols_kernel(chips, n_out, each, at_ref, right_ref, left_ref, *refs):
+def by_cols_kernel(chips, each, n_out, at_ref, right_ref, left_ref, *refs):
     adds, outs = refs[: len(refs) - n_out], refs[len(refs) - n_out :]
     acc = tn(left_ref[0], columns(right_ref, at_ref, chips, each))
     for j in range(chips):
@@ -807,19 +811,26 @@
 
 def weight_grad(kernel, whole_side, parted, tall, wide, at, adds, chips, split, name):
     ways, rows, _ = parted[0].shape
-    if split:
+    adds = list(adds or [])
+    if not split:
+        shapes = [(chips, ways, tall, wide)]
+    elif adds:
         shapes = [(2, ways, tall // 2, wide)] * 4
     else:
-        shapes = [(chips, ways, tall, wide)]
-    blocks = [pl.BlockSpec((c, 1, h, w), lambda t: (0, t, 0, 0)) for c, _, h, w in shapes]
-    adds = list(adds or [])
-    return pl.pallas_call(
-        kernel,
+        shapes = [(4, 2, ways, tall // 2, wide)]
+
+    def block(shape):
+        front = len(shape) - 3
+        return pl.BlockSpec(shape[:front] + (1,) + shape[-2:], lambda t: (0,) * front + (t, 0, 0))
+
+    outs = [block(s) for s in shapes]
+    return pl.pallas_call(
+        functools.partial(kernel, len(shapes)),
         grid=(ways,),
         in_specs=[pl.BlockSpec(memory_space=pltpu.SMEM), whole(whole_side.shape)]
         + [pl.BlockSpec((1, rows, p.shape[2]), lambda t: (t, 0, 0)) for p in parted]
-        + blocks[: len(adds)],
-        out_specs=blocks,
+        + [block(a.shape) for a in adds],
+        out_specs=outs,
         out_shape=[jax.ShapeDtypeStruct(s, BF16) for s in shapes],
         compiler_params=params(),
         name=name,
@@ -828,14 +839,14 @@
 
 def by_rows(left, rights, at, adds, chips, split):
     each = left.shape[1] // (2 * chips)
-    kernel = functools.partial(by_rows_kernel, chips, len(rights), 4 if split else 1, each)
+    kernel = functools.partial(by_rows_kernel, chips, len(rights), each)
     wide = sum(r.shape[2] for r in rights)
     return weight_grad(kernel, left, rights, each, wide, at, adds, chips, split, "by_rows")
 
 
 def by_cols(left, right, at, adds, chips, split):
     each = right.shape[1] // (2 * chips)
-    kernel = functools.partial(by_cols_kernel, chips, 4 if split else 1, each)
+    kernel = functools.partial(by_cols_kernel, chips, each)
     return weight_grad(kernel, right, [left], left.shape[2], each, at, adds, chips, split, "by_cols")
 
 
@@ -941,77 +952,121 @@
     def add(a, b):
         return a.astype(F32) + b.astype(F32)
 
-    def scatter(arrays):
-        if len(arrays) == 1:
+    class Scatter:
+        def begin(self, arrays):
             part = lax.psum_scatter(arrays[0], "chip", scatter_dimension=0, tiled=True)
-            part = part.reshape(part.shape[1:])
-        else:
-            y_send, y_keep, x_send, x_keep = arrays
-            from_y = lax.ppermute(y_send, "chip", OVER_Y)
-            from_x = lax.ppermute(x_send, "chip", OVER_X)
-            upper = add(y_keep[1], from_y[1]).astype(BF16)
-            lower_half = add(x_keep[1], from_x[1]).astype(BF16)
-            upper = lax.ppermute(upper, "chip", OVER_X)
-            lower_half = lax.ppermute(lower_half, "chip", OVER_Y)
-            upper = add(add(y_keep[0], from_y[0]), upper).astype(BF16)
-            lower_half = add(add(x_keep[0], from_x[0]), lower_half).astype(BF16)
-            part = jnp.concatenate([upper, lower_half], axis=1)
-        part = lax.psum_scatter(part, "tensor", scatter_dimension=0, tiled=True)
-        return part.reshape(part.shape[1:]).astype(F32)
+            self.part = lax.optimization_barrier(part.reshape(part.shape[1:]))
+            self.parts = [self.block(0)]
+
+        def block(self, k):
+            return lax.dynamic_index_in_dim(self.part, (way + k) % ways, 0, False)
+
+        def send(self, *steps):
+            got = [
+                lax.ppermute(self.block(k), "tensor", [(i, (i + k) % ways) for i in range(ways)])
+                for k in steps
+                if k < ways
+            ]
+            self.parts += got
+            return tuple(got)
+
+        def rest(self):
+            part = lax.psum_scatter(self.part, "tensor", scatter_dimension=0, tiled=True)
+            self.parts = [part.reshape(part.shape[1:])]
+
+        def finish(self):
+            return sum(a.astype(F32) for a in self.parts)
+
+    last = [()]
+
+    def run(fn, *arrays):
+        out = fn(*lax.optimization_barrier(arrays + last[0])[: len(arrays)])
+        last[0] = tuple(jax.tree.leaves(out))
+        return out
+
+    ours_at = {s: blocks_of(core, s) for s in (True, False)}
+    theirs_at = {s: blocks_of(1 - core, s) for s in (True, False)}
+
+    def rows_grad(split, at, rights, left, adds=None):
+        n = len(rights)
+        got = lambda left, *more: by_rows(left, more[:n], at[split], more[n:], chips, split)
+        return run(got, left, *rights, *(adds or []))
+
+    def cols_grad(split, at, left, right, adds=None):
+        got = lambda left, right, *more: by_cols(left, right, at[split], more, chips, split)
+        return run(got, left, right, *(adds or []))
 
     split_down, split_up, split_glu, split_out, split_three = [square and s for s in SPLITS]
+    down, up, glu, out, three = [Scatter() for _ in range(5)]
     gy = cotangent
 
-    theirs_down = by_cols(hidden, gy, blocks_of(1 - core, split_down), None, chips, split_down)
-    swap_down = swap(theirs_down)
-    g_up, g_glu = hidden_grad(behind(gy, *theirs_down), w_down_all, act, slope)
-    ours_down = by_cols(behind(hidden, g_up), gy, blocks_of(core, split_down), swap_down, chips, split_down)
-    grad_w_down = scatter(ours_down)
-
-    middle_now = behind(middle, *ours_down)
-    theirs_up = by_rows(middle_now, [g_up], blocks_of(1 - core, split_up), None, chips, split_up)
-    swap_up = swap(theirs_up)
-    theirs_glu = by_rows(behind(middle, *theirs_up), [g_glu], blocks_of(1 - core, split_glu), None, chips, split_glu)
-    swap_glu = swap(theirs_glu)
-    ours_up = by_rows(behind(middle, *theirs_glu), [g_up], blocks_of(core, split_up), swap_up, chips, split_up)
-    grad_w_up = scatter(ours_up)
-    ours_glu = by_rows(behind(middle, *ours_up), [g_glu], blocks_of(core, split_glu), swap_glu, chips, split_glu)
-    grad_w_glu = scatter(ours_glu)
-    g_middle = back([behind(g_up, *ours_glu), g_glu], [w_up_all, w_glu_all], [0, 0], units)
-
-    inverse2 = lax.rsqrt(jnp.mean(resid * resid, axis=1, keepdims=True) + EPS)
-    unit2 = resid * inverse2
-    mlp_gain_part = jnp.sum(g_middle * unit2, axis=0)
-    g_resid = cotangent.astype(F32) + norm_pullback(g_middle, unit2, inverse2, feedforward_gain)
-    g_branch = g_resid.astype(BF16)
-    theirs_out = by_cols(mixed, g_branch, blocks_of(1 - core, split_out), None, chips, split_out)
-    swap_out = swap(theirs_out)
-    g_mixed = mixed_grad(behind(g_branch, *theirs_out), w_out_all)
-    ours_out = by_cols(behind(mixed, g_mixed), g_branch, blocks_of(core, split_out), swap_out, chips, split_out)
-    grad_w_out = scatter(ours_out)
-
-    g_state, g_gate, gain_part, back_totals = backward_total(
-        p, state, behind(g_mixed, *ours_out), lower, gain, starts
+    def beside(arrived):
+        last[0] = last[0] + arrived
+
+    def send(scattered, *steps):
+        return scattered.send(*steps) if few else ()
+
+    few = ways <= 4
+
+    swapped = swap(cols_grad(split_down, theirs_at, hidden, gy))
+    down.begin(cols_grad(split_down, ours_at, hidden, gy, swapped))
+    g_up, g_glu = run(hidden_grad, gy, w_down_all, act, slope)
+    swapped_up = swap(rows_grad(split_up, theirs_at, [g_up], middle))
+    swapped_glu = swap(rows_grad(split_glu, theirs_at, [g_glu], middle))
+    up.begin(rows_grad(split_up, ours_at, [g_up], middle, swapped_up))
+    glu.begin(rows_grad(split_glu, ours_at, [g_glu], middle, swapped_glu))
+    g_middle = run(
+        lambda a, b, c, d: back([a, b], [c, d], [0, 0], units), g_up, g_glu, w_up_all, w_glu_all
     )
-    all_back = from_all(back_totals, "tensor")
+    def second_norm(resid, g_middle, gy):
+        inverse2 = lax.rsqrt(jnp.mean(resid * resid, axis=1, keepdims=True) + EPS)
+        unit2 = resid * inverse2
+        mlp_gain_part = jnp.sum(g_middle * unit2, axis=0)
+        g_resid = gy.astype(F32) + norm_pullback(g_middle, unit2, inverse2, feedforward_gain)
+        return mlp_gain_part, g_resid, g_resid.astype(BF16)
+
+    moving = send(down, 1)
+    mlp_gain_part, g_resid, g_branch = run(second_norm, resid, g_middle, gy)
+    swapped_out = swap(cols_grad(split_out, theirs_at, mixed, g_branch))
+    g_mixed = run(mixed_grad, g_branch, w_out_all)
+    beside(moving)
+    out.begin(cols_grad(split_out, ours_at, mixed, g_branch, swapped_out))
+    moving = send(down, 2)
+    g_state, g_gate, gain_part, back_totals = run(backward_total, p, state, g_mixed, lower, gain, starts)
+    beside(moving)
+    all_back = lax.all_gather(back_totals, "tensor", axis=0)
     after = jnp.zeros((ways, 1, chans), F32)
     seen = jnp.zeros((ways, 1, chans), F32)
     for k in range(ways - 1, 0, -1):
         seen = all_totals[k, :, 0:1] * seen + all_back[k]
         after = jnp.where(way == k - 1, seen, after)
-    g_in, g_forget, lower_part = backward_scan(p, state, g_state, lower, starts, enter, after)
+    moving = send(down, 3)
+    g_in, g_forget, lower_part = run(backward_scan, p, state, g_state, lower, starts, enter, after)
+    beside(moving)
 
     g_three = [g_in, g_forget, g_gate]
-    theirs_three = by_rows(normed, g_three, blocks_of(1 - core, split_three), None, chips, split_three)
-    swap_three = swap(theirs_three)
-    output = feed_down(behind(hidden, *theirs_three), w_down_all, resid)
-    ours_three = by_rows(behind(normed, output), g_three, blocks_of(core, split_three), swap_three, chips, split_three)
-    grad_three = scatter(ours_three)
-    g_normed = back([behind(g_in, *ours_three), g_forget, g_gate], [w3, w3, w3], [0, 1, 2], chans)
-
-    unit1 = x * inverse1
-    norm_gain_part = jnp.sum(g_normed * unit1, axis=0)
-    token_gradient = g_resid + norm_pullback(g_normed, unit1, inverse1, first_norm_gain)
+    swapped = swap(rows_grad(split_three, theirs_at, g_three, normed))
+    three.begin(rows_grad(split_three, ours_at, g_three, normed, swapped))
+    moving = send(up, 1, 2, 3)
+    output = run(feed_down, hidden, w_down_all, resid)
+    beside(moving)
+    moving = send(glu, 1)
+    g_normed = run(
+        lambda a, b, c, w: back([a, b, c], [w, w, w], [0, 1, 2], chans), g_in, g_forget, g_gate, w3
+    )
+    beside(moving)
+    moving = send(glu, 2)
+
+    def first_norm_back(x, g_normed, g_resid):
+        x = x.astype(F32)
+        inverse1 = lax.rsqrt(jnp.mean(x * x, axis=1, keepdims=True) + EPS)
+        unit1 = x * inverse1
+        norm_gain_part = jnp.sum(g_normed * unit1, axis=0)
+        return norm_gain_part, g_resid + norm_pullback(g_normed, unit1, inverse1, first_norm_gain)
+
+    norm_gain_part, token_gradient = run(first_norm_back, tokens, g_normed, g_resid)
+    beside(moving)
+    moving = send(glu, 3)
 
     small = jnp.stack(
         [
@@ -1022,7 +1077,17 @@
             jnp.sum(lam_sum, axis=1).reshape(width),
         ]
     )
-    small = lax.psum(small, every)
+    moving += send(out, 1, 2, 3)
+    small = run(lambda v: lax.psum(v, every), small)
+    beside(moving)
+    three.part = behind(three.part, *last[0])
+    three.rest()
+    if not few:
+        for s in (down, up, glu, out):
+            s.rest()
+    grad_w_down, grad_w_up, grad_w_glu, grad_w_out, grad_three = [
+        s.finish() for s in (down, up, glu, out, three)
+    ]
     mean_forget = jnp.sum(small[4]) / (rows * ways * groups * width)
     return (
         output,

time: 1370 us -> 1160 us (0.85)
  waiting for transfers between devices: 303 us -> 112 us
  other arithmetic: 116 us -> 63.8 us
  starting transfers between devices: 38.8 us -> 57.5 us
    ppermute x20 -> x12, waiting for transfers between devices: 290 us -> 3.35 us  [send(): lax.ppermute(self.block(k), 'tensor', [(i, (i + k) % ways) for i in range...]
    reduce_scatter x5 -> x1, waiting for transfers between devices: 0.01 us -> 48 us  [rest(): lax.psum_scatter(self.part, 'tensor', scatter_dimension=0, tiled=True)]
    convert_element_type x26 -> x2, other arithmetic: 54.6 us -> 7.02 us  [the longest x1 5.72 us: second_norm(): return (mlp_gain_part, g_resid, g_resid.astype(BF16))]
    ppermute x20 -> x5, waiting for transfers between devices: 3.17 us -> 36.9 us  [swap(): return [lax.ppermute(a, 'core', SWAP) for a in arrays]]
    ppermute x20 -> x12, starting transfers between devices: 19.9 us -> 44.7 us  [send(): lax.ppermute(self.block(k), 'tensor', [(i, (i + k) % ways) for i in range...]
    unnamed x6 -> x12, waiting for transfers between devices: 0.1 us -> 17.6 us
    all_gather x0 -> x1, blocking collectives: none -> 13.9 us  [local(): all_back = lax.all_gather(back_totals, 'tensor', axis=0)]
  transfers between devices with their start and end apart: 55 -> 30, of which waited for: 13 -> 7; matrix products, arithmetic and copies ran while one was open for 8% -> 6% of each run, Pallas kernels for 38% -> 48%
where the time goes in v3:
time: 1160 us
  Pallas kernels  830 us (72%)
  waiting for transfers between devices  112 us (10%)
  other arithmetic  63.8 us (6%)
  starting transfers between devices  57.5 us (5%)
  blocking collectives  51.3 us (4%)
  local copies, waits for them, and re-layouts  21.8 us (2%)
  between operations  19.7 us (2%)
    pallas_call x1, Pallas kernels, gather_weights(): pl.pallas_call(functools.partial(gather_kernel, n, ways), in_specs=[any_s...  277 us
    pallas_call x10, Pallas kernels, weight_grad(): pl.pallas_call(functools.partial(kernel, len(shapes)), grid=(ways,), in_s...  174 us
    pallas_call x2, Pallas kernels, back(): pl.pallas_call(functools.partial(back_kernel, len(grads)), grid=(width //...  101 us
    pallas_call x1, Pallas kernels, feed_up(): pl.pallas_call(up_kernel, grid=(ways, rows // part), in_specs=[pl.BlockSp...  60.8 us
    reduce_scatter x1, waiting for transfers between devices, rest(): lax.psum_scatter(self.part, 'tensor', scatter_dimension=0, tiled=True)  48 us
    ppermute x12, starting transfers between devices, send(): lax.ppermute(self.block(k), 'tensor', [(i, (i + k) % ways) for i in range...  44.7 us
    psum x1, blocking collectives, local(): small = run(lambda v: lax.psum(v, every), small)  37.3 us
    pallas_call x1, Pallas kernels, hidden_grad(): pl.pallas_call(hidden_grad_kernel, grid=(ways, rows // part), in_specs=[p...  37.2 us
  transfers between devices with their start and end apart: 30, of which 7 were waited for; matrix products, arithmetic and copies ran while one was open for 6% of the time, Pallas kernels for 48%

profile of v3, /device:TPU:0, one launch (start us, length us, event | category | flops | bytes accessed | tf_op | source)
XLA Modules:
  0.0 1155.1 jit_solution(11404382469999285832)
XLA Ops:
  14.4 276.7 %gather_weights.1 = (bf16[4,2048,1536]{2,1,0:T(8,128)(2,1)}, bf16[4,512,2048]{2,1,0:T(8,128)(2,1)}, bf16[4,2048,1408]{2,1,0:T(8,128)(2,1)}, bf16[4,2048,1408]{2,1,0:T(8,128)(2,1)}) custom-call(bf16[2048,1536]{1,0:T(8,128)(2,1)} %pad_maximum_fusion.refs_0_, bf16[512,2048]{1,0:T(8,128)(2,1)} %refs_1_.1, bf16[2048,1408]{1,0:T(8,128)(2,1)} %refs_2_.1, ...), custom_call_target="tpu_custom_call" | custom-call | tf_op jit(solution)/shard_map/gather_weights/pallas_call | solution.py:248
  311.9 32.4 %project.1.p_ref.pf_ref.pg_ref.pi_ref = f32[4,1024,1536]{2,1,0:T(8,128)} custom-call(bf16[1024,2048]{1,0:T(8,128)(2,1)} %fusion.5.x_ref.left_ref, bf16[4,2048,1536]{2,1,0:T(8,128)(2,1)} %get-tuple-element.185.w_ref.refs_3_.refs_4_.refs_5_), custom_call_target="tpu_custom_call" | custom-call | tf_op jit(solution)/shard_map/project/pallas_call | solution.py:272
  372.0 22.4 %forward_scan.1 = (f32[4,1024,512]{2,1,0:T(8,128)}, bf16[4,1024,512]{2,1,0:T(8,128)(2,1)}, f32[4,8,512]{2,1,0:T(8,128)}) custom-call(s32[3]{0:T(128)} %add_subtract_fusion.starts_ref, f32[4,1024,1536]{2,1,0:T(8,128)} %project.1.p_ref.pf_ref.pg_ref.pi_ref, f32[4,1,512]{2,1,0:T(1,128)} %get-tuple-element.164.lower_ref, ...), custom_call_target="tpu_custom_call" | custom-call | tf_op jit(solution)/shard_map/forward_scan/pallas_call | solution.py:393
  410.4 60.8 %feed_up.1 = (bf16[4,1024,1408]{2,1,0:T(8,128)(2,1)}, bf16[4,1024,1408]{2,1,0:T(8,128)(2,1)}, bf16[4,1024,1408]{2,1,0:T(8,128)(2,1)}) custom-call(bf16[1024,2048]{1,0:T(8,128)(2,1)} %get-tuple-element.133.x_ref.left_ref, bf16[4,2048,1408]{2,1,0:T(8,128)(2,1)} %get-tuple-element.138.up_ref.refs_2_, bf16[4,2048,1408]{2,1,0:T(8,128)(2,1)} %get-tuple-element.139.glu_ref.refs_3_), custom_call_target="tpu_custom_call" | custom-call | tf_op jit(solution)/shard_map/feed_up/pallas_call | solution.py:654
  471.2 17.6 %by_cols.4 = bf16[4,4,1408,256]{3,2,1,0:T(8,128)(2,1)} custom-call(s32[4]{0:T(128)} %fusion.24.at_ref, bf16[1024,2048]{1,0:T(8,128)(2,1)} %dy_ref, bf16[4,1024,1408]{2,1,0:T(8,128)(2,1)} %get-tuple-element.179.left_ref.h_ref), custom_call_target="tpu_custom_call" | custom-call | tf_op jit(solution)/shard_map/by_cols/pallas_call | solution.py:827
  489.3 17.5 %collective-permute-done.6.refs_0_ = bf16[4,4,1408,256]{3,2,1,0:T(8,128)(2,1)} collective-permute-done((bf16[4,4,1408,256]{3,2,1,0:T(8,128)(2,1)}, bf16[4,4,1408,256]{3,2,1,0:T(8,128)(2,1)}, u32[]{:S(2)}, u32[]{:S(2)}) %collective-permute-start.6) | collective-permute-done | bytes 11534368 | tf_op jit(solution)/shard_map/ppermute | solution.py:950
  506.8 19.0 %by_cols.5 = bf16[4,4,1408,256]{3,2,1,0:T(8,128)(2,1)} custom-call(s32[4]{0:T(128)} %fusion.25.at_ref, bf16[1024,2048]{1,0:T(8,128)(2,1)} %dy_ref, bf16[4,1024,1408]{2,1,0:T(8,128)(2,1)} %get-tuple-element.179.left_ref.h_ref, bf16[4,4,1408,256]{3,2,1,0:T(8,128)(2,1)} %collective-permute-done.6.refs_0_), custom_call_target="tpu_custom_call" | custom-call | tf_op jit(solution)/shard_map/by_cols/pallas_call | solution.py:827
  526.3 37.2 %hidden_grad.1 = (bf16[4,1024,1408]{2,1,0:T(8,128)(2,1)}, bf16[4,1024,1408]{2,1,0:T(8,128)(2,1)}) custom-call(bf16[1024,2048]{1,0:T(8,128)(2,1)} %dy_ref, bf16[4,1408,2048]{2,1,0:T(8,128)(2,1)} %bitcast.133, bf16[4,1024,1408]{2,1,0:T(8,128)(2,1)} %get-tuple-element.122.act_ref, bf16[4,1024,1408]{2,1,0:T(8,128)(2,1)} %get-tuple-element.123.slope_ref), custom_call_target="tpu_custom_call" | custom-call | tf_op jit(solution)/shard_map/hidden_grad/pallas_call | solution.py:702
  563.5 19.0 %by_rows.6 = bf16[4,4,256,1408]{3,2,1,0:T(8,128)(2,1)} custom-call(s32[4]{0:T(128)} %fusion.24.at_ref, bf16[1024,2048]{1,0:T(8,128)(2,1)} %get-tuple-element.133.x_ref.left_ref, bf16[4,1024,1408]{2,1,0:T(8,128)(2,1)} %get-tuple-element.136.refs_0_), custom_call_target="tpu_custom_call" | custom-call | tf_op jit(solution)/shard_map/by_rows/pallas_call | solution.py:827
  582.5 19.0 %by_rows.7 = bf16[4,4,256,1408]{3,2,1,0:T(8,128)(2,1)} custom-call(s32[4]{0:T(128)} %fusion.24.at_ref, bf16[1024,2048]{1,0:T(8,128)(2,1)} %get-tuple-element.133.x_ref.left_ref, bf16[4,1024,1408]{2,1,0:T(8,128)(2,1)} %get-tuple-element.137.refs_0_.refs_1_), custom_call_target="tpu_custom_call" | custom-call | tf_op jit(solution)/shard_map/by_rows/pallas_call | solution.py:827
  601.8 20.1 %by_rows.8 = bf16[4,4,256,1408]{3,2,1,0:T(8,128)(2,1)} custom-call(s32[4]{0:T(128)} %fusion.25.at_ref, bf16[1024,2048]{1,0:T(8,128)(2,1)} %get-tuple-element.133.x_ref.left_ref, bf16[4,1024,1408]{2,1,0:T(8,128)(2,1)} %get-tuple-element.136.refs_0_, bf16[4,4,256,1408]{3,2,1,0:T(8,128)(2,1)} %collective-permute-done.8.refs_1_), custom_call_target="tpu_custom_call" | custom-call | tf_op jit(solution)/shard_map/by_rows/pallas_call | solution.py:827
  621.9 20.1 %by_rows.9 = bf16[4,4,256,1408]{3,2,1,0:T(8,128)(2,1)} custom-call(s32[4]{0:T(128)} %fusion.25.at_ref, bf16[1024,2048]{1,0:T(8,128)(2,1)} %get-tuple-element.133.x_ref.left_ref, bf16[4,1024,1408]{2,1,0:T(8,128)(2,1)} %get-tuple-element.137.refs_0_.refs_1_, bf16[4,4,256,1408]{3,2,1,0:T(8,128)(2,1)} %collective-permute-done.7.refs_1_), custom_call_target="tpu_custom_call" | custom-call | tf_op jit(solution)/shard_map/by_rows/pallas_call | solution.py:827
  642.6 64.1 %back.2 = f32[1024,2048]{1,0:T(8,128)} custom-call(bf16[4,1024,1408]{2,1,0:T(8,128)(2,1)} %get-tuple-element.136.refs_0_, bf16[4,1024,1408]{2,1,0:T(8,128)(2,1)} %get-tuple-element.137.refs_0_.refs_1_, bf16[4,2048,1408]{2,1,0:T(8,128)(2,1)} %get-tuple-element.138.up_ref.refs_2_, bf16[4,2048,1408]{2,1,0:T(8,128)(2,1)} %get-tuple-element.139.glu_ref.refs_3_), custom_call_target="tpu_custom_call" | custom-call | tf_op jit(solution)/shard_map/back/pallas_call | solution.py:738
  770.3 23.4 %backward_total.1 = (f32[4,1024,512]{2,1,0:T(8,128)}, bf16[4,1024,512]{2,1,0:T(8,128)(2,1)}, f32[4,8,512]{2,1,0:T(8,128)}, f32[4,1,512]{2,1,0:T(1,128)}) custom-call(s32[3]{0:T(128)} %add_subtract_fusion.starts_ref, f32[4,1024,1536]{2,1,0:T(8,128)} %project.1.p_ref.pf_ref.pg_ref.pi_ref, f32[4,1024,1536]{2,1,0:T(8,128)} %project.1.p_ref.pf_ref.pg_ref.pi_ref, ...), custom_call_target="tpu_custom_call" | custom-call | tf_op jit(solution)/shard_map/backward_total/pallas_call | solution.py:481
  809.1 23.4 %backward_scan.1 = (bf16[4,1024,512]{2,1,0:T(8,128)(2,1)}, bf16[4,1024,512]{2,1,0:T(8,128)(2,1)}, f32[4,8,512]{2,1,0:T(8,128)}) custom-call(s32[3]{0:T(128)} %add_subtract_fusion.starts_ref, f32[4,1024,1536]{2,1,0:T(8,128)} %project.1.p_ref.pf_ref.pg_ref.pi_ref, f32[4,1024,1536]{2,1,0:T(8,128)} %project.1.p_ref.pf_ref.pg_ref.pi_ref, ...), custom_call_target="tpu_custom_call" | custom-call | tf_op jit(solution)/shard_map/backward_scan/pallas_call | solution.py:575
  832.5 19.2 %by_rows.10 = bf16[4,4,256,1536]{3,2,1,0:T(8,128)(2,1)} custom-call(s32[4]{0:T(128)} %fusion.24.at_ref, bf16[1024,2048]{1,0:T(8,128)(2,1)} %fusion.5.x_ref.left_ref, bf16[4,1024,512]{2,1,0:T(8,128)(2,1)} %get-tuple-element.182.refs_0_, bf16[4,1024,512]{2,1,0:T(8,128)(2,1)} %get-tuple-element.183.refs_1_, bf16[4,1024,512]{2,1,0:T(8,128)(2,1)} %get-tuple-element.184.refs_2_), custom_call_target="tpu_custom_call" | custom-call | tf_op jit(solution)/shard_map/by_rows/pallas_call | solution.py:827
  851.8 19.4 %collective-permute-done.13.refs_3_ = bf16[4,4,256,1536]{3,2,1,0:T(8,128)(2,1)} collective-permute-done((bf16[4,4,256,1536]{3,2,1,0:T(8,128)(2,1)}, bf16[4,4,256,1536]{3,2,1,0:T(8,128)(2,1)}, u32[]{:S(2)}, u32[]{:S(2)}) %collective-permute-start.13) | collective-permute-done | bytes 12582944 | tf_op jit(solution)/shard_map/ppermute | solution.py:950
  871.2 20.6 %by_rows.11 = bf16[4,4,256,1536]{3,2,1,0:T(8,128)(2,1)} custom-call(s32[4]{0:T(128)} %fusion.25.at_ref, bf16[1024,2048]{1,0:T(8,128)(2,1)} %fusion.5.x_ref.left_ref, bf16[4,1024,512]{2,1,0:T(8,128)(2,1)} %get-tuple-element.182.refs_0_, bf16[4,1024,512]{2,1,0:T(8,128)(2,1)} %get-tuple-element.183.refs_1_, bf16[4,1024,512]{2,1,0:T(8,128)(2,1)} %get-tuple-element.184.refs_2_, ...), custom_call_target="tpu_custom_call" | custom-call | tf_op jit(solution)/shard_map/by_rows/pallas_call | solution.py:827
  905.1 16.9 %reduce-scatter.27.cloned.1.call-done = bf16[1,4,512,256]{3,2,1,0:T(8,128)(2,1)} async-done(((bf16[4,4,512,256]{3,2,1,0:T(8,128)(2,1)}), bf16[1,4,512,256]{3,2,1,0:T(8,128)(2,1)}) %reduce-scatter.27.cloned.1.call-update) | async-done | bytes 1048592
  925.3 34.6 %feed_down.1 = bf16[1024,2048]{1,0:T(8,128)(2,1)} custom-call(bf16[4,1024,1408]{2,1,0:T(8,128)(2,1)} %get-tuple-element.179.left_ref.h_ref, bf16[4,1408,2048]{2,1,0:T(8,128)(2,1)} %bitcast.134, f32[1024,2048]{1,0:T(8,128)} %get-tuple-element.181.resid_ref), custom_call_target="tpu_custom_call" | custom-call | tf_op jit(solution)/shard_map/feed_down/pallas_call | solution.py:676
  963.6 25.0 %collective-permute-start.18 = (bf16[256,1408]{1,0:T(8,128)(2,1)}, bf16[256,1408]{1,0:T(8,128)(2,1)}, u32[]{:S(2)}, u32[]{:S(2)}) collective-permute-start(bf16[256,1408]{1,0:T(8,128)(2,1)} %get-tuple-element.199), channel_id=1, source_target_pairs={{0,2},{1,3},{2,0},{3,1},{4,6},{5,7},{6,4},{7,5},{8,10},{9,11},{10,... | collective-permute-start | bytes 2162696 | tf_op jit(solution)/shard_map/ppermute | solution.py:966
  988.6 36.7 %back.3 = f32[1024,2048]{1,0:T(8,128)} custom-call(bf16[4,1024,512]{2,1,0:T(8,128)(2,1)} %get-tuple-element.182.refs_0_, bf16[4,1024,512]{2,1,0:T(8,128)(2,1)} %get-tuple-element.183.refs_1_, bf16[4,1024,512]{2,1,0:T(8,128)(2,1)} %get-tuple-element.184.refs_2_, bf16[4,2048,1536]{2,1,0:T(8,128)(2,1)} %get-tuple-element.185.w_ref.refs_3_.refs_4_.refs_5_, ...), custom_call_target="tpu_custom_call" | custom-call | tf_op jit(solution)/shard_map/back/pallas_call | solution.py:738
  1045.3 37.3 %psum.7 = f32[5,2048]{1,0:T(8,128)S(1)} all-reduce(f32[5,2048]{1,0:T(8,128)S(1)} %stack.79), channel_id=1, replica_groups=mesh['chip'=4,'core'=2,'tensor'=4] {'tensor','chip','core'}, use_global_device_ids=true, to_apply=%region_13.14 | all-reduce | flops 10240 | bytes 81920 | tf_op jit(solution)/shard_map/psum | solution.py:1081
  1095.5 48.0 %reduce-scatter.17.cloned.1.call-done = bf16[1,256,1536]{2,1,0:T(8,128)(2,1)} async-done(((bf16[4,256,1536]{2,1,0:T(8,128)(2,1)}), bf16[1,256,1536]{2,1,0:T(8,128)(2,1)}) %reduce-scatter.17.cloned.1.call-update) | async-done | bytes 786448 | tf_op jit(solution)/shard_map/reduce_scatter | solution.py:974
  (158 shorter events, 205.1 us)
Async XLA Ops:
  8.0 518.3 %all-gather.3.cloned.1.call-start = ((), (), s32[]{:S(2)}) async-start(), calls=%async_computation.6 | async-start | bytes 23789568 | tf_op jit(solution)/shard_map/all_gather | solution.py:912
  293.2 442.1 %reduce-scatter.19.cloned.1.call-start = ((), (), s32[]{:S(2)}) async-start(), calls=%async_computation.8 | async-start | bytes 14417920
  293.3 51.1 %collective-permute-start = (f32[2,512]{1,0:T(2,128)S(1)}, f32[2,512]{1,0:T(2,128)S(1)}, u32[]{:S(2)}, u32[]{:S(2)}) collective-permute-start(f32[2,512]{1,0:T(2,128)S(1)} %pad_maximum_fusion.1), channel_id=1, source_target_pairs={{1,0},{2,1},{3,2},{0,3},{5,4},{6,5},{7,6},{4,7},{9,8},{10,9},{11,1... | collective-permute-start | bytes 12296 | tf_op jit(solution)/shard_map/ppermute | solution.py:876
  299.0 45.4 %collective-permute-start.1 = (f32[2,512]{1,0:T(2,128)S(1)}, f32[2,512]{1,0:T(2,128)S(1)}, u32[]{:S(2)}, u32[]{:S(2)}) collective-permute-start(f32[2,512]{1,0:T(2,128)S(1)} %pad_maximum_fusion.1), channel_id=1, source_target_pairs={{2,0},{3,1},{0,2},{1,3},{6,4},{7,5},{4,6},{5,7},{10,8},{11,9},{8,1... | collective-permute-start | bytes 12296 | tf_op jit(solution)/shard_map/ppermute | solution.py:876
  299.0 45.4 %collective-permute-start.2 = (f32[2,512]{1,0:T(2,128)S(1)}, f32[2,512]{1,0:T(2,128)S(1)}, u32[]{:S(2)}, u32[]{:S(2)}) collective-permute-start(f32[2,512]{1,0:T(2,128)S(1)} %pad_maximum_fusion.1), channel_id=1, source_target_pairs={{3,0},{0,1},{1,2},{2,3},{7,4},{4,5},{5,6},{6,7},{11,8},{8,9},{9,10... | collective-permute-start | bytes 12296 | tf_op jit(solution)/shard_map/ppermute | solution.py:876
  525.8 366.1 %reduce-scatter.23.cloned.1.call-start = ((), (), s32[]{:S(2)}) async-start(), calls=%async_computation.10 | async-start | bytes 14417920
  601.5 20.4 %collective-permute-start.7 = (bf16[4,4,256,1408]{3,2,1,0:T(8,128)(2,1)}, bf16[4,4,256,1408]{3,2,1,0:T(8,128)(2,1)}, u32[]{:S(2)}, u32[]{:S(2)}) collective-permute-start(bf16[4,4,256,1408]{3,2,1,0:T(8,128)(2,1)} %by_rows.7), channel_id=1, source_target_pairs={{0,4},{4,0},{1,5},{5,1},{2,6},{6,2},{3,7},{7,3},{8,12},{12,8},{9,1... | collective-permute-start | bytes 34603016 | tf_op jit(solution)/shard_map/ppermute | solution.py:950
  642.0 250.0 %reduce-scatter.21.cloned.1.call-start = ((), (), s32[]{:S(2)}) async-start(), calls=%async_computation.9 | async-start | bytes 14417920
  642.5 279.4 %reduce-scatter.27.cloned.1.call-start = ((), (), s32[]{:S(2)}) async-start(), calls=%async_computation.12 | async-start | bytes 5242880
  734.9 24.7 %collective-permute-start.9 = (bf16[4,4,512,256]{3,2,1,0:T(8,128)(2,1)}, bf16[4,4,512,256]{3,2,1,0:T(8,128)(2,1)}, u32[]{:S(2)}, u32[]{:S(2)}) collective-permute-start(bf16[4,4,512,256]{3,2,1,0:T(8,128)(2,1)} %by_cols.6), channel_id=1, source_target_pairs={{0,4},{4,0},{1,5},{5,1},{2,6},{6,2},{3,7},{7,3},{8,12},{12,8},{9,1... | collective-permute-start | bytes 12582920 | tf_op jit(solution)/shard_map/ppermute | solution.py:950
  738.4 21.1 %collective-permute-start.10 = (bf16[1408,256]{1,0:T(8,128)(2,1)}, bf16[1408,256]{1,0:T(8,128)(2,1)S(1)}, u32[]{:S(2)}, u32[]{:S(2)}) collective-permute-start(bf16[1408,256]{1,0:T(8,128)(2,1)} %get-tuple-element.206), channel_id=1, source_target_pairs={{0,1},{1,2},{2,3},{3,0},{4,5},{5,6},{6,7},{7,4},{8,9},{9,10},{10,1... | collective-permute-start | bytes 2162696 | tf_op jit(solution)/shard_map/ppermute | solution.py:966
  738.4 70.6 %collective-permute-start.11 = (bf16[1408,256]{1,0:T(8,128)(2,1)}, bf16[1408,256]{1,0:T(8,128)(2,1)S(1)}, u32[]{:S(2)}, u32[]{:S(2)}) collective-permute-start(bf16[1408,256]{1,0:T(8,128)(2,1)} %get-tuple-element.205), channel_id=1, source_target_pairs={{0,2},{1,3},{2,0},{3,1},{4,6},{5,7},{6,4},{7,5},{8,10},{9,11},{10,... | collective-permute-start | bytes 2162696 | tf_op jit(solution)/shard_map/ppermute | solution.py:966
  738.4 94.1 %collective-permute-start.12 = (bf16[1408,256]{1,0:T(8,128)(2,1)S(1)}, bf16[1408,256]{1,0:T(8,128)(2,1)S(1)}, u32[]{:S(2)}, u32[]{:S(2)}) collective-permute-start(bf16[1408,256]{1,0:T(8,128)(2,1)S(1)} %get-tuple-element.204), channel_id=1, source_target_pairs={{0,3},{1,0},{2,1},{3,2},{4,7},{5,4},{6,5},{7,6},{8,11},{9,8},{10,9... | collective-permute-start | bytes 2162696 | tf_op jit(solution)/shard_map/ppermute | solution.py:966
  851.7 230.9 %reduce-scatter.25.cloned.1.call-start = ((), (), s32[]{:S(2)}) async-start(), calls=%async_computation.11 | async-start | bytes 15728640
  891.8 251.7 %reduce-scatter.17.cloned.1.call-start = ((), (), s32[]{:S(2)}) async-start(), calls=%async_computation.7 | async-start | bytes 3932160 | tf_op jit(solution)/shard_map/reduce_scatter | solution.py:974
  894.9 65.0 %collective-permute-start.14 = (bf16[256,1408]{1,0:T(8,128)(2,1)}, bf16[256,1408]{1,0:T(8,128)(2,1)S(1)}, u32[]{:S(2)}, u32[]{:S(2)}) collective-permute-start(bf16[256,1408]{1,0:T(8,128)(2,1)} %get-tuple-element.203), channel_id=1, source_target_pairs={{0,1},{1,2},{2,3},{3,0},{4,5},{5,6},{6,7},{7,4},{8,9},{9,10},{10,1... | collective-permute-start | bytes 2162696 | tf_op jit(solution)/shard_map/ppermute | solution.py:966
  897.5 64.6 %collective-permute-start.15 = (bf16[256,1408]{1,0:T(8,128)(2,1)}, bf16[256,1408]{1,0:T(8,128)(2,1)}, u32[]{:S(2)}, u32[]{:S(2)}) collective-permute-start(bf16[256,1408]{1,0:T(8,128)(2,1)} %get-tuple-element.202), channel_id=1, source_target_pairs={{0,2},{1,3},{2,0},{3,1},{4,6},{5,7},{6,4},{7,5},{8,10},{9,11},{10,... | collective-permute-start | bytes 2162696 | tf_op jit(solution)/shard_map/ppermute | solution.py:966
  899.9 63.7 %collective-permute-start.16 = (bf16[256,1408]{1,0:T(8,128)(2,1)}, bf16[256,1408]{1,0:T(8,128)(2,1)}, u32[]{:S(2)}, u32[]{:S(2)}) collective-permute-start(bf16[256,1408]{1,0:T(8,128)(2,1)} %get-tuple-element.201), channel_id=1, source_target_pairs={{0,3},{1,0},{2,1},{3,2},{4,7},{5,4},{6,5},{7,6},{8,11},{9,8},{10,9... | collective-permute-start | bytes 2162696 | tf_op jit(solution)/shard_map/ppermute | solution.py:966
  902.9 122.5 %collective-permute-start.17 = (bf16[256,1408]{1,0:T(8,128)(2,1)}, bf16[256,1408]{1,0:T(8,128)(2,1)}, u32[]{:S(2)}, u32[]{:S(2)}) collective-permute-start(bf16[256,1408]{1,0:T(8,128)(2,1)} %get-tuple-element.200), channel_id=1, source_target_pairs={{0,1},{1,2},{2,3},{3,0},{4,5},{5,6},{6,7},{7,4},{8,9},{9,10},{10,1... | collective-permute-start | bytes 2162696 | tf_op jit(solution)/shard_map/ppermute | solution.py:966
  923.8 158.9 %collective-permute-start.20 = (bf16[512,256]{1,0:T(8,128)(2,1)}, bf16[512,256]{1,0:T(8,128)(2,1)}, u32[]{:S(2)}, u32[]{:S(2)}) collective-permute-start(bf16[512,256]{1,0:T(8,128)(2,1)} %get-tuple-element.212), channel_id=1, source_target_pairs={{0,1},{1,2},{2,3},{3,0},{4,5},{5,6},{6,7},{7,4},{8,9},{9,10},{10,1... | collective-permute-start | bytes 786440 | tf_op jit(solution)/shard_map/ppermute | solution.py:966
  959.9 122.8 %collective-permute-start.21 = (bf16[512,256]{1,0:T(8,128)(2,1)S(1)}, bf16[512,256]{1,0:T(8,128)(2,1)}, u32[]{:S(2)}, u32[]{:S(2)}) collective-permute-start(bf16[512,256]{1,0:T(8,128)(2,1)S(1)} %get-tuple-element.211), channel_id=1, source_target_pairs={{0,2},{1,3},{2,0},{3,1},{4,6},{5,7},{6,4},{7,5},{8,10},{9,11},{10,... | collective-permute-start | bytes 786440 | tf_op jit(solution)/shard_map/ppermute | solution.py:966
  962.1 120.6 %collective-permute-start.22 = (bf16[512,256]{1,0:T(8,128)(2,1)S(1)}, bf16[512,256]{1,0:T(8,128)(2,1)}, u32[]{:S(2)}, u32[]{:S(2)}) collective-permute-start(bf16[512,256]{1,0:T(8,128)(2,1)S(1)} %get-tuple-element.210), channel_id=1, source_target_pairs={{0,3},{1,0},{2,1},{3,2},{4,7},{5,4},{6,5},{7,6},{8,11},{9,8},{10,9... | collective-permute-start | bytes 786440 | tf_op jit(solution)/shard_map/ppermute | solution.py:966
  963.6 81.7 %collective-permute-start.18 = (bf16[256,1408]{1,0:T(8,128)(2,1)}, bf16[256,1408]{1,0:T(8,128)(2,1)}, u32[]{:S(2)}, u32[]{:S(2)}) collective-permute-start(bf16[256,1408]{1,0:T(8,128)(2,1)} %get-tuple-element.199), channel_id=1, source_target_pairs={{0,2},{1,3},{2,0},{3,1},{4,6},{5,7},{6,4},{7,5},{8,10},{9,11},{10,... | collective-permute-start | bytes 2162696 | tf_op jit(solution)/shard_map/ppermute | solution.py:966
  1025.4 57.3 %collective-permute-start.19 = (bf16[256,1408]{1,0:T(8,128)(2,1)}, bf16[256,1408]{1,0:T(8,128)(2,1)}, u32[]{:S(2)}, u32[]{:S(2)}) collective-permute-start(bf16[256,1408]{1,0:T(8,128)(2,1)} %get-tuple-element.198), channel_id=1, source_target_pairs={{0,3},{1,0},{2,1},{3,2},{4,7},{5,4},{6,5},{7,6},{8,11},{9,8},{10,9... | collective-permute-start | bytes 2162696 | tf_op jit(solution)/shard_map/ppermute | solution.py:966
  (22 other events, 1378.7 us)
Sparse Core Ops, SparseCore 0:
  293.3 147.8 all-gather.2
  1082.9 60.5 reduce-scatter.16
Sparse Core Ops, SparseCore 1:
  525.9 109.1 reduce-scatter.18
  642.0 109.3 reduce-scatter.22
  754.4 112.0 reduce-scatter.20
  869.4 52.5 reduce-scatter.26
  925.4 120.6 reduce-scatter.24

commit v4 on v3

--- a/solution.py
+++ b/solution.py
@@ -13,7 +13,6 @@
 F32 = jnp.float32
 BF16 = jnp.bfloat16
 MESH = pl.DeviceIdType.MESH
-SPLITS = (False, False, False, False, False)
 
 
 def params(**kw):
@@ -213,7 +212,7 @@
     own = lambda k: pltpu.make_async_copy(held[k], outs[k].at[way], own_sem.at[k])
     for k in range(n):
         load(k).start()
-    for i in range(len(steps) + 2):
+    for i in range(len(steps) + 4):
         if i < len(steps):
             k, hop = steps[i]
             if hop == 1:
@@ -222,10 +221,10 @@
                 if k + 1 < n:
                     start_own(k + 1)
             stage1(k, hop)
-        if 0 <= i - 1 < len(steps):
-            stage2(*steps[i - 1])
         if 0 <= i - 2 < len(steps):
-            stage3(*steps[i - 2])
+            stage2(*steps[i - 2])
+        if 0 <= i - 4 < len(steps):
+            stage3(*steps[i - 4])
     for k in range(n):
         own(k).wait()
 
@@ -262,25 +261,31 @@
     )(*shards)
 
 
-def proj_kernel(x_ref, w_ref, o_ref):
-    o_ref[0] = nn(x_ref[...], w_ref[0])
-
-
-def project(normed, w3, chans):
+def proj_kernel(x_ref, in_ref, forget_ref, gate_ref, o_ref):
+    for j, w_ref in enumerate((in_ref, forget_ref, gate_ref)):
+
+        @pl.when(pl.program_id(1) == j)
+        def _(w_ref=w_ref):
+            o_ref[0] = nn(x_ref[...], w_ref[0])
+
+
+def project(normed, w_in, w_forget, w_gate):
     rows, width = normed.shape
-    ways, _, wide = w3.shape
+    ways, _, chans = w_in.shape
+
+    def weights(k):
+        following = lambda t, j: jnp.where(j > k, jnp.minimum(t + 1, ways - 1), t)
+        return pl.BlockSpec((1, width, chans), lambda t, j: (following(t, j), 0, 0))
+
     return pl.pallas_call(
         proj_kernel,
-        grid=(ways, wide // chans),
-        in_specs=[
-            whole((rows, width)),
-            pl.BlockSpec((1, width, chans), lambda t, j: (t, 0, j)),
-        ],
+        grid=(ways, 3),
+        in_specs=[whole((rows, width)), weights(0), weights(1), weights(2)],
         out_specs=pl.BlockSpec((1, rows, chans), lambda t, j: (t, 0, j)),
-        out_shape=jax.ShapeDtypeStruct((ways, rows, wide), F32),
+        out_shape=jax.ShapeDtypeStruct((ways, rows, 3 * chans), F32),
         compiler_params=params(),
         name="project",
-    )(normed, w3)
+    )(normed, w_in, w_forget, w_gate)
 
 
 def gates(p_in, p_forget, lower, ids, starts):
@@ -731,7 +736,7 @@
         o_ref[...] += acc
 
 
-def back(grads, weights, picks, units):
+def back(grads, weights, units):
     ways, rows, _ = grads[0].shape
     width = weights[0].shape[1]
     part = min(width, 1024)
@@ -739,7 +744,7 @@
         functools.partial(back_kernel, len(grads)),
         grid=(width // part, ways),
         in_specs=[pl.BlockSpec((1, rows, units), lambda j, t: (t, 0, 0)) for _ in grads]
-        + [pl.BlockSpec((1, part, units), functools.partial(lambda k, j, t: (t, j, k), k)) for k in picks],
+        + [pl.BlockSpec((1, part, units), lambda j, t: (t, j, 0)) for _ in weights],
         out_specs=pl.BlockSpec((rows, part), lambda j, t: (0, j)),
         out_shape=jax.ShapeDtypeStruct((rows, width), F32),
         compiler_params=params(),
@@ -770,84 +775,58 @@
     return jnp.concatenate(picks, axis=1)
 
 
-def put(outs, adds, j, at, wide, value):
-    if len(outs[0].shape) == 4 and len(outs) == 1:
-        if adds:
-            value = value + adds[0][j, 0, :, at : at + wide].astype(F32)
-        outs[0][j, 0, :, at : at + wide] = value.astype(BF16)
-        return
-    half = value.shape[0] // 2
-    far_y, far_x = j // 2, j % 2
-    spots = ((0 if far_y else 1, far_x), (2 if far_x else 3, far_y))
-    for part, (which, row) in enumerate(spots):
-        got = value[part * half : (part + 1) * half]
-        if adds:
-            got = got + adds[0][which, row, 0, :, at : at + wide].astype(F32)
-        got = got.astype(BF16)
-        if len(outs) == 1:
-            outs[0][which, row, 0, :, at : at + wide] = got
-        else:
-            outs[which][row, 0, :, at : at + wide] = got
-
-
-def by_rows_kernel(chips, n, each, n_out, at_ref, left_ref, *refs):
-    rights, adds, outs = refs[:n], refs[n : len(refs) - n_out], refs[len(refs) - n_out :]
+def put(o_ref, adds, j, at, wide, value):
+    if adds:
+        value = value + adds[0][j, 0, :, at : at + wide].astype(F32)
+    o_ref[j, 0, :, at : at + wide] = value.astype(BF16)
+
+
+def by_rows_kernel(chips, n, each, at_ref, left_ref, *refs):
+    rights, adds, o_ref = refs[:n], refs[n:-1], refs[-1]
     left = columns(left_ref, at_ref, chips, each)
     at = 0
     for right_ref in rights:
         wide = right_ref.shape[2]
         acc = tn(left, right_ref[0])
         for j in range(chips):
-            put(outs, adds, j, at, wide, acc[j * each : (j + 1) * each])
+            put(o_ref, adds, j, at, wide, acc[j * each : (j + 1) * each])
         at += wide
 
 
-def by_cols_kernel(chips, each, n_out, at_ref, right_ref, left_ref, *refs):
-    adds, outs = refs[: len(refs) - n_out], refs[len(refs) - n_out :]
+def by_cols_kernel(chips, each, at_ref, right_ref, left_ref, *refs):
+    adds, o_ref = refs[:-1], refs[-1]
     acc = tn(left_ref[0], columns(right_ref, at_ref, chips, each))
     for j in range(chips):
-        put(outs, adds, j, 0, each, acc[:, j * each : (j + 1) * each])
-
-
-def weight_grad(kernel, whole_side, parted, tall, wide, at, adds, chips, split, name):
+        put(o_ref, adds, j, 0, each, acc[:, j * each : (j + 1) * each])
+
+
+def weight_grad(kernel, whole_side, parted, tall, wide, at, adds, chips, name):
     ways, rows, _ = parted[0].shape
-    adds = list(adds or [])
-    if not split:
-        shapes = [(chips, ways, tall, wide)]
-    elif adds:
-        shapes = [(2, ways, tall // 2, wide)] * 4
-    else:
-        shapes = [(4, 2, ways, tall // 2, wide)]
-
-    def block(shape):
-        front = len(shape) - 3
-        return pl.BlockSpec(shape[:front] + (1,) + shape[-2:], lambda t: (0,) * front + (t, 0, 0))
-
-    outs = [block(s) for s in shapes]
-    return pl.pallas_call(
-        functools.partial(kernel, len(shapes)),
+    block = pl.BlockSpec((chips, 1, tall, wide), lambda t: (0, t, 0, 0))
+    return pl.pallas_call(
+        kernel,
         grid=(ways,),
         in_specs=[pl.BlockSpec(memory_space=pltpu.SMEM), whole(whole_side.shape)]
         + [pl.BlockSpec((1, rows, p.shape[2]), lambda t: (t, 0, 0)) for p in parted]
-        + [block(a.shape) for a in adds],
-        out_specs=outs,
-        out_shape=[jax.ShapeDtypeStruct(s, BF16) for s in shapes],
+        + [block for _ in adds],
+        out_specs=block,
+        out_shape=jax.ShapeDtypeStruct((chips, ways, tall, wide), BF16),
         compiler_params=params(),
         name=name,
     )(at, whole_side, *parted, *adds)
 
 
-def by_rows(left, rights, at, adds, chips, split):
+def by_rows(left, rights, at, adds, chips):
     each = left.shape[1] // (2 * chips)
     kernel = functools.partial(by_rows_kernel, chips, len(rights), each)
     wide = sum(r.shape[2] for r in rights)
-    return weight_grad(kernel, left, rights, each, wide, at, adds, chips, split, "by_rows")
-
-
-def by_cols(left, right, at, adds, chips, split):
+    return weight_grad(kernel, left, rights, each, wide, at, adds, chips, "by_rows")
+
+
+def by_cols(left, right, at, adds, chips):
     each = right.shape[1] // (2 * chips)
     kernel = functools.partial(by_cols_kernel, chips, each)
-    return weight_grad(kernel, right, [left], left.shape[2], each, at, adds, chips, split, "by_cols")
+    return weight_grad(kernel, right, [left], left.shape[2], each, at, adds, chips, "by_cols")
 
 
 def norm_pullback(upstream_gradient, unit_rows, inverse_rms, gain_vector):
@@ -858,8 +837,6 @@
 
 
 SWAP = ((0, 1), (1, 0))
-OVER_X = ((0, 1), (1, 0), (2, 3), (3, 2))
-OVER_Y = ((0, 2), (2, 0), (1, 3), (3, 1))
 
 
 def behind(value, *done):
@@ -920,15 +897,16 @@
     inverse1 = lax.rsqrt(jnp.mean(x * x, axis=1, keepdims=True) + EPS)
     normed = (x * inverse1 * first_norm_gain).astype(BF16)
 
-    shards = [jnp.concatenate([w_in, w_forget, w_gate], axis=1), w_out, w_glu, w_up]
+    shards = [w_in, w_forget, w_gate, w_glu, w_up, w_out]
     if square:
-        w3, w_out_all, w_glu_all, w_up_all = gather_weights(shards, ways)
-        w_down_all = gather(behind(w_down, w_out_all))
+        all_shards = gather_weights(shards, ways)
+        w_down_all = gather(behind(w_down, all_shards[5]))
     else:
-        w3, w_out_all, w_glu_all, w_up_all = [gather(w) for w in shards]
+        all_shards = [gather(w) for w in shards]
         w_down_all = gather(w_down)
-
-    p = project(normed, w3, chans)
+    w_three, (w_glu_all, w_up_all, w_out_all) = all_shards[:3], all_shards[3:]
+
+    p = project(normed, *w_three)
     totals = forward_total(p, lower, starts)
     all_totals = from_all(totals, "tensor")
     enter = jnp.zeros((ways, 1, chans), F32)
@@ -943,18 +921,14 @@
 
     places = jnp.arange(chips, dtype=jnp.int32)
 
-    def blocks_of(c, split):
-        return (jnp.bitwise_xor(places, chip) if split else places) * 2 + c
-
-    def swap(arrays):
-        return [lax.ppermute(a, "core", SWAP) for a in arrays]
-
-    def add(a, b):
-        return a.astype(F32) + b.astype(F32)
+    ours_at, theirs_at = places * 2 + core, places * 2 + (1 - core)
+
+    def swap(array):
+        return lax.ppermute(array, "core", SWAP)
 
     class Scatter:
-        def begin(self, arrays):
-            part = lax.psum_scatter(arrays[0], "chip", scatter_dimension=0, tiled=True)
+        def begin(self, array):
+            part = lax.psum_scatter(array, "chip", scatter_dimension=0, tiled=True)
             self.part = lax.optimization_barrier(part.reshape(part.shape[1:]))
             self.parts = [self.block(0)]
 
@@ -984,19 +958,14 @@
         last[0] = tuple(jax.tree.leaves(out))
         return out
 
-    ours_at = {s: blocks_of(core, s) for s in (True, False)}
-    theirs_at = {s: blocks_of(1 - core, s) for s in (True, False)}
-
-    def rows_grad(split, at, rights, left, adds=None):
+    def rows_grad(at, rights, left, *adds):
         n = len(rights)
-        got = lambda left, *more: by_rows(left, more[:n], at[split], more[n:], chips, split)
-        return run(got, left, *rights, *(adds or []))
-
-    def cols_grad(split, at, left, right, adds=None):
-        got = lambda left, right, *more: by_cols(left, right, at[split], more, chips, split)
-        return run(got, left, right, *(adds or []))
-
-    split_down, split_up, split_glu, split_out, split_three = [square and s for s in SPLITS]
+        got = lambda left, *more: by_rows(left, more[:n], at, more[n:], chips)
+        return run(got, left, *rights, *adds)
+
+    def cols_grad(at, left, right, *adds):
+        return run(lambda left, right, *more: by_cols(left, right, at, more, chips), left, right, *adds)
+
     down, up, glu, out, three = [Scatter() for _ in range(5)]
     gy = cotangent
 
@@ -1008,15 +977,15 @@
 
     few = ways <= 4
 
-    swapped = swap(cols_grad(split_down, theirs_at, hidden, gy))
-    down.begin(cols_grad(split_down, ours_at, hidden, gy, swapped))
+    swapped = swap(cols_grad(theirs_at, hidden, gy))
+    down.begin(cols_grad(ours_at, hidden, gy, swapped))
     g_up, g_glu = run(hidden_grad, gy, w_down_all, act, slope)
-    swapped_up = swap(rows_grad(split_up, theirs_at, [g_up], middle))
-    swapped_glu = swap(rows_grad(split_glu, theirs_at, [g_glu], middle))
-    up.begin(rows_grad(split_up, ours_at, [g_up], middle, swapped_up))
-    glu.begin(rows_grad(split_glu, ours_at, [g_glu], middle, swapped_glu))
+    swapped_up = swap(rows_grad(theirs_at, [g_up], middle))
+    swapped_glu = swap(rows_grad(theirs_at, [g_glu], middle))
+    up.begin(rows_grad(ours_at, [g_up], middle, swapped_up))
+    glu.begin(rows_grad(ours_at, [g_glu], middle, swapped_glu))
     g_middle = run(
-        lambda a, b, c, d: back([a, b], [c, d], [0, 0], units), g_up, g_glu, w_up_all, w_glu_all
+        lambda a, b, c, d: back([a, b], [c, d], units), g_up, g_glu, w_up_all, w_glu_all
     )
     def second_norm(resid, g_middle, gy):
         inverse2 = lax.rsqrt(jnp.mean(resid * resid, axis=1, keepdims=True) + EPS)
@@ -1027,10 +996,10 @@
 
     moving = send(down, 1)
     mlp_gain_part, g_resid, g_branch = run(second_norm, resid, g_middle, gy)
-    swapped_out = swap(cols_grad(split_out, theirs_at, mixed, g_branch))
+    swapped_out = swap(cols_grad(theirs_at, mixed, g_branch))
     g_mixed = run(mixed_grad, g_branch, w_out_all)
     beside(moving)
-    out.begin(cols_grad(split_out, ours_at, mixed, g_branch, swapped_out))
+    out.begin(cols_grad(ours_at, mixed, g_branch, swapped_out))
     moving = send(down, 2)
     g_state, g_gate, gain_part, back_totals = run(backward_total, p, state, g_mixed, lower, gain, starts)
     beside(moving)
@@ -1045,17 +1014,17 @@
     beside(moving)
 
     g_three = [g_in, g_forget, g_gate]
-    swapped = swap(rows_grad(split_three, theirs_at, g_three, normed))
-    three.begin(rows_grad(split_three, ours_at, g_three, normed, swapped))
+    swapped = swap(rows_grad(theirs_at, g_three, normed))
+    three.begin(rows_grad(ours_at, g_three, normed, swapped))
     moving = send(up, 1, 2, 3)
     output = run(feed_down, hidden, w_down_all, resid)
     beside(moving)
     moving = send(glu, 1)
     g_normed = run(
-        lambda a, b, c, w: back([a, b, c], [w, w, w], [0, 1, 2], chans), g_in, g_forget, g_gate, w3
+        lambda *a: back(a[:3], a[3:], chans), *g_three, *w_three
     )
     beside(moving)
-    moving = send(glu, 2)
+    moving = send(glu, 2) + send(out, 1, 2, 3)
 
     def first_norm_back(x, g_normed, g_resid):
         x = x.astype(F32)
@@ -1077,11 +1046,12 @@
             jnp.sum(lam_sum, axis=1).reshape(width),
         ]
     )
-    moving += send(out, 1, 2, 3)
-    small = run(lambda v: lax.psum(v, every), small)
     beside(moving)
     three.part = behind(three.part, *last[0])
+    beside((three.part,))
     three.rest()
+    small = run(lambda v: lax.psum(v, every), small)
+    three.parts = [behind(three.parts[0], small)]
     if not few:
         for s in (down, up, glu, out):
             s.rest()

time: 1160 us -> 1110 us (0.957)
  waiting for transfers between devices: 112 us -> 67 us
    reduce_scatter x1, waiting for transfers between devices: 48 us -> 2.2 us  [rest(): lax.psum_scatter(self.part, 'tensor', scatter_dimension=0, tiled=True)]
  transfers between devices with their start and end apart: 30 -> 30, of which waited for: 7 -> 9; matrix products, arithmetic and copies ran while one was open for 6% -> 6% of each run, Pallas kernels for 48% -> 50%
where the time goes in v4:
time: 1110 us; the launch traced here: 1100 us
  Pallas kernels  821 us (74%)
  waiting for transfers between devices  67 us (6%)
  blocking collectives  59.9 us (5%)
  other arithmetic  57.3 us (5%)
  starting transfers between devices  53.8 us (5%)
  local copies, waits for them, and re-layouts  22.6 us (2%)
  between operations  19.6 us (2%)
    pallas_call x1, Pallas kernels, gather_weights(): pl.pallas_call(functools.partial(gather_kernel, n, ways), in_specs=[any_s...  267 us
    pallas_call x10, Pallas kernels, weight_grad(): pl.pallas_call(kernel, grid=(ways,), in_specs=[pl.BlockSpec(memory_space=...  174 us
    pallas_call x2, Pallas kernels, back(): pl.pallas_call(functools.partial(back_kernel, len(grads)), grid=(width //...  101 us
    pallas_call x1, Pallas kernels, feed_up(): pl.pallas_call(up_kernel, grid=(ways, rows // part), in_specs=[pl.BlockSp...  61.3 us
    psum x1, blocking collectives, local(): small = run(lambda v: lax.psum(v, every), small)  45 us
    ppermute x12, starting transfers between devices, send(): lax.ppermute(self.block(k), 'tensor', [(i, (i + k) % ways) for i in range...  44.4 us
    pallas_call x1, Pallas kernels, hidden_grad(): pl.pallas_call(hidden_grad_kernel, grid=(ways, rows // part), in_specs=[p...  37.2 us
    ppermute x5, waiting for transfers between devices, swap(): return lax.ppermute(array, 'core', SWAP)  36.9 us
  transfers between devices with their start and end apart: 30, of which 9 were waited for; matrix products, arithmetic and copies ran while one was open for 6% of the time, Pallas kernels for 50%

profile of v4, /device:TPU:0, one launch (start us, length us, event | category | flops | bytes accessed | tf_op | source)
XLA Modules:
  0.0 1101.3 jit_solution(17433436503542699292)
XLA Ops:
  8.1 267.1 %gather_weights.1 = (bf16[4,2048,512]{2,1,0:T(8,128)(2,1)}, bf16[4,2048,512]{2,1,0:T(8,128)(2,1)}, bf16[4,2048,512]{2,1,0:T(8,128)(2,1)}, bf16[4,2048,1408]{2,1,...) custom-call(bf16[2048,512]{1,0:T(8,128)(2,1)} %refs_0_.1, bf16[2048,512]{1,0:T(8,128)(2,1)} %refs_1_.1, ...), custom_call_target="tpu_custom_call" | custom-call | tf_op jit(solution)/shard_map/gather_weights/pallas_call | solution.py:247
  292.9 34.4 %project.1.p_ref.pf_ref.pg_ref.pi_ref = f32[4,1024,1536]{2,1,0:T(8,128)} custom-call(bf16[1024,2048]{1,0:T(8,128)(2,1)} %fusion.5.x_ref.left_ref, bf16[4,2048,512]{2,1,0:T(8,128)(2,1)} %get-tuple-element.192.in_ref.refs_3_, bf16[4,2048,512]{2,1,0:T(8,128)(2,1)} %get-tuple-element.193.forget_ref.refs_4_, bf16[4,2048,512]{2,1,0:T(8,128)(2,1)} %get-tuple-element.194.gate_ref.refs_5_), custom_call_target="tpu_custom_call" | custom-call | tf_op jit(solution)/shard_map/project/pallas_call | solution.py:280
  354.5 21.6 %forward_scan.1 = (f32[4,1024,512]{2,1,0:T(8,128)}, bf16[4,1024,512]{2,1,0:T(8,128)(2,1)}, f32[4,8,512]{2,1,0:T(8,128)}) custom-call(s32[3]{0:T(128)} %add_subtract_fusion.starts_ref, f32[4,1024,1536]{2,1,0:T(8,128)} %project.1.p_ref.pf_ref.pg_ref.pi_ref, f32[4,1,512]{2,1,0:T(1,128)} %get-tuple-element.171.lower_ref, ...), custom_call_target="tpu_custom_call" | custom-call | tf_op jit(solution)/shard_map/forward_scan/pallas_call | solution.py:398
  376.2 15.9 %branch.1 = (f32[1024,2048]{1,0:T(8,128)}, bf16[1024,2048]{1,0:T(8,128)(2,1)}) custom-call(bf16[4,1024,512]{2,1,0:T(8,128)(2,1)} %get-tuple-element.155.mixed_ref.left_ref, bf16[4,512,2048]{2,1,0:T(8,128)(2,1)} %get-tuple-element.153.w_ref, bf16[1024,2048]{1,0:T(8,128)(2,1)} %x_ref.1, f32[1,2048]{1,0:T(1,128)} %bitcast.143), custom_call_target="tpu_custom_call" | custom-call | tf_op jit(solution)/shard_map/branch/pallas_call | solution.py:623
  392.0 61.3 %feed_up.1 = (bf16[4,1024,1408]{2,1,0:T(8,128)(2,1)}, bf16[4,1024,1408]{2,1,0:T(8,128)(2,1)}, bf16[4,1024,1408]{2,1,0:T(8,128)(2,1)}) custom-call(bf16[1024,2048]{1,0:T(8,128)(2,1)} %get-tuple-element.140.x_ref.left_ref, bf16[4,2048,1408]{2,1,0:T(8,128)(2,1)} %get-tuple-element.145.up_ref.refs_2_, bf16[4,2048,1408]{2,1,0:T(8,128)(2,1)} %get-tuple-element.146.glu_ref.refs_3_), custom_call_target="tpu_custom_call" | custom-call | tf_op jit(solution)/shard_map/feed_up/pallas_call | solution.py:659
  453.3 17.6 %by_cols.4 = bf16[4,4,1408,256]{3,2,1,0:T(8,128)(2,1)} custom-call(s32[4]{0:T(128)} %fusion.24.at_ref, bf16[1024,2048]{1,0:T(8,128)(2,1)} %dy_ref, bf16[4,1024,1408]{2,1,0:T(8,128)(2,1)} %get-tuple-element.186.left_ref.h_ref), custom_call_target="tpu_custom_call" | custom-call | tf_op jit(solution)/shard_map/by_cols/pallas_call | solution.py:806
  471.4 17.5 %collective-permute-done.6.refs_0_ = bf16[4,4,1408,256]{3,2,1,0:T(8,128)(2,1)} collective-permute-done((bf16[4,4,1408,256]{3,2,1,0:T(8,128)(2,1)}, bf16[4,4,1408,256]{3,2,1,0:T(8,128)(2,1)}, u32[]{:S(2)}, u32[]{:S(2)}) %collective-permute-start.6) | collective-permute-done | bytes 11534368 | tf_op jit(solution)/shard_map/ppermute | solution.py:927
  488.9 19.0 %by_cols.5 = bf16[4,4,1408,256]{3,2,1,0:T(8,128)(2,1)} custom-call(s32[4]{0:T(128)} %fusion.25.at_ref, bf16[1024,2048]{1,0:T(8,128)(2,1)} %dy_ref, bf16[4,1024,1408]{2,1,0:T(8,128)(2,1)} %get-tuple-element.186.left_ref.h_ref, bf16[4,4,1408,256]{3,2,1,0:T(8,128)(2,1)} %collective-permute-done.6.refs_0_), custom_call_target="tpu_custom_call" | custom-call | tf_op jit(solution)/shard_map/by_cols/pallas_call | solution.py:806
  508.4 37.2 %hidden_grad.1 = (bf16[4,1024,1408]{2,1,0:T(8,128)(2,1)}, bf16[4,1024,1408]{2,1,0:T(8,128)(2,1)}) custom-call(bf16[1024,2048]{1,0:T(8,128)(2,1)} %dy_ref, bf16[4,1408,2048]{2,1,0:T(8,128)(2,1)} %bitcast.131, bf16[4,1024,1408]{2,1,0:T(8,128)(2,1)} %get-tuple-element.129.act_ref, bf16[4,1024,1408]{2,1,0:T(8,128)(2,1)} %get-tuple-element.130.slope_ref), custom_call_target="tpu_custom_call" | custom-call | tf_op jit(solution)/shard_map/hidden_grad/pallas_call | solution.py:707
  545.6 19.0 %by_rows.6 = bf16[4,4,256,1408]{3,2,1,0:T(8,128)(2,1)} custom-call(s32[4]{0:T(128)} %fusion.24.at_ref, bf16[1024,2048]{1,0:T(8,128)(2,1)} %get-tuple-element.140.x_ref.left_ref, bf16[4,1024,1408]{2,1,0:T(8,128)(2,1)} %get-tuple-element.143.refs_0_), custom_call_target="tpu_custom_call" | custom-call | tf_op jit(solution)/shard_map/by_rows/pallas_call | solution.py:806
  564.6 19.0 %by_rows.7 = bf16[4,4,256,1408]{3,2,1,0:T(8,128)(2,1)} custom-call(s32[4]{0:T(128)} %fusion.24.at_ref, bf16[1024,2048]{1,0:T(8,128)(2,1)} %get-tuple-element.140.x_ref.left_ref, bf16[4,1024,1408]{2,1,0:T(8,128)(2,1)} %get-tuple-element.144.refs_0_.refs_1_), custom_call_target="tpu_custom_call" | custom-call | tf_op jit(solution)/shard_map/by_rows/pallas_call | solution.py:806
  584.0 20.0 %by_rows.8 = bf16[4,4,256,1408]{3,2,1,0:T(8,128)(2,1)} custom-call(s32[4]{0:T(128)} %fusion.25.at_ref, bf16[1024,2048]{1,0:T(8,128)(2,1)} %get-tuple-element.140.x_ref.left_ref, bf16[4,1024,1408]{2,1,0:T(8,128)(2,1)} %get-tuple-element.143.refs_0_, bf16[4,4,256,1408]{3,2,1,0:T(8,128)(2,1)} %collective-permute-done.8.refs_1_), custom_call_target="tpu_custom_call" | custom-call | tf_op jit(solution)/shard_map/by_rows/pallas_call | solution.py:806
  604.0 20.1 %by_rows.9 = bf16[4,4,256,1408]{3,2,1,0:T(8,128)(2,1)} custom-call(s32[4]{0:T(128)} %fusion.25.at_ref, bf16[1024,2048]{1,0:T(8,128)(2,1)} %get-tuple-element.140.x_ref.left_ref, bf16[4,1024,1408]{2,1,0:T(8,128)(2,1)} %get-tuple-element.144.refs_0_.refs_1_, bf16[4,4,256,1408]{3,2,1,0:T(8,128)(2,1)} %collective-permute-done.7.refs_1_), custom_call_target="tpu_custom_call" | custom-call | tf_op jit(solution)/shard_map/by_rows/pallas_call | solution.py:806
  624.8 63.8 %back.2 = f32[1024,2048]{1,0:T(8,128)} custom-call(bf16[4,1024,1408]{2,1,0:T(8,128)(2,1)} %get-tuple-element.143.refs_0_, bf16[4,1024,1408]{2,1,0:T(8,128)(2,1)} %get-tuple-element.144.refs_0_.refs_1_, bf16[4,2048,1408]{2,1,0:T(8,128)(2,1)} %get-tuple-element.145.up_ref.refs_2_, bf16[4,2048,1408]{2,1,0:T(8,128)(2,1)} %get-tuple-element.146.glu_ref.refs_3_), custom_call_target="tpu_custom_call" | custom-call | tf_op jit(solution)/shard_map/back/pallas_call | solution.py:743
  751.7 23.2 %backward_total.1 = (f32[4,1024,512]{2,1,0:T(8,128)}, bf16[4,1024,512]{2,1,0:T(8,128)(2,1)}, f32[4,8,512]{2,1,0:T(8,128)}, f32[4,1,512]{2,1,0:T(1,128)}) custom-call(s32[3]{0:T(128)} %add_subtract_fusion.starts_ref, f32[4,1024,1536]{2,1,0:T(8,128)} %project.1.p_ref.pf_ref.pg_ref.pi_ref, f32[4,1024,1536]{2,1,0:T(8,128)} %project.1.p_ref.pf_ref.pg_ref.pi_ref, ...), custom_call_target="tpu_custom_call" | custom-call | tf_op jit(solution)/shard_map/backward_total/pallas_call | solution.py:486
  791.2 23.4 %backward_scan.1 = (bf16[4,1024,512]{2,1,0:T(8,128)(2,1)}, bf16[4,1024,512]{2,1,0:T(8,128)(2,1)}, f32[4,8,512]{2,1,0:T(8,128)}) custom-call(s32[3]{0:T(128)} %add_subtract_fusion.starts_ref, f32[4,1024,1536]{2,1,0:T(8,128)} %project.1.p_ref.pf_ref.pg_ref.pi_ref, f32[4,1024,1536]{2,1,0:T(8,128)} %project.1.p_ref.pf_ref.pg_ref.pi_ref, ...), custom_call_target="tpu_custom_call" | custom-call | tf_op jit(solution)/shard_map/backward_scan/pallas_call | solution.py:580
  814.6 19.3 %by_rows.10 = bf16[4,4,256,1536]{3,2,1,0:T(8,128)(2,1)} custom-call(s32[4]{0:T(128)} %fusion.24.at_ref, bf16[1024,2048]{1,0:T(8,128)(2,1)} %fusion.5.x_ref.left_ref, bf16[4,1024,512]{2,1,0:T(8,128)(2,1)} %get-tuple-element.189.refs_0_, bf16[4,1024,512]{2,1,0:T(8,128)(2,1)} %get-tuple-element.190.refs_1_, bf16[4,1024,512]{2,1,0:T(8,128)(2,1)} %get-tuple-element.191.refs_2_), custom_call_target="tpu_custom_call" | custom-call | tf_op jit(solution)/shard_map/by_rows/pallas_call | solution.py:806
  834.0 19.4 %collective-permute-done.13.refs_3_ = bf16[4,4,256,1536]{3,2,1,0:T(8,128)(2,1)} collective-permute-done((bf16[4,4,256,1536]{3,2,1,0:T(8,128)(2,1)}, bf16[4,4,256,1536]{3,2,1,0:T(8,128)(2,1)}, u32[]{:S(2)}, u32[]{:S(2)}) %collective-permute-start.13) | collective-permute-done | bytes 12582944 | tf_op jit(solution)/shard_map/ppermute | solution.py:927
  853.4 20.6 %by_rows.11 = bf16[4,4,256,1536]{3,2,1,0:T(8,128)(2,1)} custom-call(s32[4]{0:T(128)} %fusion.25.at_ref, bf16[1024,2048]{1,0:T(8,128)(2,1)} %fusion.5.x_ref.left_ref, bf16[4,1024,512]{2,1,0:T(8,128)(2,1)} %get-tuple-element.189.refs_0_, bf16[4,1024,512]{2,1,0:T(8,128)(2,1)} %get-tuple-element.190.refs_1_, bf16[4,1024,512]{2,1,0:T(8,128)(2,1)} %get-tuple-element.191.refs_2_, ...), custom_call_target="tpu_custom_call" | custom-call | tf_op jit(solution)/shard_map/by_rows/pallas_call | solution.py:806
  887.0 17.3 %reduce-scatter.25.cloned.1.call-done = bf16[1,4,512,256]{3,2,1,0:T(8,128)(2,1)} async-done(((bf16[4,4,512,256]{3,2,1,0:T(8,128)(2,1)}), bf16[1,4,512,256]{3,2,1,0:T(8,128)(2,1)}) %reduce-scatter.25.cloned.1.call-update) | async-done | bytes 1048592
  907.7 34.6 %feed_down.1 = bf16[1024,2048]{1,0:T(8,128)(2,1)} custom-call(bf16[4,1024,1408]{2,1,0:T(8,128)(2,1)} %get-tuple-element.186.left_ref.h_ref, bf16[4,1408,2048]{2,1,0:T(8,128)(2,1)} %bitcast.132, f32[1024,2048]{1,0:T(8,128)} %get-tuple-element.188.resid_ref), custom_call_target="tpu_custom_call" | custom-call | tf_op jit(solution)/shard_map/feed_down/pallas_call | solution.py:681
  946.0 24.8 %collective-permute-start.18 = (bf16[256,1408]{1,0:T(8,128)(2,1)}, bf16[256,1408]{1,0:T(8,128)(2,1)}, u32[]{:S(2)}, u32[]{:S(2)}) collective-permute-start(bf16[256,1408]{1,0:T(8,128)(2,1)} %get-tuple-element.209), channel_id=1, source_target_pairs={{0,2},{1,3},{2,0},{3,1},{4,6},{5,7},{6,4},{7,5},{8,10},{9,11},{10,... | collective-permute-start | bytes 2162696 | tf_op jit(solution)/shard_map/ppermute | solution.py:940
  970.8 36.8 %back.3 = f32[1024,2048]{1,0:T(8,128)} custom-call(bf16[4,1024,512]{2,1,0:T(8,128)(2,1)} %get-tuple-element.189.refs_0_, bf16[4,1024,512]{2,1,0:T(8,128)(2,1)} %get-tuple-element.190.refs_1_, bf16[4,1024,512]{2,1,0:T(8,128)(2,1)} %get-tuple-element.191.refs_2_, bf16[4,2048,512]{2,1,0:T(8,128)(2,1)} %get-tuple-element.192.in_ref.refs_3_, ...), custom_call_target="tpu_custom_call" | custom-call | tf_op jit(solution)/shard_map/back/pallas_call | solution.py:743
  1040.8 45.0 %psum.7 = f32[5,2048]{1,0:T(8,128)S(1)} all-reduce(f32[5,2048]{1,0:T(8,128)S(1)} %stack.79), channel_id=1, replica_groups=mesh['chip'=4,'core'=2,'tensor'=4] {'tensor','chip','core'}, use_global_device_ids=true, to_apply=%region_15.16 | all-reduce | flops 10240 | bytes 81920 | tf_op jit(solution)/shard_map/psum | solution.py:1053
  (154 shorter events, 183.8 us)
Async XLA Ops:
  8.0 500.4 %all-gather.3.cloned.1.call-start = ((), (), s32[]{:S(2)}) async-start(), calls=%async_computation.6 | async-start | bytes 23789568 | tf_op jit(solution)/shard_map/all_gather | solution.py:889
  277.3 439.9 %reduce-scatter.19.cloned.1.call-start = ((), (), s32[]{:S(2)}) async-start(), calls=%async_computation.8 | async-start | bytes 14417920
  277.4 49.9 %collective-permute-start = (f32[2,512]{1,0:T(2,128)S(1)}, f32[2,512]{1,0:T(2,128)S(1)}, u32[]{:S(2)}, u32[]{:S(2)}) collective-permute-start(f32[2,512]{1,0:T(2,128)S(1)} %pad_maximum_fusion), channel_id=1, source_target_pairs={{1,0},{2,1},{3,2},{0,3},{5,4},{6,5},{7,6},{4,7},{9,8},{10,9},{11,1... | collective-permute-start | bytes 12296 | tf_op jit(solution)/shard_map/ppermute | solution.py:853
  280.0 47.3 %collective-permute-start.1 = (f32[2,512]{1,0:T(2,128)S(1)}, f32[2,512]{1,0:T(2,128)S(1)}, u32[]{:S(2)}, u32[]{:S(2)}) collective-permute-start(f32[2,512]{1,0:T(2,128)S(1)} %pad_maximum_fusion), channel_id=1, source_target_pairs={{2,0},{3,1},{0,2},{1,3},{6,4},{7,5},{4,6},{5,7},{10,8},{11,9},{8,1... | collective-permute-start | bytes 12296 | tf_op jit(solution)/shard_map/ppermute | solution.py:853
  280.0 47.4 %collective-permute-start.2 = (f32[2,512]{1,0:T(2,128)S(1)}, f32[2,512]{1,0:T(2,128)S(1)}, u32[]{:S(2)}, u32[]{:S(2)}) collective-permute-start(f32[2,512]{1,0:T(2,128)S(1)} %pad_maximum_fusion), channel_id=1, source_target_pairs={{3,0},{0,1},{1,2},{2,3},{7,4},{4,5},{5,6},{6,7},{11,8},{8,9},{9,10... | collective-permute-start | bytes 12296 | tf_op jit(solution)/shard_map/ppermute | solution.py:853
  507.9 366.1 %reduce-scatter.23.cloned.1.call-start = ((), (), s32[]{:S(2)}) async-start(), calls=%async_computation.10 | async-start | bytes 14417920
  583.6 20.4 %collective-permute-start.7 = (bf16[4,4,256,1408]{3,2,1,0:T(8,128)(2,1)}, bf16[4,4,256,1408]{3,2,1,0:T(8,128)(2,1)}, u32[]{:S(2)}, u32[]{:S(2)}) collective-permute-start(bf16[4,4,256,1408]{3,2,1,0:T(8,128)(2,1)} %by_rows.7), channel_id=1, source_target_pairs={{0,4},{4,0},{1,5},{5,1},{2,6},{6,2},{3,7},{7,3},{8,12},{12,8},{9,1... | collective-permute-start | bytes 34603016 | tf_op jit(solution)/shard_map/ppermute | solution.py:927
  624.2 249.9 %reduce-scatter.21.cloned.1.call-start = ((), (), s32[]{:S(2)}) async-start(), calls=%async_computation.9 | async-start | bytes 14417920
  624.8 279.6 %reduce-scatter.25.cloned.1.call-start = ((), (), s32[]{:S(2)}) async-start(), calls=%async_computation.11 | async-start | bytes 5242880
  716.8 24.4 %collective-permute-start.9 = (bf16[4,4,512,256]{3,2,1,0:T(8,128)(2,1)}, bf16[4,4,512,256]{3,2,1,0:T(8,128)(2,1)}, u32[]{:S(2)}, u32[]{:S(2)}) collective-permute-start(bf16[4,4,512,256]{3,2,1,0:T(8,128)(2,1)} %by_cols.6), channel_id=1, source_target_pairs={{0,4},{4,0},{1,5},{5,1},{2,6},{6,2},{3,7},{7,3},{8,12},{12,8},{9,1... | collective-permute-start | bytes 12582920 | tf_op jit(solution)/shard_map/ppermute | solution.py:927
  720.1 21.1 %collective-permute-start.10 = (bf16[1408,256]{1,0:T(8,128)(2,1)}, bf16[1408,256]{1,0:T(8,128)(2,1)S(1)}, u32[]{:S(2)}, u32[]{:S(2)}) collective-permute-start(bf16[1408,256]{1,0:T(8,128)(2,1)} %get-tuple-element.216), channel_id=1, source_target_pairs={{0,1},{1,2},{2,3},{3,0},{4,5},{5,6},{6,7},{7,4},{8,9},{9,10},{10,1... | collective-permute-start | bytes 2162696 | tf_op jit(solution)/shard_map/ppermute | solution.py:940
  720.1 71.1 %collective-permute-start.11 = (bf16[1408,256]{1,0:T(8,128)(2,1)}, bf16[1408,256]{1,0:T(8,128)(2,1)S(1)}, u32[]{:S(2)}, u32[]{:S(2)}) collective-permute-start(bf16[1408,256]{1,0:T(8,128)(2,1)} %get-tuple-element.215), channel_id=1, source_target_pairs={{0,2},{1,3},{2,0},{3,1},{4,6},{5,7},{6,4},{7,5},{8,10},{9,11},{10,... | collective-permute-start | bytes 2162696 | tf_op jit(solution)/shard_map/ppermute | solution.py:940
  720.1 94.5 %collective-permute-start.12 = (bf16[1408,256]{1,0:T(8,128)(2,1)S(1)}, bf16[1408,256]{1,0:T(8,128)(2,1)S(1)}, u32[]{:S(2)}, u32[]{:S(2)}) collective-permute-start(bf16[1408,256]{1,0:T(8,128)(2,1)S(1)} %get-tuple-element.214), channel_id=1, source_target_pairs={{0,3},{1,0},{2,1},{3,2},{4,7},{5,4},{6,5},{7,6},{8,11},{9,8},{10,9... | collective-permute-start | bytes 2162696 | tf_op jit(solution)/shard_map/ppermute | solution.py:940
  833.9 194.5 %reduce-scatter.27.cloned.1.call-start = ((), (), s32[]{:S(2)}) async-start(), calls=%async_computation.12 | async-start | bytes 15728640
  874.0 215.9 %reduce-scatter.17.cloned.1.call-start = ((), (), s32[]{:S(2)}) async-start(), calls=%async_computation.7 | async-start | bytes 3932160 | tf_op jit(solution)/shard_map/reduce_scatter | solution.py:948
  877.0 65.3 %collective-permute-start.14 = (bf16[256,1408]{1,0:T(8,128)(2,1)}, bf16[256,1408]{1,0:T(8,128)(2,1)S(1)}, u32[]{:S(2)}, u32[]{:S(2)}) collective-permute-start(bf16[256,1408]{1,0:T(8,128)(2,1)} %get-tuple-element.213), channel_id=1, source_target_pairs={{0,1},{1,2},{2,3},{3,0},{4,5},{5,6},{6,7},{7,4},{8,9},{9,10},{10,1... | collective-permute-start | bytes 2162696 | tf_op jit(solution)/shard_map/ppermute | solution.py:940
  879.7 64.9 %collective-permute-start.15 = (bf16[256,1408]{1,0:T(8,128)(2,1)}, bf16[256,1408]{1,0:T(8,128)(2,1)}, u32[]{:S(2)}, u32[]{:S(2)}) collective-permute-start(bf16[256,1408]{1,0:T(8,128)(2,1)} %get-tuple-element.212), channel_id=1, source_target_pairs={{0,2},{1,3},{2,0},{3,1},{4,6},{5,7},{6,4},{7,5},{8,10},{9,11},{10,... | collective-permute-start | bytes 2162696 | tf_op jit(solution)/shard_map/ppermute | solution.py:940
  882.1 63.9 %collective-permute-start.16 = (bf16[256,1408]{1,0:T(8,128)(2,1)}, bf16[256,1408]{1,0:T(8,128)(2,1)}, u32[]{:S(2)}, u32[]{:S(2)}) collective-permute-start(bf16[256,1408]{1,0:T(8,128)(2,1)} %get-tuple-element.211), channel_id=1, source_target_pairs={{0,3},{1,0},{2,1},{3,2},{4,7},{5,4},{6,5},{7,6},{8,11},{9,8},{10,9... | collective-permute-start | bytes 2162696 | tf_op jit(solution)/shard_map/ppermute | solution.py:940
  885.2 122.4 %collective-permute-start.17 = (bf16[256,1408]{1,0:T(8,128)(2,1)}, bf16[256,1408]{1,0:T(8,128)(2,1)}, u32[]{:S(2)}, u32[]{:S(2)}) collective-permute-start(bf16[256,1408]{1,0:T(8,128)(2,1)} %get-tuple-element.210), channel_id=1, source_target_pairs={{0,1},{1,2},{2,3},{3,0},{4,5},{5,6},{6,7},{7,4},{8,9},{9,10},{10,1... | collective-permute-start | bytes 2162696 | tf_op jit(solution)/shard_map/ppermute | solution.py:940
  906.2 122.2 %collective-permute-start.19 = (bf16[512,256]{1,0:T(8,128)(2,1)}, bf16[512,256]{1,0:T(8,128)(2,1)}, u32[]{:S(2)}, u32[]{:S(2)}) collective-permute-start(bf16[512,256]{1,0:T(8,128)(2,1)} %get-tuple-element.219), channel_id=1, source_target_pairs={{0,1},{1,2},{2,3},{3,0},{4,5},{5,6},{6,7},{7,4},{8,9},{9,10},{10,1... | collective-permute-start | bytes 786440 | tf_op jit(solution)/shard_map/ppermute | solution.py:940
  942.3 86.1 %collective-permute-start.20 = (bf16[512,256]{1,0:T(8,128)(2,1)S(1)}, bf16[512,256]{1,0:T(8,128)(2,1)}, u32[]{:S(2)}, u32[]{:S(2)}) collective-permute-start(bf16[512,256]{1,0:T(8,128)(2,1)S(1)} %get-tuple-element.218), channel_id=1, source_target_pairs={{0,2},{1,3},{2,0},{3,1},{4,6},{5,7},{6,4},{7,5},{8,10},{9,11},{10,... | collective-permute-start | bytes 786440 | tf_op jit(solution)/shard_map/ppermute | solution.py:940
  944.6 83.8 %collective-permute-start.21 = (bf16[512,256]{1,0:T(8,128)(2,1)S(1)}, bf16[512,256]{1,0:T(8,128)(2,1)}, u32[]{:S(2)}, u32[]{:S(2)}) collective-permute-start(bf16[512,256]{1,0:T(8,128)(2,1)S(1)} %get-tuple-element.217), channel_id=1, source_target_pairs={{0,3},{1,0},{2,1},{3,2},{4,7},{5,4},{6,5},{7,6},{8,11},{9,8},{10,9... | collective-permute-start | bytes 786440 | tf_op jit(solution)/shard_map/ppermute | solution.py:940
  946.0 82.4 %collective-permute-start.18 = (bf16[256,1408]{1,0:T(8,128)(2,1)}, bf16[256,1408]{1,0:T(8,128)(2,1)}, u32[]{:S(2)}, u32[]{:S(2)}) collective-permute-start(bf16[256,1408]{1,0:T(8,128)(2,1)} %get-tuple-element.209), channel_id=1, source_target_pairs={{0,2},{1,3},{2,0},{3,1},{4,6},{5,7},{6,4},{7,5},{8,10},{9,11},{10,... | collective-permute-start | bytes 2162696 | tf_op jit(solution)/shard_map/ppermute | solution.py:940
  1007.6 21.1 %collective-permute-start.22 = (bf16[256,1408]{1,0:T(8,128)(2,1)}, bf16[256,1408]{1,0:T(8,128)(2,1)}, u32[]{:S(2)}, u32[]{:S(2)}) collective-permute-start(bf16[256,1408]{1,0:T(8,128)(2,1)} %get-tuple-element.208), channel_id=1, source_target_pairs={{0,3},{1,0},{2,1},{3,2},{4,7},{5,4},{6,5},{7,6},{8,11},{9,8},{10,9... | collective-permute-start | bytes 2162696 | tf_op jit(solution)/shard_map/ppermute | solution.py:940
  (21 other events, 1313.5 us)
Sparse Core Ops, SparseCore 0:
  277.4 144.3 all-gather.2
  1028.8 60.9 reduce-scatter.16
Sparse Core Ops, SparseCore 1:
  508.0 109.3 reduce-scatter.18
  624.3 109.5 reduce-scatter.22
  736.8 112.0 reduce-scatter.20
  851.8 52.5 reduce-scatter.24
  907.8 120.6 reduce-scatter.26

commit v5 on v4

--- a/solution.py
+++ b/solution.py
@@ -44,8 +44,9 @@
 
 
 def gather_kernel(n, ways, *refs):
-    ins, outs, held = refs[:n], refs[n : 2 * n], refs[2 * n : 3 * n]
-    in_sem, own_sem, send_sem, recv_sem = refs[3 * n :]
+    ins, normed_ref, outs, p_ref = refs[:n], refs[n], refs[n + 1 : 2 * n + 1], refs[2 * n + 1]
+    held = refs[2 * n + 2 : 3 * n + 2]
+    w_buf, p_buf, w_sem, p_sem, in_sem, own_sem, send_sem, recv_sem = refs[3 * n + 2 :]
     way = lax.axis_index("tensor")
     chip = lax.axis_index("chip")
     core = lax.axis_index("core")
@@ -193,8 +194,6 @@
             @pl.when(arrives)
             def _():
                 to = plane(k, hop, up)
-                for name in ("c0", "c1", "c2", "c3"):
-                    to[name]().wait_recv()
                 for name in to:
                     to[name]().wait_send()
 
@@ -205,6 +204,44 @@
                     z_next(k, hop, up).wait_send()
 
         both(run)
+
+    def whole_shards(k):
+        own(k).wait()
+
+        def run(hop, up):
+            @pl.when(guard(hop, up)[0])
+            def _():
+                to = plane(k, hop, up)
+                for name in ("c0", "c1", "c2", "c3"):
+                    to[name]().wait_recv()
+
+        for hop in range(1, ways):
+            both(functools.partial(run, hop))
+
+    rows, chans = p_buf.shape[1:]
+    part = min(rows, 256)
+
+    def fetch(m):
+        return pltpu.make_async_copy(outs[m // ways].at[m % ways], w_buf.at[m % 2], w_sem.at[m % 2])
+
+    def put_back(m):
+        place = p_ref.at[m % ways, :, pl.ds((m // ways) * chans, chans)]
+        return pltpu.make_async_copy(p_buf.at[m % 2], place, p_sem.at[m % 2])
+
+    def tile(m):
+        fetch(m).wait()
+        if m >= 2:
+            put_back(m - 2).wait()
+
+        def rows_of(r, carry):
+            at = pl.ds(pl.multiple_of(r * part, part), part)
+            p_buf[m % 2, at, :] = nn(normed_ref[at, :], w_buf[m % 2])
+            return carry
+
+        lax.fori_loop(0, rows // part, rows_of, 0)
+        put_back(m).start()
+        if m + 2 < (m // ways + 1) * ways:
+            fetch(m + 2).start()
 
     steps = [(k, hop) for k in range(n) for hop in range(1, ways)]
     start_own(0)
@@ -212,6 +249,7 @@
     own = lambda k: pltpu.make_async_copy(held[k], outs[k].at[way], own_sem.at[k])
     for k in range(n):
         load(k).start()
+    todo = []
     for i in range(len(steps) + 4):
         if i < len(steps):
             k, hop = steps[i]
@@ -225,8 +263,20 @@
             stage2(*steps[i - 2])
         if 0 <= i - 4 < len(steps):
             stage3(*steps[i - 4])
+        if i >= 4 + ways and (i - 4 - ways) % (ways - 1) == 0 and (i - 4 - ways) // (ways - 1) < 3:
+            j = (i - 4 - ways) // (ways - 1)
+            whole_shards(j)
+            todo += range(j * ways, (j + 1) * ways)
+            for m in todo[-ways:][:2]:
+                fetch(m).start()
+            tile(todo.pop(0))
+        if todo:
+            tile(todo.pop(0))
+    put_back(3 * ways - 2).wait()
+    put_back(3 * ways - 1).wait()
     for k in range(n):
-        own(k).wait()
+        if k >= 3:
+            whole_shards(k)
 
         @pl.when(way < ways - 1)
         def _():
@@ -240,17 +290,24 @@
             finish(k, hop)
 
 
-def gather_weights(shards, ways):
+def gather_weights(shards, ways, normed):
     n = len(shards)
     any_space = pl.BlockSpec(memory_space=pl.ANY)
     kinds = 2 * (ways - 1)
-    return pl.pallas_call(
+    rows, width = normed.shape
+    chans = shards[0].shape[1]
+    outs = pl.pallas_call(
         functools.partial(gather_kernel, n, ways),
-        in_specs=[any_space] * n,
-        out_specs=[any_space] * n,
-        out_shape=[jax.ShapeDtypeStruct((ways,) + w.shape, w.dtype) for w in shards],
+        in_specs=[any_space] * n + [pl.BlockSpec(memory_space=pltpu.VMEM)],
+        out_specs=[any_space] * (n + 1),
+        out_shape=[jax.ShapeDtypeStruct((ways,) + w.shape, w.dtype) for w in shards]
+        + [jax.ShapeDtypeStruct((ways, rows, 3 * chans), F32)],
         scratch_shapes=[pltpu.VMEM(w.shape, w.dtype) for w in shards]
         + [
+            pltpu.VMEM((2, width, chans), BF16),
+            pltpu.VMEM((2, rows, chans), F32),
+            pltpu.SemaphoreType.DMA((2,)),
+            pltpu.SemaphoreType.DMA((2,)),
             pltpu.SemaphoreType.DMA((n,)),
             pltpu.SemaphoreType.DMA((n,)),
             pltpu.SemaphoreType.DMA((n, kinds, GATHER_SLOTS)),
@@ -258,7 +315,8 @@
         ],
         compiler_params=params(collective_id=1, has_side_effects=True),
         name="gather_weights",
-    )(*shards)
+    )(*shards, normed)
+    return outs[:n], outs[n]
 
 
 def proj_kernel(x_ref, in_ref, forget_ref, gate_ref, o_ref):
@@ -899,14 +957,15 @@
 
     shards = [w_in, w_forget, w_gate, w_glu, w_up, w_out]
     if square:
-        all_shards = gather_weights(shards, ways)
+        all_shards, p = gather_weights(shards, ways, normed)
         w_down_all = gather(behind(w_down, all_shards[5]))
     else:
         all_shards = [gather(w) for w in shards]
         w_down_all = gather(w_down)
     w_three, (w_glu_all, w_up_all, w_out_all) = all_shards[:3], all_shards[3:]
 
-    p = project(normed, *w_three)
+    if not square:
+        p = project(normed, *w_three)
     totals = forward_total(p, lower, starts)
     all_totals = from_all(totals, "tensor")
     enter = jnp.zeros((ways, 1, chans), F32)

time: 1110 us -> 1090 us (0.982)
  Pallas kernels: 821 us -> 797 us
    pallas_call x1 -> x0, Pallas kernels: 34.4 us -> none  [project(): pl.pallas_call(proj_kernel, grid=(ways, 3), in_specs=[whole((rows, width)...]
  transfers between devices with their start and end apart: 30 -> 30, of which waited for: 9 -> 10; matrix products, arithmetic and copies ran while one was open for 6% -> 6% of each run, Pallas kernels for 50% -> 49%
where the time goes in v5:
time: 1090 us; the launch traced here: 1070 us
  Pallas kernels  797 us (73%)
  waiting for transfers between devices  66.8 us (6%)
  blocking collectives  58.3 us (5%)
  other arithmetic  56.8 us (5%)
  starting transfers between devices  53 us (5%)
  local copies, waits for them, and re-layouts  22.9 us (2%)
  between operations  19.3 us (2%)
    pallas_call x1, Pallas kernels, gather_weights(): pl.pallas_call(functools.partial(gather_kernel, n, ways), in_specs=[any_s...  274 us
    pallas_call x10, Pallas kernels, weight_grad(): pl.pallas_call(kernel, grid=(ways,), in_specs=[pl.BlockSpec(memory_space=...  175 us
    pallas_call x2, Pallas kernels, back(): pl.pallas_call(functools.partial(back_kernel, len(grads)), grid=(width //...  101 us
    pallas_call x1, Pallas kernels, feed_up(): pl.pallas_call(up_kernel, grid=(ways, rows // part), in_specs=[pl.BlockSp...  63.7 us
    ppermute x12, starting transfers between devices, send(): lax.ppermute(self.block(k), 'tensor', [(i, (i + k) % ways) for i in range...  45.2 us
    psum x1, blocking collectives, local(): small = run(lambda v: lax.psum(v, every), small)  44.2 us
    pallas_call x1, Pallas kernels, hidden_grad(): pl.pallas_call(hidden_grad_kernel, grid=(ways, rows // part), in_specs=[p...  37.2 us
    ppermute x5, waiting for transfers between devices, swap(): return lax.ppermute(array, 'core', SWAP)  36.9 us
  transfers between devices with their start and end apart: 30, of which 10 were waited for; matrix products, arithmetic and copies ran while one was open for 6% of the time, Pallas kernels for 49%

profile of v5, /device:TPU:0, one launch (start us, length us, event | category | flops | bytes accessed | tf_op | source)
XLA Modules:
  0.0 1073.9 jit_solution(13396977782539176340)
XLA Ops:
  16.4 273.6 %gather_weights.1 = (bf16[4,2048,512]{2,1,0:T(8,128)(2,1)}, bf16[4,2048,512]{2,1,0:T(8,128)(2,1)}, bf16[4,2048,512]{2,1,0:T(8,128)(2,1)}, bf16[4,2048,1408]{2,1,...) custom-call(bf16[2048,512]{1,0:T(8,128)(2,1)} %refs_0_.1, ...), custom_call_target="tpu_custom_call" | custom-call | tf_op jit(solution)/shard_map/gather_weights/pallas_call | solution.py:299
  325.3 21.7 %forward_scan.1 = (f32[4,1024,512]{2,1,0:T(8,128)}, bf16[4,1024,512]{2,1,0:T(8,128)(2,1)}, f32[4,8,512]{2,1,0:T(8,128)}) custom-call(s32[3]{0:T(128)} %add_subtract_fusion.starts_ref, f32[4,1024,1536]{2,1,0:T(8,128)} %get-tuple-element.167.p_ref.pf_ref.pg_ref.pi_ref, f32[4,1,512]{2,1,0:T(1,128)} %get-tuple-element.170.lower_ref, ...), custom_call_target="tpu_custom_call" | custom-call | tf_op jit(solution)/shard_map/forward_scan/pallas_call | solution.py:456
  347.0 16.0 %branch.1 = (f32[1024,2048]{1,0:T(8,128)}, bf16[1024,2048]{1,0:T(8,128)(2,1)}) custom-call(bf16[4,1024,512]{2,1,0:T(8,128)(2,1)} %get-tuple-element.154.mixed_ref.left_ref, bf16[4,512,2048]{2,1,0:T(8,128)(2,1)} %get-tuple-element.152.w_ref, bf16[1024,2048]{1,0:T(8,128)(2,1)} %x_ref.1, f32[1,2048]{1,0:T(1,128)} %bitcast.143), custom_call_target="tpu_custom_call" | custom-call | tf_op jit(solution)/shard_map/branch/pallas_call | solution.py:681
  363.0 63.7 %feed_up.1 = (bf16[4,1024,1408]{2,1,0:T(8,128)(2,1)}, bf16[4,1024,1408]{2,1,0:T(8,128)(2,1)}, bf16[4,1024,1408]{2,1,0:T(8,128)(2,1)}) custom-call(bf16[1024,2048]{1,0:T(8,128)(2,1)} %get-tuple-element.139.x_ref.left_ref, bf16[4,2048,1408]{2,1,0:T(8,128)(2,1)} %get-tuple-element.144.up_ref.refs_2_, bf16[4,2048,1408]{2,1,0:T(8,128)(2,1)} %get-tuple-element.145.glu_ref.refs_3_), custom_call_target="tpu_custom_call" | custom-call | tf_op jit(solution)/shard_map/feed_up/pallas_call | solution.py:717
  426.7 17.6 %by_cols.4 = bf16[4,4,1408,256]{3,2,1,0:T(8,128)(2,1)} custom-call(s32[4]{0:T(128)} %fusion.24.at_ref, bf16[1024,2048]{1,0:T(8,128)(2,1)} %dy_ref, bf16[4,1024,1408]{2,1,0:T(8,128)(2,1)} %get-tuple-element.185.left_ref.h_ref), custom_call_target="tpu_custom_call" | custom-call | tf_op jit(solution)/shard_map/by_cols/pallas_call | solution.py:864
  444.8 17.5 %collective-permute-done.6.refs_0_ = bf16[4,4,1408,256]{3,2,1,0:T(8,128)(2,1)} collective-permute-done((bf16[4,4,1408,256]{3,2,1,0:T(8,128)(2,1)}, bf16[4,4,1408,256]{3,2,1,0:T(8,128)(2,1)}, u32[]{:S(2)}, u32[]{:S(2)}) %collective-permute-start.6) | collective-permute-done | bytes 11534368 | tf_op jit(solution)/shard_map/ppermute | solution.py:986
  462.3 19.0 %by_cols.5 = bf16[4,4,1408,256]{3,2,1,0:T(8,128)(2,1)} custom-call(s32[4]{0:T(128)} %fusion.25.at_ref, bf16[1024,2048]{1,0:T(8,128)(2,1)} %dy_ref, bf16[4,1024,1408]{2,1,0:T(8,128)(2,1)} %get-tuple-element.185.left_ref.h_ref, bf16[4,4,1408,256]{3,2,1,0:T(8,128)(2,1)} %collective-permute-done.6.refs_0_), custom_call_target="tpu_custom_call" | custom-call | tf_op jit(solution)/shard_map/by_cols/pallas_call | solution.py:864
  481.6 37.2 %hidden_grad.1 = (bf16[4,1024,1408]{2,1,0:T(8,128)(2,1)}, bf16[4,1024,1408]{2,1,0:T(8,128)(2,1)}) custom-call(bf16[1024,2048]{1,0:T(8,128)(2,1)} %dy_ref, bf16[4,1408,2048]{2,1,0:T(8,128)(2,1)} %bitcast.131, bf16[4,1024,1408]{2,1,0:T(8,128)(2,1)} %get-tuple-element.128.act_ref, bf16[4,1024,1408]{2,1,0:T(8,128)(2,1)} %get-tuple-element.129.slope_ref), custom_call_target="tpu_custom_call" | custom-call | tf_op jit(solution)/shard_map/hidden_grad/pallas_call | solution.py:765
  518.8 19.0 %by_rows.6 = bf16[4,4,256,1408]{3,2,1,0:T(8,128)(2,1)} custom-call(s32[4]{0:T(128)} %fusion.24.at_ref, bf16[1024,2048]{1,0:T(8,128)(2,1)} %get-tuple-element.139.x_ref.left_ref, bf16[4,1024,1408]{2,1,0:T(8,128)(2,1)} %get-tuple-element.142.refs_0_), custom_call_target="tpu_custom_call" | custom-call | tf_op jit(solution)/shard_map/by_rows/pallas_call | solution.py:864
  537.8 18.9 %by_rows.7 = bf16[4,4,256,1408]{3,2,1,0:T(8,128)(2,1)} custom-call(s32[4]{0:T(128)} %fusion.24.at_ref, bf16[1024,2048]{1,0:T(8,128)(2,1)} %get-tuple-element.139.x_ref.left_ref, bf16[4,1024,1408]{2,1,0:T(8,128)(2,1)} %get-tuple-element.143.refs_0_.refs_1_), custom_call_target="tpu_custom_call" | custom-call | tf_op jit(solution)/shard_map/by_rows/pallas_call | solution.py:864
  557.0 20.1 %by_rows.8 = bf16[4,4,256,1408]{3,2,1,0:T(8,128)(2,1)} custom-call(s32[4]{0:T(128)} %fusion.25.at_ref, bf16[1024,2048]{1,0:T(8,128)(2,1)} %get-tuple-element.139.x_ref.left_ref, bf16[4,1024,1408]{2,1,0:T(8,128)(2,1)} %get-tuple-element.142.refs_0_, bf16[4,4,256,1408]{3,2,1,0:T(8,128)(2,1)} %collective-permute-done.8.refs_1_), custom_call_target="tpu_custom_call" | custom-call | tf_op jit(solution)/shard_map/by_rows/pallas_call | solution.py:864
  577.1 20.1 %by_rows.9 = bf16[4,4,256,1408]{3,2,1,0:T(8,128)(2,1)} custom-call(s32[4]{0:T(128)} %fusion.25.at_ref, bf16[1024,2048]{1,0:T(8,128)(2,1)} %get-tuple-element.139.x_ref.left_ref, bf16[4,1024,1408]{2,1,0:T(8,128)(2,1)} %get-tuple-element.143.refs_0_.refs_1_, bf16[4,4,256,1408]{3,2,1,0:T(8,128)(2,1)} %collective-permute-done.7.refs_1_), custom_call_target="tpu_custom_call" | custom-call | tf_op jit(solution)/shard_map/by_rows/pallas_call | solution.py:864
  597.9 64.3 %back.2 = f32[1024,2048]{1,0:T(8,128)} custom-call(bf16[4,1024,1408]{2,1,0:T(8,128)(2,1)} %get-tuple-element.142.refs_0_, bf16[4,1024,1408]{2,1,0:T(8,128)(2,1)} %get-tuple-element.143.refs_0_.refs_1_, bf16[4,2048,1408]{2,1,0:T(8,128)(2,1)} %get-tuple-element.144.up_ref.refs_2_, bf16[4,2048,1408]{2,1,0:T(8,128)(2,1)} %get-tuple-element.145.glu_ref.refs_3_), custom_call_target="tpu_custom_call" | custom-call | tf_op jit(solution)/shard_map/back/pallas_call | solution.py:801
  697.7 14.2 %mixed_grad.1.gm_ref = f32[4,1024,512]{2,1,0:T(8,128)} custom-call(bf16[1024,2048]{1,0:T(8,128)(2,1)} %get-tuple-element.153.right_ref.g_ref, bf16[4,512,2048]{2,1,0:T(8,128)(2,1)} %get-tuple-element.152.w_ref), custom_call_target="tpu_custom_call" | custom-call | tf_op jit(solution)/shard_map/mixed_grad/pallas_call | solution.py:820
  725.8 23.3 %backward_total.1 = (f32[4,1024,512]{2,1,0:T(8,128)}, bf16[4,1024,512]{2,1,0:T(8,128)(2,1)}, f32[4,8,512]{2,1,0:T(8,128)}, f32[4,1,512]{2,1,0:T(1,128)}) custom-call(s32[3]{0:T(128)} %add_subtract_fusion.starts_ref, f32[4,1024,1536]{2,1,0:T(8,128)} %get-tuple-element.167.p_ref.pf_ref.pg_ref.pi_ref, ...), custom_call_target="tpu_custom_call" | custom-call | tf_op jit(solution)/shard_map/backward_total/pallas_call | solution.py:544
  764.6 23.6 %backward_scan.1 = (bf16[4,1024,512]{2,1,0:T(8,128)(2,1)}, bf16[4,1024,512]{2,1,0:T(8,128)(2,1)}, f32[4,8,512]{2,1,0:T(8,128)}) custom-call(s32[3]{0:T(128)} %add_subtract_fusion.starts_ref, f32[4,1024,1536]{2,1,0:T(8,128)} %get-tuple-element.167.p_ref.pf_ref.pg_ref.pi_ref, f32[4,1024,1536]{2,1,0:T(8,128)} %get-tuple-element.167.p_ref.pf_ref.pg_ref.pi_ref, ...), custom_call_target="tpu_custom_call" | custom-call | tf_op jit(solution)/shard_map/backward_scan/pallas_call | solution.py:638
  788.2 19.2 %by_rows.10 = bf16[4,4,256,1536]{3,2,1,0:T(8,128)(2,1)} custom-call(s32[4]{0:T(128)} %fusion.24.at_ref, bf16[1024,2048]{1,0:T(8,128)(2,1)} %fusion.5.refs_6_.left_ref, bf16[4,1024,512]{2,1,0:T(8,128)(2,1)} %get-tuple-element.191.refs_0_, bf16[4,1024,512]{2,1,0:T(8,128)(2,1)} %get-tuple-element.192.refs_1_, bf16[4,1024,512]{2,1,0:T(8,128)(2,1)} %get-tuple-element.193.refs_2_), custom_call_target="tpu_custom_call" | custom-call | tf_op jit(solution)/shard_map/by_rows/pallas_call | solution.py:864
  807.5 19.4 %collective-permute-done.13.refs_3_ = bf16[4,4,256,1536]{3,2,1,0:T(8,128)(2,1)} collective-permute-done((bf16[4,4,256,1536]{3,2,1,0:T(8,128)(2,1)}, bf16[4,4,256,1536]{3,2,1,0:T(8,128)(2,1)}, u32[]{:S(2)}, u32[]{:S(2)}) %collective-permute-start.13) | collective-permute-done | bytes 12582944 | tf_op jit(solution)/shard_map/ppermute | solution.py:986
  826.9 20.6 %by_rows.11 = bf16[4,4,256,1536]{3,2,1,0:T(8,128)(2,1)} custom-call(s32[4]{0:T(128)} %fusion.25.at_ref, bf16[1024,2048]{1,0:T(8,128)(2,1)} %fusion.5.refs_6_.left_ref, bf16[4,1024,512]{2,1,0:T(8,128)(2,1)} %get-tuple-element.191.refs_0_, bf16[4,1024,512]{2,1,0:T(8,128)(2,1)} %get-tuple-element.192.refs_1_, bf16[4,1024,512]{2,1,0:T(8,128)(2,1)} %get-tuple-element.193.refs_2_, ...), custom_call_target="tpu_custom_call" | custom-call | tf_op jit(solution)/shard_map/by_rows/pallas_call | solution.py:864
  860.5 16.6 %reduce-scatter.25.cloned.1.call-done = bf16[1,4,512,256]{3,2,1,0:T(8,128)(2,1)} async-done(((bf16[4,4,512,256]{3,2,1,0:T(8,128)(2,1)}), bf16[1,4,512,256]{3,2,1,0:T(8,128)(2,1)}) %reduce-scatter.25.cloned.1.call-update) | async-done | bytes 1048592
  880.5 34.4 %feed_down.1 = bf16[1024,2048]{1,0:T(8,128)(2,1)} custom-call(bf16[4,1024,1408]{2,1,0:T(8,128)(2,1)} %get-tuple-element.185.left_ref.h_ref, bf16[4,1408,2048]{2,1,0:T(8,128)(2,1)} %bitcast.132, f32[1024,2048]{1,0:T(8,128)} %get-tuple-element.187.resid_ref), custom_call_target="tpu_custom_call" | custom-call | tf_op jit(solution)/shard_map/feed_down/pallas_call | solution.py:739
  919.1 25.4 %collective-permute-start.18 = (bf16[256,1408]{1,0:T(8,128)(2,1)}, bf16[256,1408]{1,0:T(8,128)(2,1)}, u32[]{:S(2)}, u32[]{:S(2)}) collective-permute-start(bf16[256,1408]{1,0:T(8,128)(2,1)} %get-tuple-element.211), channel_id=1, source_target_pairs={{0,2},{1,3},{2,0},{3,1},{4,6},{5,7},{6,4},{7,5},{8,10},{9,11},{10,... | collective-permute-start | bytes 2162696 | tf_op jit(solution)/shard_map/ppermute | solution.py:999
  944.5 36.6 %back.3 = f32[1024,2048]{1,0:T(8,128)} custom-call(bf16[4,1024,512]{2,1,0:T(8,128)(2,1)} %get-tuple-element.191.refs_0_, bf16[4,1024,512]{2,1,0:T(8,128)(2,1)} %get-tuple-element.192.refs_1_, bf16[4,1024,512]{2,1,0:T(8,128)(2,1)} %get-tuple-element.193.refs_2_, bf16[4,2048,512]{2,1,0:T(8,128)(2,1)} %get-tuple-element.194.refs_3_, ...), custom_call_target="tpu_custom_call" | custom-call | tf_op jit(solution)/shard_map/back/pallas_call | solution.py:801
  1014.4 44.2 %psum.7 = f32[5,2048]{1,0:T(8,128)S(1)} all-reduce(f32[5,2048]{1,0:T(8,128)S(1)} %stack.79), channel_id=1, replica_groups=mesh['chip'=4,'core'=2,'tensor'=4] {'tensor','chip','core'}, use_global_device_ids=true, to_apply=%region_15.16 | all-reduce | flops 10240 | bytes 81920 | tf_op jit(solution)/shard_map/psum | solution.py:1112
  (151 shorter events, 168.3 us)
Async XLA Ops:
  8.0 473.6 %all-gather.3.cloned.1.call-start = ((), (), s32[]{:S(2)}) async-start(), calls=%async_computation.6 | async-start | bytes 23789568 | tf_op jit(solution)/shard_map/all_gather | solution.py:947
  292.1 398.8 %reduce-scatter.19.cloned.1.call-start = ((), (), s32[]{:S(2)}) async-start(), calls=%async_computation.8 | async-start | bytes 14417920
  444.3 18.0 %collective-permute-start.6 = (bf16[4,4,1408,256]{3,2,1,0:T(8,128)(2,1)}, bf16[4,4,1408,256]{3,2,1,0:T(8,128)(2,1)}, u32[]{:S(2)}, u32[]{:S(2)}) collective-permute-start(bf16[4,4,1408,256]{3,2,1,0:T(8,128)(2,1)} %by_cols.4), channel_id=1, source_target_pairs={{0,4},{4,0},{1,5},{5,1},{2,6},{6,2},{3,7},{7,3},{8,12},{12,8},{9,1... | collective-permute-start | bytes 34603016 | tf_op jit(solution)/shard_map/ppermute | solution.py:986
  481.4 366.3 %reduce-scatter.23.cloned.1.call-start = ((), (), s32[]{:S(2)}) async-start(), calls=%async_computation.10 | async-start | bytes 14417920
  537.7 19.3 %collective-permute-start.8 = (bf16[4,4,256,1408]{3,2,1,0:T(8,128)(2,1)}, bf16[4,4,256,1408]{3,2,1,0:T(8,128)(2,1)}, u32[]{:S(2)}, u32[]{:S(2)}) collective-permute-start(bf16[4,4,256,1408]{3,2,1,0:T(8,128)(2,1)} %by_rows.6), channel_id=1, source_target_pairs={{0,4},{4,0},{1,5},{5,1},{2,6},{6,2},{3,7},{7,3},{8,12},{12,8},{9,1... | collective-permute-start | bytes 34603016 | tf_op jit(solution)/shard_map/ppermute | solution.py:986
  556.7 20.4 %collective-permute-start.7 = (bf16[4,4,256,1408]{3,2,1,0:T(8,128)(2,1)}, bf16[4,4,256,1408]{3,2,1,0:T(8,128)(2,1)}, u32[]{:S(2)}, u32[]{:S(2)}) collective-permute-start(bf16[4,4,256,1408]{3,2,1,0:T(8,128)(2,1)} %by_rows.7), channel_id=1, source_target_pairs={{0,4},{4,0},{1,5},{5,1},{2,6},{6,2},{3,7},{7,3},{8,12},{12,8},{9,1... | collective-permute-start | bytes 34603016 | tf_op jit(solution)/shard_map/ppermute | solution.py:986
  597.2 250.4 %reduce-scatter.21.cloned.1.call-start = ((), (), s32[]{:S(2)}) async-start(), calls=%async_computation.9 | async-start | bytes 14417920
  597.8 279.3 %reduce-scatter.25.cloned.1.call-start = ((), (), s32[]{:S(2)}) async-start(), calls=%async_computation.11 | async-start | bytes 5242880
  690.5 24.5 %collective-permute-start.9 = (bf16[4,4,512,256]{3,2,1,0:T(8,128)(2,1)}, bf16[4,4,512,256]{3,2,1,0:T(8,128)(2,1)}, u32[]{:S(2)}, u32[]{:S(2)}) collective-permute-start(bf16[4,4,512,256]{3,2,1,0:T(8,128)(2,1)} %by_cols.6), channel_id=1, source_target_pairs={{0,4},{4,0},{1,5},{5,1},{2,6},{6,2},{3,7},{7,3},{8,12},{12,8},{9,1... | collective-permute-start | bytes 12582920 | tf_op jit(solution)/shard_map/ppermute | solution.py:986
  693.9 21.1 %collective-permute-start.10 = (bf16[1408,256]{1,0:T(8,128)(2,1)}, bf16[1408,256]{1,0:T(8,128)(2,1)S(1)}, u32[]{:S(2)}, u32[]{:S(2)}) collective-permute-start(bf16[1408,256]{1,0:T(8,128)(2,1)} %get-tuple-element.218), channel_id=1, source_target_pairs={{0,1},{1,2},{2,3},{3,0},{4,5},{5,6},{6,7},{7,4},{8,9},{9,10},{10,1... | collective-permute-start | bytes 2162696 | tf_op jit(solution)/shard_map/ppermute | solution.py:999
  693.9 70.7 %collective-permute-start.11 = (bf16[1408,256]{1,0:T(8,128)(2,1)}, bf16[1408,256]{1,0:T(8,128)(2,1)S(1)}, u32[]{:S(2)}, u32[]{:S(2)}) collective-permute-start(bf16[1408,256]{1,0:T(8,128)(2,1)} %get-tuple-element.217), channel_id=1, source_target_pairs={{0,2},{1,3},{2,0},{3,1},{4,6},{5,7},{6,4},{7,5},{8,10},{9,11},{10,... | collective-permute-start | bytes 2162696 | tf_op jit(solution)/shard_map/ppermute | solution.py:999
  693.9 94.3 %collective-permute-start.12 = (bf16[1408,256]{1,0:T(8,128)(2,1)S(1)}, bf16[1408,256]{1,0:T(8,128)(2,1)S(1)}, u32[]{:S(2)}, u32[]{:S(2)}) collective-permute-start(bf16[1408,256]{1,0:T(8,128)(2,1)S(1)} %get-tuple-element.216), channel_id=1, source_target_pairs={{0,3},{1,0},{2,1},{3,2},{4,7},{5,4},{6,5},{7,6},{8,11},{9,8},{10,9... | collective-permute-start | bytes 2162696 | tf_op jit(solution)/shard_map/ppermute | solution.py:999
  807.4 19.5 %collective-permute-start.13 = (bf16[4,4,256,1536]{3,2,1,0:T(8,128)(2,1)}, bf16[4,4,256,1536]{3,2,1,0:T(8,128)(2,1)}, u32[]{:S(2)}, u32[]{:S(2)}) collective-permute-start(bf16[4,4,256,1536]{3,2,1,0:T(8,128)(2,1)} %by_rows.10), channel_id=1, source_target_pairs={{0,4},{4,0},{1,5},{5,1},{2,6},{6,2},{3,7},{7,3},{8,12},{12,8},{9,1... | collective-permute-start | bytes 37748744 | tf_op jit(solution)/shard_map/ppermute | solution.py:986
  807.4 193.8 %reduce-scatter.27.cloned.1.call-start = ((), (), s32[]{:S(2)}) async-start(), calls=%async_computation.12 | async-start | bytes 15728640
  847.6 215.1 %reduce-scatter.17.cloned.1.call-start = ((), (), s32[]{:S(2)}) async-start(), calls=%async_computation.7 | async-start | bytes 3932160 | tf_op jit(solution)/shard_map/reduce_scatter | solution.py:1007
  850.7 64.3 %collective-permute-start.14 = (bf16[256,1408]{1,0:T(8,128)(2,1)}, bf16[256,1408]{1,0:T(8,128)(2,1)S(1)}, u32[]{:S(2)}, u32[]{:S(2)}) collective-permute-start(bf16[256,1408]{1,0:T(8,128)(2,1)} %get-tuple-element.215), channel_id=1, source_target_pairs={{0,1},{1,2},{2,3},{3,0},{4,5},{5,6},{6,7},{7,4},{8,9},{9,10},{10,1... | collective-permute-start | bytes 2162696 | tf_op jit(solution)/shard_map/ppermute | solution.py:999
  853.1 64.2 %collective-permute-start.15 = (bf16[256,1408]{1,0:T(8,128)(2,1)}, bf16[256,1408]{1,0:T(8,128)(2,1)}, u32[]{:S(2)}, u32[]{:S(2)}) collective-permute-start(bf16[256,1408]{1,0:T(8,128)(2,1)} %get-tuple-element.214), channel_id=1, source_target_pairs={{0,2},{1,3},{2,0},{3,1},{4,6},{5,7},{6,4},{7,5},{8,10},{9,11},{10,... | collective-permute-start | bytes 2162696 | tf_op jit(solution)/shard_map/ppermute | solution.py:999
  855.4 63.6 %collective-permute-start.16 = (bf16[256,1408]{1,0:T(8,128)(2,1)}, bf16[256,1408]{1,0:T(8,128)(2,1)}, u32[]{:S(2)}, u32[]{:S(2)}) collective-permute-start(bf16[256,1408]{1,0:T(8,128)(2,1)} %get-tuple-element.213), channel_id=1, source_target_pairs={{0,3},{1,0},{2,1},{3,2},{4,7},{5,4},{6,5},{7,6},{8,11},{9,8},{10,9... | collective-permute-start | bytes 2162696 | tf_op jit(solution)/shard_map/ppermute | solution.py:999
  858.4 122.6 %collective-permute-start.17 = (bf16[256,1408]{1,0:T(8,128)(2,1)}, bf16[256,1408]{1,0:T(8,128)(2,1)}, u32[]{:S(2)}, u32[]{:S(2)}) collective-permute-start(bf16[256,1408]{1,0:T(8,128)(2,1)} %get-tuple-element.212), channel_id=1, source_target_pairs={{0,1},{1,2},{2,3},{3,0},{4,5},{5,6},{6,7},{7,4},{8,9},{9,10},{10,1... | collective-permute-start | bytes 2162696 | tf_op jit(solution)/shard_map/ppermute | solution.py:999
  879.0 122.2 %collective-permute-start.19 = (bf16[512,256]{1,0:T(8,128)(2,1)}, bf16[512,256]{1,0:T(8,128)(2,1)}, u32[]{:S(2)}, u32[]{:S(2)}) collective-permute-start(bf16[512,256]{1,0:T(8,128)(2,1)} %get-tuple-element.221), channel_id=1, source_target_pairs={{0,1},{1,2},{2,3},{3,0},{4,5},{5,6},{6,7},{7,4},{8,9},{9,10},{10,1... | collective-permute-start | bytes 786440 | tf_op jit(solution)/shard_map/ppermute | solution.py:999
  914.9 86.3 %collective-permute-start.20 = (bf16[512,256]{1,0:T(8,128)(2,1)S(1)}, bf16[512,256]{1,0:T(8,128)(2,1)}, u32[]{:S(2)}, u32[]{:S(2)}) collective-permute-start(bf16[512,256]{1,0:T(8,128)(2,1)S(1)} %get-tuple-element.220), channel_id=1, source_target_pairs={{0,2},{1,3},{2,0},{3,1},{4,6},{5,7},{6,4},{7,5},{8,10},{9,11},{10,... | collective-permute-start | bytes 786440 | tf_op jit(solution)/shard_map/ppermute | solution.py:999
  917.3 84.0 %collective-permute-start.21 = (bf16[512,256]{1,0:T(8,128)(2,1)S(1)}, bf16[512,256]{1,0:T(8,128)(2,1)}, u32[]{:S(2)}, u32[]{:S(2)}) collective-permute-start(bf16[512,256]{1,0:T(8,128)(2,1)S(1)} %get-tuple-element.219), channel_id=1, source_target_pairs={{0,3},{1,0},{2,1},{3,2},{4,7},{5,4},{6,5},{7,6},{8,11},{9,8},{10,9... | collective-permute-start | bytes 786440 | tf_op jit(solution)/shard_map/ppermute | solution.py:999
  919.1 82.2 %collective-permute-start.18 = (bf16[256,1408]{1,0:T(8,128)(2,1)}, bf16[256,1408]{1,0:T(8,128)(2,1)}, u32[]{:S(2)}, u32[]{:S(2)}) collective-permute-start(bf16[256,1408]{1,0:T(8,128)(2,1)} %get-tuple-element.211), channel_id=1, source_target_pairs={{0,2},{1,3},{2,0},{3,1},{4,6},{5,7},{6,4},{7,5},{8,10},{9,11},{10,... | collective-permute-start | bytes 2162696 | tf_op jit(solution)/shard_map/ppermute | solution.py:999
  981.1 21.3 %collective-permute-start.22 = (bf16[256,1408]{1,0:T(8,128)(2,1)}, bf16[256,1408]{1,0:T(8,128)(2,1)}, u32[]{:S(2)}, u32[]{:S(2)}) collective-permute-start(bf16[256,1408]{1,0:T(8,128)(2,1)} %get-tuple-element.210), channel_id=1, source_target_pairs={{0,3},{1,0},{2,1},{3,2},{4,7},{5,4},{6,5},{7,6},{8,11},{9,8},{10,9... | collective-permute-start | bytes 2162696 | tf_op jit(solution)/shard_map/ppermute | solution.py:999
  (20 other events, 988.2 us)
Sparse Core Ops, SparseCore 0:
  292.2 143.3 all-gather.2
  1002.6 60.0 reduce-scatter.16
Sparse Core Ops, SparseCore 1:
  481.4 108.7 reduce-scatter.18
  597.3 109.2 reduce-scatter.22
  709.6 112.0 reduce-scatter.20
  824.6 52.5 reduce-scatter.24
  880.6 120.6 reduce-scatter.26
